TPU v7x, 32 devices: a whole 2x2x4 slice. The times are simulated.
32 devices in a mesh: rep: 4 (over x, core), fsdp: 8 (over z, y).
Axes of the slice: x: 2, y: 2, z: 4, core: 2. Of those that a mesh axis runs over, the one named last changes fastest.
Arguments:
- tokens: bfloat16 [4096, 1536], P(('rep', 'fsdp')), may hold values from -6 to 6
- context: bfloat16 [4, 512, 1536], P('rep', 'fsdp'), may hold values from -6 to 6
- cotangent: bfloat16 [4096, 1536], P(('rep', 'fsdp')), may hold values from -6 to 6
- positions: int32 [3, 4096], P(None, ('rep', 'fsdp')), may hold values from 0 to 63
- sequence_lengths: int32 [4], P('rep'), may hold values from 512 to 1024, as said below
- sequence_adapter: int32 [4], P('rep'), may hold values from 0 to 7
- text_token_count: int32 [4], P('rep'), may hold values from 64 to 512, as said below
- timestep_modulation: float32 [4, 6, 1536], P('rep'), may hold values from -4 to 4
- modulation: float32 [2, 6, 1536], replicated, may hold values from -2 to 2
- gains: float32 [2, 5, 1536], replicated, may hold values from 0.5 to 1.5
- query_key_value_weight: bfloat16 [2, 6, 1536, 1536], P(None, None, 'fsdp'), may hold values from -0.15625 to 0.15625
- output_weight: bfloat16 [2, 2, 1536, 1536], P(None, None, 'fsdp'), may hold values from -0.3125 to 0.3125
- up_weight: bfloat16 [2, 1536, 8960], P(None, 'fsdp'), may hold values from -0.15625 to 0.15625
- down_weight: bfloat16 [2, 8960, 1536], P(None, 'fsdp'), may hold values from -0.0625 to 0.0625
- first_factors: bfloat16 [2, 9, 1536, 128], P(None, None, 'fsdp'), may hold values from -0.15625 to 0.15625
- down_first_factor: bfloat16 [2, 8960, 128], P(None, 'fsdp'), may hold values from -0.0625 to 0.0625
- second_factors: bfloat16 [2, 9, 128, 1536], P(None, None, None, 'fsdp'), may hold values from -1.5 to 1.5
- up_second_factor: bfloat16 [2, 128, 8960], P(None, None, 'fsdp'), may hold values from -1.5 to 1.5
Outputs:
- block_out: bfloat16 [4096, 1536], P(('rep', 'fsdp'))
- grad_tokens: float32 [4096, 1536], P(('rep', 'fsdp'))
- grad_context: float32 [4, 512, 1536], P('rep', 'fsdp')
- grad_lora_a: float32 [2, 9, 1536, 128], P(None, None, 'fsdp')
- grad_lora_a_down: float32 [2, 8960, 128], P(None, 'fsdp')
- grad_lora_b: float32 [2, 9, 128, 1536], P(None, None, None, 'fsdp')
- grad_lora_b_up: float32 [2, 128, 8960], P(None, None, 'fsdp')
Inputs may be any that keep to these rules, and one draw needn't show every extreme that they name: `sequence_lengths`: the 1 entries of a group hold its sequences' valid lengths; at least one sequence in all has exactly 1024 tokens. `text_token_count`: some sequence uses all 512 text slots.
All inputs are finite; a program needn't handle non-finite values.
Results may differ from a plain program's by a relative error of at most 0.035.
Values may be sent and summed in bfloat16 or wider, within the bound.
No kernel may reach another device: no remote copies, remote signals or barrier semaphores. Data moves between devices by JAX's collectives and lax.ppermute only.
A program may use at most 704 MiB of HBM per device.

v0:
```python
import math

import jax
import jax.numpy as jnp
from jax import lax
from jax.sharding import PartitionSpec as P

HD = 128
ADAPTER_RANK = 16
TENSOR = 4

AXES = ("rep", "fsdp")
epsilon = 1e-06
masked_score = -1e30
f32 = jnp.float32
bf16 = jnp.bfloat16


def dot(left, right):
    return jnp.dot(left, right, preferred_element_type=f32)


def dot_nt(left, right):
    return lax.dot_general(left, right, (((1,), (1,)), ((), ())), preferred_element_type=f32)


def dot_tn(left, right):
    return lax.dot_general(left, right, (((0,), (0,)), ((), ())), preferred_element_type=f32)


class Place:
    def __init__(self):
        self.rep = lax.axis_size(AXES[0])
        self.size = lax.axis_size(AXES[1])
        self.outer = self.rep // 2
        self.half = self.size // 2
        self.blocks = self.half // TENSOR
        self.shards = self.size // TENSOR
        self.r = lax.axis_index(AXES[0])
        self.f = lax.axis_index(AXES[1])
        self.c = self.r % 2
        self.h = self.f // self.half
        self.b = (self.f // TENSOR) % self.blocks
        self.p = self.f % TENSOR

    def send(self, values, move):
        pairs = []
        for r in range(self.rep):
            for f in range(self.size):
                o, c = divmod(r, 2)
                h, rest = divmod(f, self.half)
                b, p = divmod(rest, TENSOR)
                o, c, h, b, p = move(o, c, h, b, p)
                target = (2 * o + c) * self.size + h * self.half + b * TENSOR + p
                pairs.append((r * self.size + f, target))
        return lax.ppermute(values, AXES, pairs)

    def send_rows(self, values, move):
        pairs = [(f, move(f)) for f in range(self.size)]
        return lax.ppermute(values, AXES[1], pairs)

    def swap(self, values):
        return self.send(values, lambda o, c, h, b, p: (o, h, c, b, p))

    def part(self, values, k):
        return self.send_rows(values, lambda f: f ^ k)

    def other_block(self, values, k):
        return self.send_rows(values, lambda f: f ^ (TENSOR * k))

    def other_core(self, values):
        return self.send(values, lambda o, c, h, b, p: (o, 1 - c, h, b, p))

    def other_outer(self, values, k):
        return self.send(values, lambda o, c, h, b, p: (o ^ k, c, h, b, p))

    def gather(self, rows):
        cut = rows.shape[1] // 2
        one = self.part(rows, 1)
        two = self.part(rows, 2)
        far = jnp.concatenate([self.part(one[:, :cut], 2), self.part(two[:, cut:], 1)], 1)
        return jnp.concatenate([rows, one, two, far], 0)

    def scatter(self, rows):
        cut = rows.shape[1] // 2
        count = rows.shape[0] // TENSOR
        rows = rows.astype(bf16)
        left = [rows[k * count : (k + 1) * count, :cut] for k in range(TENSOR)]
        right = [rows[k * count : (k + 1) * count, cut:] for k in range(TENSOR)]
        from_one = self.part(jnp.concatenate([left[1], left[3]], 0), 1).astype(f32)
        from_two = self.part(jnp.concatenate([right[2], right[3]], 0), 2).astype(f32)
        left_far = (left[2].astype(f32) + from_one[count:]).astype(bf16)
        right_far = (right[1].astype(f32) + from_two[count:]).astype(bf16)
        left_sum = left[0].astype(f32) + from_one[:count] + self.part(left_far, 2).astype(f32)
        right_sum = right[0].astype(f32) + from_two[:count] + self.part(right_far, 1).astype(f32)
        return jnp.concatenate([left_sum, right_sum], 1)

    def total(self, stats):
        result = stats
        for k in range(1, TENSOR):
            arrived = self.part(stats, k)
            result = result + jnp.stack([arrived[:, j ^ k] for j in range(TENSOR)], 1)
        return result

    def spread(self, rows):
        own = [rows] + [self.other_block(rows, k) for k in range(1, self.blocks)]
        stacked = jnp.concatenate(own, 0) if len(own) > 1 else rows
        return jnp.concatenate([stacked, self.other_core(stacked)], 0)

    def collect(self, rows):
        count = rows.shape[0] // 2
        block = count // self.blocks
        total = rows[:count] + self.other_core(rows[count:].astype(bf16)).astype(f32)
        result = total[:block]
        for k in range(1, self.blocks):
            piece = total[k * block : (k + 1) * block].astype(bf16)
            result = result + self.other_block(piece, k).astype(f32)
        return result

    def gather_rep(self, rows):
        n, q, w = rows.shape
        whole = jnp.zeros((n, self.rep, q, w), rows.dtype)

        def put(whole, piece, index):
            return lax.dynamic_update_slice(whole, piece[:, None], (0, index, 0, 0))

        for k in range(self.outer):
            piece = rows if k == 0 else self.other_outer(rows, k)
            whole = put(whole, piece, self.r ^ (2 * k))
            whole = put(whole, self.other_core(piece), self.r ^ (2 * k + 1))
        return whole.reshape(n * self.rep * q, w)

    def quarter(self, rows):
        count = rows.shape[0] // self.rep
        return lax.dynamic_slice_in_dim(rows, self.r * count, count, 0)

    def fetch_columns(self, matrices, extras, after):
        matrices = [self.quarter(m) for m in matrices]
        extras = [self.quarter(e) for e in extras]
        matrices, extras, _ = lax.optimization_barrier((matrices, extras, after))
        pieces = []
        for k in range(TENSOR):
            part = self.p ^ k
            pieces.append(
                [
                    lax.dynamic_slice_in_dim(
                        m, part * (m.shape[1] // TENSOR), m.shape[1] // TENSOR, 1
                    )
                    for m in matrices
                ]
            )
        width = sum(m.shape[1] // TENSOR for m in matrices) + sum(e.shape[2] for e in extras)
        whole = jnp.zeros((self.size, matrices[0].shape[0], width), bf16)
        arrived = []
        for k in range(self.size):
            to_half = self.h ^ (k // self.half)
            chosen = [jnp.where(to_half == 0, e[:, 0], e[:, 1]) for e in extras]
            piece = jnp.concatenate(pieces[k % TENSOR] + chosen, 1)
            if k:
                piece = self.send_rows(piece, lambda f, k=k: f ^ k)
            arrived.append(piece)
            whole = lax.dynamic_update_slice(whole, piece[None], (self.f ^ k, 0, 0))
        return self.gather_rep(whole), arrived[-1]

    def fetch_rows(self, matrix, extras, after):
        matrix = self.quarter(matrix)
        extras = [self.quarter(e) for e in extras]
        matrix, extras, _ = lax.optimization_barrier((matrix, extras, after))
        width = matrix.shape[1] + sum(e.shape[2] for e in extras)
        whole = jnp.zeros((self.shards, matrix.shape[0], width), bf16)
        shard = self.f % self.shards
        arrived = []
        for k in range(self.shards):
            to_half = ((shard + k) % self.shards) // self.blocks
            chosen = [jnp.where(to_half == 0, e[:, 0], e[:, 1]) for e in extras]
            piece = jnp.concatenate([matrix] + chosen, 1)
            piece = self.send_rows(
                piece,
                lambda f, k=k: f // self.shards + TENSOR * ((f % self.shards + k) % self.shards),
            )
            arrived.append(piece)
            source = (self.f // TENSOR - k) % self.shards
            whole = lax.dynamic_update_slice(whole, piece[None], (source, 0, 0))
        return self.gather_rep(whole), arrived[-1]


def norm_parts(values):
    centred = values - jnp.mean(values, -1, keepdims=True)
    scale = lax.rsqrt(jnp.mean(centred * centred, -1, keepdims=True) + epsilon)
    return centred * scale, scale


def layer_norm_back(values, grad):
    hat, scale = norm_parts(values)
    along = jnp.mean(grad * hat, -1, keepdims=True)
    return scale * (grad - jnp.mean(grad, -1, keepdims=True) - hat * along)


def rotary_tables(positions):
    pair_count = HD // 2
    third_part = pair_count // 3
    first_part = pair_count - 2 * third_part
    pieces = []
    for column, amount in ((0, first_part), (1, third_part), (2, third_part)):
        frequency = jnp.power(10000.0, -jnp.arange(amount, dtype=f32) / amount)
        pieces.append(positions[column].astype(f32)[:, None] * frequency[None, :])
    angles = jnp.repeat(jnp.concatenate(pieces, 1), 2, 1)
    sign = jnp.where(jnp.arange(HD) % 2 == 0, -1.0, 1.0)
    return jnp.cos(angles), jnp.sin(angles) * sign


def swap_pairs(values):
    rows, width = values.shape
    index = jnp.arange(HD)
    exchange = (index[:, None] == (index[None, :] ^ 1)).astype(f32)
    flat = values.reshape(rows, width // HD, HD)
    turned = lax.dot_general(
        flat, exchange, (((2,), (0,)), ((), ())), precision=lax.Precision.HIGHEST
    )
    return turned.reshape(rows, width)


def rotate(values, cosine, sine):
    heads = values.shape[1] // HD
    return values * jnp.tile(cosine, (1, heads)) + swap_pairs(values) * jnp.tile(sine, (1, heads))


def rotate_back(grad, cosine, sine):
    heads = grad.shape[1] // HD
    return grad * jnp.tile(cosine, (1, heads)) + swap_pairs(grad * jnp.tile(sine, (1, heads)))


def attend(query, keys, values, allowed):
    scale = 1.0 / math.sqrt(HD)
    results, totals = [], []
    for head in range(query.shape[1] // HD):
        at = slice(head * HD, (head + 1) * HD)
        scores = jnp.where(allowed, dot_nt(query[:, at], keys[:, at]) * scale, masked_score)
        peak = jnp.max(scores, -1, keepdims=True)
        weights = jnp.where(allowed, jnp.exp(scores - peak), 0.0)
        total = jnp.sum(weights, -1, keepdims=True)
        results.append(dot(weights.astype(bf16), values[:, at]) / total)
        totals.append(peak + jnp.log(total))
    return jnp.concatenate(results, 1), totals


def attend_back(query, keys, values, grad, out, totals, allowed):
    scale = 1.0 / math.sqrt(HD)
    grad_query, grad_keys, grad_values = [], [], []
    for head in range(query.shape[1] // HD):
        at = slice(head * HD, (head + 1) * HD)
        q, k, v, g = query[:, at], keys[:, at], values[:, at], grad[:, at]
        delta = jnp.sum(g.astype(f32) * out[:, at], -1, keepdims=True)
        probs = jnp.where(allowed, jnp.exp(dot_nt(q, k) * scale - totals[head]), 0.0)
        grad_scores = (probs * (dot_nt(g, v) - delta)).astype(bf16)
        grad_query.append(dot(grad_scores, k) * scale)
        grad_keys.append(dot_tn(grad_scores, q) * scale)
        grad_values.append(dot_tn(probs.astype(bf16), g))
    return tuple(jnp.concatenate(parts, 1) for parts in (grad_query, grad_keys, grad_values))


def on_device(
    tokens,
    context,
    cotangent,
    positions,
    sequence_lengths,
    sequence_adapter,
    text_token_count,
    timestep_modulation,
    modulation,
    gains,
    query_key_value_weight,
    output_weight,
    up_weight,
    down_weight,
    first_factors,
    down_first_factor,
    second_factors,
    up_second_factor,
):
    place = Place()
    rows, width = tokens.shape
    seq_count, text_local = context.shape[:2]
    layers = query_key_value_weight.shape[0]
    columns = first_factors.shape[3]
    rank = place.outer * seq_count * ADAPTER_RANK
    own = width // TENSOR
    wide = up_weight.shape[2] // TENSOR
    set_rows = TENSOR * rows

    table = jnp.zeros((place.rep, seq_count), jnp.int32)
    arrived = sequence_adapter
    for k in range(place.outer):
        arrived = sequence_adapter if k == 0 else place.other_outer(sequence_adapter, k)
        for m, values in enumerate((arrived, place.other_core(arrived))):
            here = jnp.arange(place.rep) == (place.r ^ (2 * k + m))
            table = jnp.where(here[:, None], values[None], table)

    def chooser(adapters):
        column = (adapters[:, None] * ADAPTER_RANK + jnp.arange(ADAPTER_RANK)[None, :]).reshape(-1)
        return (jnp.arange(columns)[:, None] == column[None, :]).astype(bf16)

    choosers = [chooser(table[half::2].reshape(-1)) for half in range(2)]
    choose = jnp.concatenate(choosers, 1)

    def down_columns(factor):
        return dot(factor, choose).astype(bf16).reshape(factor.shape[0], 2, rank)

    def up_columns(factor):
        return dot_tn(factor, choose).astype(bf16).reshape(factor.shape[1], 2, rank)

    numbers = jnp.concatenate([positions.reshape(-1), sequence_lengths, text_token_count])
    numbers = place.swap(numbers)
    state = place.swap(tokens).astype(f32)
    times = place.swap(timestep_modulation)
    positions = numbers[: 3 * rows].reshape(3, rows)
    lengths, counts = [
        numbers[3 * rows + k * seq_count : 3 * rows + (k + 1) * seq_count] for k in range(2)
    ]

    bounds = jnp.cumsum(lengths)

    def first_index(core, block, part):
        return core * place.half + block * TENSOR + part

    def token_segments(index):
        packed = jnp.arange(rows, dtype=jnp.int32) * place.size + index
        return jnp.sum((packed[:, None] >= bounds[None, :]).astype(jnp.int32), 1)

    def text_marks(index):
        at = index * text_local + jnp.arange(text_local)
        marks = jnp.where(at[None, :] < counts[:, None], jnp.arange(seq_count)[:, None], -1)
        return marks.reshape(-1)

    def over_set(function, core, block):
        return jnp.concatenate(
            [function(first_index(core, block, place.p ^ k)) for k in range(TENSOR)]
        )

    def over_group(function):
        return jnp.concatenate(
            [
                over_set(function, core, place.b ^ k)
                for core in (place.c, 1 - place.c)
                for k in range(place.blocks)
            ]
        )

    segment = over_set(token_segments, place.c, place.b)
    sequence = jnp.minimum(segment, seq_count - 1)
    self_allowed = segment[:, None] == over_group(token_segments)[None, :]
    cross_allowed = sequence[:, None] == over_group(text_marks)[None, :]
    column_sequence = jnp.arange(rank) // ADAPTER_RANK - (place.r // 2) * seq_count
    mask = (sequence[:, None] == column_sequence[None, :]) & (segment < seq_count)[:, None]
    mask = mask.astype(f32)
    text_sequence = jnp.tile(jnp.repeat(jnp.arange(seq_count), text_local), TENSOR)
    text_mask = (text_sequence[:, None] == column_sequence[None, :]).astype(f32)
    valid = (segment[:rows] < seq_count).astype(f32)[:, None]

    def mods_of(layer):
        table = modulation[layer][None] + times
        chosen = [table[0, k][None] for k in range(6)]
        for s in range(1, seq_count):
            here = (sequence[:rows] == s)[:, None]
            chosen = [jnp.where(here, table[s, k][None], chosen[k]) for k in range(6)]
        return chosen

    def own_gain(layer, index):
        return lax.dynamic_slice_in_dim(gains[layer, index], place.p * own, own, 0)[None]

    fetched = []
    after = choose
    for layer in range(layers):
        qkv, proj = query_key_value_weight[layer], output_weight[layer]
        first, second = first_factors[layer], second_factors[layer]
        down = [down_columns(first[k]) for k in range(9)]
        up = [up_columns(second[k]) for k in range(9)]
        self_in, after = place.fetch_columns(
            [qkv[0], qkv[1], qkv[2]], [down[0], down[1], down[2], up[3]], after
        )
        self_out, after = place.fetch_rows(proj[0], [down[3], up[0], up[1], up[2]], after)
        cross_in, after = place.fetch_columns(
            [qkv[3], qkv[4], qkv[5]], [down[4], down[5], down[6], up[7]], after
        )
        cross_out, after = place.fetch_rows(proj[1], [down[7], up[4], up[5], up[6]], after)
        ffn_in, after = place.fetch_columns([up_weight[layer]], [down[8], up[8]], after)
        ffn_out, after = place.fetch_rows(
            down_weight[layer],
            [down_columns(down_first_factor[layer]), up_columns(up_second_factor[layer])],
            after,
        )
        fetched.append((self_in, self_out, cross_in, cross_out, ffn_in, ffn_out))

    cotangent = place.swap(cotangent)
    text = place.gather(place.swap(context.reshape(seq_count * text_local, width)))
    positions = jnp.stack([positions] + [place.part(positions, k) for k in range(1, TENSOR)], 1)
    cosine, sine = rotary_tables(positions.reshape(3, set_rows))

    def column(value):
        return value.reshape(-1, 1)

    def rms_scales(values):
        squares = jnp.stack([jnp.sum(v * v, -1).reshape(TENSOR, -1) for v in values])
        total = place.total(squares)
        return [column(lax.rsqrt(t / width + epsilon)) for t in total]

    def rms_backs(items):
        scaled = [(v * s, s, g * w) for v, s, w, g in items]
        along = jnp.stack([jnp.sum(h * g, -1).reshape(TENSOR, -1) for h, s, g in scaled])
        along = place.total(along) / width
        return [s * (g - h * column(a)) for (h, s, g), a in zip(scaled, along)]

    def extra(bundle, start, index):
        return bundle[:, start + index * rank : start + (index + 1) * rank]

    def narrow(values, mask):
        return (values * mask).astype(bf16)

    saved = []
    for layer in range(layers):
        self_in, self_out, cross_in, cross_out, ffn_in, ffn_out = fetched[layer]
        shift_one, scale_one, gate_one, shift_two, scale_two, gate_two = mods_of(layer)
        normed = (norm_parts(state)[0] * (1.0 + scale_one) + shift_one).astype(bf16)
        normed = place.gather(normed)
        raw = dot(normed, self_in)
        self_inner = [
            narrow(raw[:, 3 * own + k * rank : 3 * own + (k + 1) * rank], mask) for k in range(3)
        ]
        query_raw, key_raw, value_raw = [
            raw[:, k * own : (k + 1) * own] + dot_nt(self_inner[k], extra(self_out, width, 1 + k))
            for k in range(3)
        ]
        query_scale, key_scale = rms_scales([query_raw, key_raw])
        query = rotate(query_raw * query_scale * own_gain(layer, 0), cosine, sine).astype(bf16)
        keys = rotate(key_raw * key_scale * own_gain(layer, 1), cosine, sine).astype(bf16)
        both = place.spread(jnp.concatenate([keys, value_raw.astype(bf16)], 1))
        keys, values = both[:, :own], both[:, own:]
        self_result, self_totals = attend(query, keys, values, self_allowed)
        attended = self_result.astype(bf16)
        raw = dot(attended, self_out[:, : width + rank])
        out_inner = narrow(raw[:, width:], mask)
        branch = raw[:, :width] + dot_nt(out_inner, extra(self_in, 3 * own, 3))
        state_one = state + valid * gate_one * place.scatter(branch)

        normed_cross = (norm_parts(state_one)[0] * gains[layer, 4][None]).astype(bf16)
        normed_cross = place.gather(normed_cross)
        cross_inner = narrow(dot(normed_cross, extra(cross_in, 3 * own, 0)), mask)
        cross_raw = dot(normed_cross, cross_in[:, :own]) + dot_nt(
            cross_inner, extra(cross_out, width, 1)
        )
        text_raw = dot(text, cross_in[:, own : 3 * own])
        text_inner = [narrow(dot(text, extra(cross_in, 3 * own, k)), text_mask) for k in (1, 2)]
        text_key_raw, text_value_raw = [
            text_raw[:, k * own : (k + 1) * own]
            + dot_nt(text_inner[k], extra(cross_out, width, 2 + k))
            for k in range(2)
        ]
        (text_scale,) = rms_scales([text_key_raw])
        text_keys = (text_key_raw * text_scale * own_gain(layer, 3)).astype(bf16)
        both = place.spread(jnp.concatenate([text_keys, text_value_raw.astype(bf16)], 1))
        text_keys, text_values = both[:, :own], both[:, own:]
        (cross_scale,) = rms_scales([cross_raw])
        cross_query = (cross_raw * cross_scale * own_gain(layer, 2)).astype(bf16)
        cross_result, cross_totals = attend(cross_query, text_keys, text_values, cross_allowed)
        crossed = cross_result.astype(bf16)
        raw = dot(crossed, cross_out[:, : width + rank])
        crossed_inner = narrow(raw[:, width:], mask)
        branch = raw[:, :width] + dot_nt(crossed_inner, extra(cross_in, 3 * own, 3))
        state_two = state_one + valid * place.scatter(branch)

        normed_ffn = (norm_parts(state_two)[0] * (1.0 + scale_two) + shift_two).astype(bf16)
        normed_ffn = place.gather(normed_ffn)
        up_inner = narrow(dot(normed_ffn, extra(ffn_in, wide, 0)), mask)
        up_raw = dot(normed_ffn, ffn_in[:, :wide]) + dot_nt(up_inner, extra(ffn_out, width, 1))
        hidden = jax.nn.gelu(up_raw, approximate=True).astype(bf16)
        raw = dot(hidden, ffn_out[:, : width + rank])
        down_inner = narrow(raw[:, width:], mask)
        branch = raw[:, :width] + dot_nt(down_inner, extra(ffn_in, wide, 1))
        saved.append(
            (
                (state, state_one, state_two),
                (scale_one, gate_one, scale_two, gate_two),
                (normed, self_inner, query_raw, key_raw, query_scale, key_scale),
                (query, keys, values, self_result, self_totals, attended, out_inner),
                (normed_cross, cross_inner, cross_raw, cross_scale, cross_query),
                (text_inner, text_key_raw, text_scale, text_keys, text_values),
                (cross_result, cross_totals, crossed, crossed_inner),
                (normed_ffn, up_inner, up_raw, hidden, down_inner),
            )
        )
        state = state_two + valid * gate_two * place.scatter(branch)

    grad = cotangent.astype(f32)
    grad_text = jnp.zeros((TENSOR * seq_count * text_local, width), f32)
    whole_grads, part_grads, wide_grads = [], [], []
    for layer in reversed(range(layers)):
        self_in, self_out, cross_in, cross_out, ffn_in, ffn_out = fetched[layer]
        (
            (state_zero, state_one, state_two),
            (scale_one, gate_one, scale_two, gate_two),
            (normed, self_inner, query_raw, key_raw, query_scale, key_scale),
            (query, keys, values, self_result, self_totals, attended, out_inner),
            (normed_cross, cross_inner, cross_raw, cross_scale, cross_query),
            (text_inner, text_key_raw, text_scale, text_keys, text_values),
            (cross_result, cross_totals, crossed, crossed_inner),
            (normed_ffn, up_inner, up_raw, hidden, down_inner),
        ) = saved[layer]

        grad_down = place.gather((grad * (valid * gate_two)).astype(bf16))
        down_back = narrow(dot(grad_down, extra(ffn_in, wide, 1)), mask)
        grad_hidden = dot_nt(
            jnp.concatenate([grad_down, down_back], 1), ffn_out[:, : width + rank]
        )
        gelu_back = jax.vjp(lambda raw: jax.nn.gelu(raw, approximate=True), up_raw)[1]
        grad_up = gelu_back(grad_hidden)[0].astype(bf16)
        up_back = narrow(dot(grad_up, extra(ffn_out, width, 1)), mask)
        grad_normed = place.scatter(
            dot_nt(jnp.concatenate([grad_up, up_back], 1), ffn_in[:, : wide + rank])
        )
        grad_two = grad + layer_norm_back(state_two, grad_normed * (1.0 + scale_two))

        grad_branch = place.gather((grad_two * valid).astype(bf16))
        crossed_back = narrow(dot(grad_branch, extra(cross_in, 3 * own, 3)), mask)
        grad_crossed = dot_nt(
            jnp.concatenate([grad_branch, crossed_back], 1), cross_out[:, : width + rank]
        ).astype(bf16)
        grad_query, grad_keys, grad_values = attend_back(
            cross_query, text_keys, text_values, grad_crossed, cross_result, cross_totals,
            cross_allowed,
        )
        (grad_cross_raw,) = rms_backs([(cross_raw, cross_scale, own_gain(layer, 2), grad_query)])
        grad_cross_raw = grad_cross_raw.astype(bf16)
        cross_back = narrow(dot(grad_cross_raw, extra(cross_out, width, 1)), mask)
        grad_normed = place.scatter(
            dot_nt(grad_cross_raw, cross_in[:, :own])
            + dot_nt(cross_back, extra(cross_in, 3 * own, 0))
        )
        grad_one = grad_two + layer_norm_back(state_one, grad_normed * gains[layer, 4][None])

        both = place.collect(jnp.concatenate([grad_keys, grad_values], 1))
        (grad_text_key,) = rms_backs(
            [(text_key_raw, text_scale, own_gain(layer, 3), both[:, :own])]
        )
        grad_text_raw = jnp.concatenate([grad_text_key, both[:, own:]], 1).astype(bf16)
        grad_text_key, grad_text_value = grad_text_raw[:, :own], grad_text_raw[:, own:]
        text_key_back = narrow(dot(grad_text_key, extra(cross_out, width, 2)), text_mask)
        text_value_back = narrow(dot(grad_text_value, extra(cross_out, width, 3)), text_mask)
        grad_text = (
            grad_text
            + dot_nt(grad_text_raw, cross_in[:, own : 3 * own])
            + dot_nt(text_key_back, extra(cross_in, 3 * own, 1))
            + dot_nt(text_value_back, extra(cross_in, 3 * own, 2))
        )

        grad_branch_self = place.gather((grad_one * (valid * gate_one)).astype(bf16))
        out_back = narrow(dot(grad_branch_self, extra(self_in, 3 * own, 3)), mask)
        grad_attended = dot_nt(
            jnp.concatenate([grad_branch_self, out_back], 1), self_out[:, : width + rank]
        ).astype(bf16)
        grad_query, grad_keys, grad_values = attend_back(
            query, keys, values, grad_attended, self_result, self_totals, self_allowed
        )
        both = place.collect(jnp.concatenate([grad_keys, grad_values], 1))
        grad_query_raw, grad_key_raw = rms_backs(
            [
                (query_raw, query_scale, own_gain(layer, 0), rotate_back(grad_query, cosine, sine)),
                (key_raw, key_scale, own_gain(layer, 1), rotate_back(both[:, :own], cosine, sine)),
            ]
        )
        raw_grads = [
            grad_query_raw.astype(bf16), grad_key_raw.astype(bf16), both[:, own:].astype(bf16)
        ]
        self_backs = [
            narrow(dot(raw_grads[k], extra(self_out, width, 1 + k)), mask) for k in range(3)
        ]
        grad_normed = place.scatter(
            dot_nt(
                jnp.concatenate(raw_grads + self_backs, 1), self_in[:, : 3 * own + 3 * rank]
            )
        )
        grad = grad_one + layer_norm_back(state_zero, grad_normed * (1.0 + scale_one))

        whole_grads.append(
            [
                dot_tn(normed, jnp.concatenate(self_backs, 1)),
                dot_tn(normed_cross, cross_back),
                dot_tn(text, jnp.concatenate([text_key_back, text_value_back], 1)),
                dot_tn(normed_ffn, up_back),
                dot_tn(grad_branch_self, out_inner),
                dot_tn(grad_branch, crossed_inner),
                dot_tn(grad_down, down_inner),
            ]
        )
        part_grads.append(
            [
                dot_tn(attended, out_back),
                dot_tn(crossed, crossed_back),
                dot_tn(raw_grads[0], self_inner[0]),
                dot_tn(raw_grads[1], self_inner[1]),
                dot_tn(raw_grads[2], self_inner[2]),
                dot_tn(grad_cross_raw, cross_inner),
                dot_tn(grad_text_key, text_inner[0]),
                dot_tn(grad_text_value, text_inner[1]),
            ]
        )
        wide_grads.append([dot_tn(hidden, down_back), dot_tn(grad_up, up_inner)])

    def flat(lists):
        return jnp.concatenate([item for items in reversed(lists) for item in items], 1)

    whole_all = flat(whole_grads).astype(bf16)
    whole_all = jnp.concatenate(
        [lax.dynamic_slice_in_dim(whole_all, (place.p ^ k) * own, own, 0) for k in range(TENSOR)]
    )
    from_parts = place.scatter(whole_all)

    def sum_set(values):
        values = values + place.other_core(values.astype(bf16)).astype(f32)
        result = values
        for k in range(1, place.blocks):
            result = result + place.other_block(values.astype(bf16), k).astype(f32)
        return result.astype(bf16)

    narrow_all = sum_set(jnp.concatenate([from_parts, flat(part_grads)], 1))
    wide_all = sum_set(flat(wide_grads))

    def to_owner(values, turn):
        count = values.shape[0] // place.shards
        shard = place.b + place.blocks * (place.h ^ turn)
        piece = lax.dynamic_slice_in_dim(values, shard * count, count, 0)

        def move(f):
            h, rest = divmod(f, place.half)
            b, p = divmod(rest, TENSOR)
            return place.shards * p + b + place.blocks * (h ^ turn)

        return place.send_rows(piece, move)

    def all_groups(values):
        pieces = jnp.concatenate([to_owner(values, 0), to_owner(values, 1)], 1)
        total = pieces.astype(f32)
        for k in range(1, place.outer):
            total = total + place.other_outer(pieces, k).astype(f32)
        total = total.astype(bf16)
        return total[:, : values.shape[1]], total[:, values.shape[1] :]

    narrow_pieces = all_groups(narrow_all)
    wide_pieces = all_groups(wide_all)
    mine = place.f % place.shards // place.blocks
    choose_all = jnp.concatenate(
        [
            jnp.where(mine == 0, choosers[0], choosers[1]),
            jnp.where(mine == 0, choosers[1], choosers[0]),
        ],
        1,
    )

    def pick(pieces, index):
        return jnp.concatenate([p[:, index * rank : (index + 1) * rank] for p in pieces], 1)

    whole_count, part_count = 10, 8
    lora_a, lora_b, lora_a_down, lora_b_up = [], [], [], []
    for layer in range(layers):
        base = layer * whole_count
        q_a, k_a, v_a, cq_a, ck_a, cv_a, up_a, o_b, co_b, down_b = range(base, base + whole_count)
        base = layers * whole_count + layer * part_count
        o_a, co_a, q_b, k_b, v_b, cq_b, ck_b, cv_b = range(base, base + part_count)
        a_order = (q_a, k_a, v_a, o_a, cq_a, ck_a, cv_a, co_a, up_a)
        b_order = (q_b, k_b, v_b, o_b, cq_b, ck_b, cv_b, co_b, down_b)
        lora_a.append(jnp.stack([dot_nt(pick(narrow_pieces, k), choose_all) for k in a_order]))
        lora_b.append(jnp.stack([dot_nt(choose_all, pick(narrow_pieces, k)) for k in b_order]))
        lora_a_down.append(dot_nt(pick(wide_pieces, 2 * layer), choose_all))
        lora_b_up.append(dot_nt(choose_all, pick(wide_pieces, 2 * layer + 1)))

    grad_text = place.swap(place.scatter(grad_text).astype(bf16)).astype(f32)
    return (
        place.swap(state.astype(bf16)),
        place.swap(grad.astype(bf16)).astype(f32),
        grad_text.reshape(context.shape),
        jnp.stack(lora_a),
        jnp.stack(lora_a_down),
        jnp.stack(lora_b),
        jnp.stack(lora_b_up),
    )


def solution(mesh):
    rep, fsdp = AXES
    in_specs = (
        P(AXES, None),
        P(rep, fsdp, None),
        P(AXES, None),
        P(None, AXES),
        P(rep),
        P(rep),
        P(rep),
        P(rep, None, None),
        P(),
        P(),
        P(None, None, fsdp, None),
        P(None, None, fsdp, None),
        P(None, fsdp, None),
        P(None, fsdp, None),
        P(None, None, fsdp, None),
        P(None, fsdp, None),
        P(None, None, None, fsdp),
        P(None, None, fsdp),
    )
    out_specs = (
        P(AXES, None),
        P(AXES, None),
        P(rep, fsdp, None),
        P(None, None, fsdp, None),
        P(None, fsdp, None),
        P(None, None, None, fsdp),
        P(None, None, fsdp),
    )
    return jax.shard_map(
        on_device, mesh=mesh, in_specs=in_specs, out_specs=out_specs, check_vma=False
    )
```

profile of v0, /device:TPU:1, one launch (start us, length us, event | category | flops | bytes accessed | tf_op | source)
XLA Modules:
  0.0 1864.7 jit_solution(13759583378157574988)
XLA Ops:
  173.4 7.8 collective-permute-start.11
  351.0 7.4 collective-permute-done.78
  360.1 11.7 collective-permute-done.79
  373.5 12.3 collective-permute-start.47
  405.4 7.6 collective-permute-done.53
  427.6 11.0 collective-permute-done.48
  438.5 9.0 collective-permute-start.85
  486.5 17.8 collective-permute-start.99
  596.2 9.5 collective-permute-start.19
  722.0 13.6 collective-permute-done.159
  744.8 7.8 collective-permute-start.87
  769.5 21.3 %collective-permute-done.138 = bf16[2,48,1664]{2,1,0:T(8,128)(2,1)} collective-permute-done((bf16[2,48,1664]{2,1,0:T(8,128)(2,1)S(1)}, bf16[2,48,1664]{2,1,0:T(8,128)(2,1)}, u32[]{:S(2)}, u32[]{:S(2)}) %collective-permute-start.138) | collective-permute-done | bytes 319520 | tf_op jit(solution)/shard_map/ppermute | solution.py:56
  832.0 22.3 %collective-permute-done.32 = bf16[256,768]{0,1:T(8,128)(2,1)S(1)} collective-permute-done((bf16[256,768]{0,1:T(8,128)(2,1)S(1)}, bf16[256,768]{0,1:T(8,128)(2,1)S(1)}, u32[]{:S(2)}, u32[]{:S(2)}) %collective-permute-start.32) | collective-permute-done | bytes 393248 | tf_op jit(solution)/shard_map/ppermute | solution.py:60
  857.7 8.5 collective-permute-start.33
  866.5 13.9 collective-permute-done.33
  887.8 16.8 collective-permute-start.37
  905.4 8.2 collective-permute-done.37
  954.4 7.3 collective-permute-done.67
  964.8 7.0 collective-permute-done.69
  1007.1 10.3 multiply_convert_fusion.1
  1017.4 8.2 fusion.14
  1266.3 11.3 multiply_convert_fusion
  1277.6 9.5 fusion.35
  1292.1 7.9 fusion.58
  1301.5 7.3 fusion.10
  1342.1 16.6 collective-permute-start.174
  1534.3 10.3 fusion.28
  1548.4 7.6 fusion.61
  1584.6 13.1 collective-permute-done.216
  1619.5 9.3 collective-permute-start.243
  1812.8 19.5 %collective-permute-done.258 = bf16[192,1152]{1,0:T(8,128)(2,1)S(1)} collective-permute-done((bf16[192,1152]{1,0:T(8,128)(2,1)}, bf16[192,1152]{1,0:T(8,128)(2,1)S(1)}, u32[]{:S(2)}, u32[]{:S(2)}) %collective-permute-start.258) | collective-permute-done | bytes 442400 | tf_op jit(solution)/shard_map/ppermute | solution.py:60
  1838.0 9.4 collective-permute-done.238
  (2923 shorter events, 1490.3 us)
Async XLA Ops:
  0.6 62.4 %collective-permute-start.9 = (s32[1]{0:T(128)}, s32[1]{0:T(128)}, u32[]{:S(2)}, u32[]{:S(2)}) collective-permute-start(s32[1]{0:T(128)} %param.23), channel_id=1, source_target_pairs={{0,8},{1,9},{2,10},{3,11},{4,12},{5,13},{6,14},{7,15},{8,0},{9,1},... | collective-permute-start | bytes 20 | tf_op jit(solution)/shard_map/ppermute | solution.py:56
  0.8 62.3 %collective-permute-start.7 = (s32[1]{0:T(128)}, s32[1]{0:T(128)}, u32[]{:S(2)}, u32[]{:S(2)}) collective-permute-start(s32[1]{0:T(128)} %param.23), channel_id=1, source_target_pairs={{0,16},{1,17},{2,18},{3,19},{4,20},{5,21},{6,22},{7,23},{8,24},{9,... | collective-permute-start | bytes 20 | tf_op jit(solution)/shard_map/ppermute | solution.py:56
  5.5 140.3 %collective-permute-start.1 = (s32[386]{0:T(512)S(1)}, s32[386]{0:T(512)S(1)}, u32[]{:S(2)}, u32[]{:S(2)}) collective-permute-start(s32[386]{0:T(512)S(1)} %pad_add_fusion.1), channel_id=1, source_target_pairs={{0,0},{1,1},{2,2},{3,3},{4,8},{5,9},{6,10},{7,11},{8,4},{9,5},{10,... | collective-permute-start | bytes 4640 | tf_op jit(solution)/shard_map/ppermute | solution.py:56
  11.8 233.1 %collective-permute-start = (bf16[128,1536]{0,1:T(8,128)(2,1)}, bf16[128,1536]{0,1:T(8,128)(2,1)S(1)}, u32[]{:S(2)}, u32[]{:S(2)}) collective-permute-start(bf16[128,1536]{0,1:T(8,128)(2,1)} %copy.804), channel_id=1, source_target_pairs={{0,0},{1,1},{2,2},{3,3},{4,8},{5,9},{6,10},{7,11},{8,4},{9,5},{10,... | collective-permute-start | bytes 1179656 | tf_op jit(solution)/shard_map/ppermute | solution.py:56
  13.9 155.1 %collective-permute-start.2 = (f32[1,6,1536]{2,0,1:T(1,128)}, f32[1,6,1536]{2,0,1:T(1,128)}, u32[]{:S(2)}, u32[]{:S(2)}) collective-permute-start(f32[1,6,1536]{2,0,1:T(1,128)} %param.25), channel_id=1, source_target_pairs={{0,0},{1,1},{2,2},{3,3},{4,8},{5,9},{6,10},{7,11},{8,4},{9,5},{10,... | collective-permute-start | bytes 110600 | tf_op jit(solution)/shard_map/ppermute | solution.py:56
  158.5 55.5 %collective-permute-start.58 = (bf16[64,1536]{1,0:T(8,128)(2,1)}, bf16[64,1536]{1,0:T(8,128)(2,1)}, u32[]{:S(2)}, u32[]{:S(2)}) collective-permute-start(bf16[64,1536]{1,0:T(8,128)(2,1)} %bitcast.182), channel_id=1, source_target_pairs={{0,0},{1,1},{2,2},{3,3},{4,8},{5,9},{6,10},{7,11},{8,4},{9,5},{10,... | collective-permute-start | bytes 589832 | tf_op jit(solution)/shard_map/ppermute | solution.py:56
  161.4 822.2 %collective-permute-start.175 = (bf16[128,1536]{0,1:T(8,128)(2,1)}, bf16[128,1536]{0,1:T(8,128)(2,1)S(1)}, u32[]{:S(2)}, u32[]{:S(2)}) collective-permute-start(bf16[128,1536]{0,1:T(8,128)(2,1)} %copy.939), channel_id=1, source_target_pairs={{0,0},{1,1},{2,2},{3,3},{4,8},{5,9},{6,10},{7,11},{8,4},{9,5},{10,... | collective-permute-start | bytes 1179656 | tf_op jit(solution)/shard_map/ppermute | solution.py:56
  205.9 210.1 %collective-permute-start.17 = (bf16[8,48,1280]{2,1,0:T(8,128)(2,1)}, bf16[8,48,1280]{2,1,0:T(8,128)(2,1)}, u32[]{:S(2)}, u32[]{:S(2)}) collective-permute-start(bf16[8,48,1280]{2,1,0:T(8,128)(2,1)} %bitcast_dynamic-update-slice_fusion.100), channel_id=1, source_target_pairs={{0,8},{1,9},{2,10},{3,11},{4,12},{5,13},{6,14},{7,15},{8,0},{9,1},... | collective-permute-start | bytes 2949128 | tf_op jit(solution)/shard_map/ppermute | solution.py:56
  246.8 72.1 %collective-permute-start.22 = (bf16[2,48,1664]{2,1,0:T(8,128)(2,1)}, bf16[2,48,1664]{2,1,0:T(8,128)(2,1)}, u32[]{:S(2)}, u32[]{:S(2)}) collective-permute-start(bf16[2,48,1664]{2,1,0:T(8,128)(2,1)} %bitcast_dynamic-update-slice_fusion.74), channel_id=1, source_target_pairs={{0,8},{1,9},{2,10},{3,11},{4,12},{5,13},{6,14},{7,15},{8,0},{9,1},... | collective-permute-start | bytes 958472 | tf_op jit(solution)/shard_map/ppermute | solution.py:56
  284.3 41.1 %collective-permute-start.23 = (bf16[2,48,1664]{2,1,0:T(8,128)(2,1)}, bf16[2,48,1664]{2,1,0:T(8,128)(2,1)}, u32[]{:S(2)}, u32[]{:S(2)}) collective-permute-start(bf16[2,48,1664]{2,1,0:T(8,128)(2,1)} %bitcast_dynamic-update-slice_fusion.74), channel_id=1, source_target_pairs={{0,16},{1,17},{2,18},{3,19},{4,20},{5,21},{6,22},{7,23},{8,24},{9,... | collective-permute-start | bytes 958472 | tf_op jit(solution)/shard_map/ppermute | solution.py:56
  327.4 91.7 %collective-permute-start.18 = (bf16[8,48,1280]{2,1,0:T(8,128)(2,1)}, bf16[8,48,1280]{2,1,0:T(8,128)(2,1)}, u32[]{:S(2)}, u32[]{:S(2)}) collective-permute-start(bf16[8,48,1280]{2,1,0:T(8,128)(2,1)} %bitcast_dynamic-update-slice_fusion.100), channel_id=1, source_target_pairs={{0,16},{1,17},{2,18},{3,19},{4,20},{5,21},{6,22},{7,23},{8,24},{9,... | collective-permute-start | bytes 2949128 | tf_op jit(solution)/shard_map/ppermute | solution.py:56
  330.8 42.7 %collective-permute-start.81 = (bf16[48,2304]{1,0:T(8,128)(2,1)S(1)}, bf16[48,2304]{1,0:T(8,128)(2,1)S(1)}, u32[]{:S(2)}, u32[]{:S(2)}) collective-permute-start(bf16[48,2304]{1,0:T(8,128)(2,1)S(1)} %copy-done.267), channel_id=1, source_target_pairs={{0,7},{1,6},{2,5},{3,4},{4,3},{5,2},{6,1},{7,0},{8,15},{9,14},{10,... | collective-permute-start | bytes 663560 | tf_op jit(solution)/shard_map/ppermute | solution.py:60
  373.5 49.5 %collective-permute-start.47 = (bf16[8,48,1280]{2,1,0:T(8,128)(2,1)}, bf16[8,48,1280]{2,1,0:T(8,128)(2,1)}, u32[]{:S(2)}, u32[]{:S(2)}) collective-permute-start(bf16[8,48,1280]{2,1,0:T(8,128)(2,1)} %bitcast_dynamic-update-slice_fusion.92), channel_id=1, source_target_pairs={{0,8},{1,9},{2,10},{3,11},{4,12},{5,13},{6,14},{7,15},{8,0},{9,1},... | collective-permute-start | bytes 2949128 | tf_op jit(solution)/shard_map/ppermute | solution.py:56
  416.0 195.9 %collective-permute-start.6 = (bf16[128,768]{0,1:T(8,128)(2,1)}, bf16[128,768]{0,1:T(8,128)(2,1)}, u32[]{:S(2)}, u32[]{:S(2)}) collective-permute-start(bf16[128,768]{0,1:T(8,128)(2,1)} %slice.3446), channel_id=1, source_target_pairs={{0,1},{1,0},{2,3},{3,2},{4,5},{5,4},{6,7},{7,6},{8,9},{9,8},{10,11... | collective-permute-start | bytes 589832 | tf_op jit(solution)/shard_map/ppermute | solution.py:60
  422.3 189.8 %collective-permute-start.5 = (bf16[128,768]{0,1:T(8,128)(2,1)}, bf16[128,768]{0,1:T(8,128)(2,1)}, u32[]{:S(2)}, u32[]{:S(2)}) collective-permute-start(bf16[128,768]{0,1:T(8,128)(2,1)} %slice.3445), channel_id=1, source_target_pairs={{0,2},{1,3},{2,0},{3,1},{4,6},{5,7},{6,4},{7,5},{8,10},{9,11},{10,... | collective-permute-start | bytes 589832 | tf_op jit(solution)/shard_map/ppermute | solution.py:60
  460.7 43.6 %collective-permute-start.98 = (bf16[48,1280]{1,0:T(8,128)(2,1)}, bf16[48,1280]{1,0:T(8,128)(2,1)}, u32[]{:S(2)}, u32[]{:S(2)}) collective-permute-start(bf16[48,1280]{1,0:T(8,128)(2,1)} %concatenate.801), channel_id=1, source_target_pairs={{0,1},{1,0},{2,3},{3,2},{4,5},{5,4},{6,7},{7,6},{8,9},{9,8},{10,11... | collective-permute-start | bytes 368648 | tf_op jit(solution)/shard_map/ppermute | solution.py:60
  564.1 196.6 %collective-permute-start.82 = (bf16[8,48,2304]{2,1,0:T(8,128)(2,1)}, bf16[8,48,2304]{2,1,0:T(8,128)(2,1)}, u32[]{:S(2)}, u32[]{:S(2)}) collective-permute-start(bf16[8,48,2304]{2,1,0:T(8,128)(2,1)} %bitcast_dynamic-update-slice_fusion.60), channel_id=1, source_target_pairs={{0,8},{1,9},{2,10},{3,11},{4,12},{5,13},{6,14},{7,15},{8,0},{9,1},... | collective-permute-start | bytes 5308424 | tf_op jit(solution)/shard_map/ppermute | solution.py:56
  609.7 155.5 %collective-permute-start.83 = (bf16[8,48,2304]{2,1,0:T(8,128)(2,1)}, bf16[8,48,2304]{2,1,0:T(8,128)(2,1)}, u32[]{:S(2)}, u32[]{:S(2)}) collective-permute-start(bf16[8,48,2304]{2,1,0:T(8,128)(2,1)} %bitcast_dynamic-update-slice_fusion.60), channel_id=1, source_target_pairs={{0,16},{1,17},{2,18},{3,19},{4,20},{5,21},{6,22},{7,23},{8,24},{9,... | collective-permute-start | bytes 5308424 | tf_op jit(solution)/shard_map/ppermute | solution.py:56
  611.9 73.2 %collective-permute-start.49 = (bf16[8,48,1280]{2,1,0:T(8,128)(2,1)}, bf16[8,48,1280]{2,1,0:T(8,128)(2,1)}, u32[]{:S(2)}, u32[]{:S(2)}) collective-permute-start(bf16[8,48,1280]{2,1,0:T(8,128)(2,1)} %collective-permute-done.48), channel_id=1, source_target_pairs={{0,8},{1,9},{2,10},{3,11},{4,12},{5,13},{6,14},{7,15},{8,0},{9,1},... | collective-permute-start | bytes 2949128 | tf_op jit(solution)/shard_map/ppermute | solution.py:56
  744.8 170.0 %collective-permute-start.87 = (bf16[2,280,1600]{2,1,0:T(8,128)(2,1)}, bf16[2,280,1600]{2,1,0:T(8,128)(2,1)}, u32[]{:S(2)}, u32[]{:S(2)}) collective-permute-start(bf16[2,280,1600]{2,1,0:T(8,128)(2,1)} %bitcast_dynamic-update-slice_fusion.34), channel_id=1, source_target_pairs={{0,8},{1,9},{2,10},{3,11},{4,12},{5,13},{6,14},{7,15},{8,0},{9,1},... | collective-permute-start | bytes 5376008 | tf_op jit(solution)/shard_map/ppermute | solution.py:56
  752.6 44.0 %collective-permute-start.105 = (bf16[8,48,1280]{2,1,0:T(8,128)(2,1)}, bf16[8,48,1280]{2,1,0:T(8,128)(2,1)}, u32[]{:S(2)}, u32[]{:S(2)}) collective-permute-start(bf16[8,48,1280]{2,1,0:T(8,128)(2,1)} %bitcast_dynamic-update-slice_fusion.84), channel_id=1, source_target_pairs={{0,8},{1,9},{2,10},{3,11},{4,12},{5,13},{6,14},{7,15},{8,0},{9,1},... | collective-permute-start | bytes 2949128 | tf_op jit(solution)/shard_map/ppermute | solution.py:56
  856.7 70.3 %collective-permute-start.88 = (bf16[2,280,1600]{2,1,0:T(8,128)(2,1)}, bf16[2,280,1600]{2,1,0:T(8,128)(2,1)S(1)}, u32[]{:S(2)}, u32[]{:S(2)}) collective-permute-start(bf16[2,280,1600]{2,1,0:T(8,128)(2,1)} %bitcast_dynamic-update-slice_fusion.34), channel_id=1, source_target_pairs={{0,16},{1,17},{2,18},{3,19},{4,20},{5,21},{6,22},{7,23},{8,24},{9,... | collective-permute-start | bytes 5376008 | tf_op jit(solution)/shard_map/ppermute | solution.py:56
  913.6 225.3 %collective-permute-start.162 = (bf16[8,48,2304]{2,1,0:T(8,128)(2,1)}, bf16[8,48,2304]{2,1,0:T(8,128)(2,1)}, u32[]{:S(2)}, u32[]{:S(2)}) collective-permute-start(bf16[8,48,2304]{2,1,0:T(8,128)(2,1)} %bitcast_dynamic-update-slice_fusion.52), channel_id=1, source_target_pairs={{0,8},{1,9},{2,10},{3,11},{4,12},{5,13},{6,14},{7,15},{8,0},{9,1},... | collective-permute-start | bytes 5308424 | tf_op jit(solution)/shard_map/ppermute | solution.py:56
  919.8 230.2 %collective-permute-start.163 = (bf16[8,48,2304]{2,1,0:T(8,128)(2,1)}, bf16[8,48,2304]{2,1,0:T(8,128)(2,1)}, u32[]{:S(2)}, u32[]{:S(2)}) collective-permute-start(bf16[8,48,2304]{2,1,0:T(8,128)(2,1)} %bitcast_dynamic-update-slice_fusion.52), channel_id=1, source_target_pairs={{0,16},{1,17},{2,18},{3,19},{4,20},{5,21},{6,22},{7,23},{8,24},{9,... | collective-permute-start | bytes 5308424 | tf_op jit(solution)/shard_map/ppermute | solution.py:56
  1064.6 113.2 %collective-permute-start.167 = (bf16[2,280,1600]{2,1,0:T(8,128)(2,1)}, bf16[2,280,1600]{2,1,0:T(8,128)(2,1)}, u32[]{:S(2)}, u32[]{:S(2)}) collective-permute-start(bf16[2,280,1600]{2,1,0:T(8,128)(2,1)} %copy-done.57), channel_id=1, source_target_pairs={{0,8},{1,9},{2,10},{3,11},{4,12},{5,13},{6,14},{7,15},{8,0},{9,1},... | collective-permute-start | bytes 5376008 | tf_op jit(solution)/shard_map/ppermute | solution.py:56
  1076.8 104.7 %collective-permute-start.168 = (bf16[2,280,1600]{2,1,0:T(8,128)(2,1)}, bf16[2,280,1600]{2,1,0:T(8,128)(2,1)}, u32[]{:S(2)}, u32[]{:S(2)}) collective-permute-start(bf16[2,280,1600]{2,1,0:T(8,128)(2,1)} %copy-done.57), channel_id=1, source_target_pairs={{0,16},{1,17},{2,18},{3,19},{4,20},{5,21},{6,22},{7,23},{8,24},{9,... | collective-permute-start | bytes 5376008 | tf_op jit(solution)/shard_map/ppermute | solution.py:56
  1120.9 50.0 %collective-permute-start.146 = (bf16[256,768]{1,0:T(8,128)(2,1)}, bf16[256,768]{1,0:T(8,128)(2,1)}, u32[]{:S(2)}, u32[]{:S(2)}) collective-permute-start(bf16[256,768]{1,0:T(8,128)(2,1)} %pad_maximum_fusion.21), channel_id=1, source_target_pairs={{0,8},{1,9},{2,10},{3,11},{4,12},{5,13},{6,14},{7,15},{8,0},{9,1},... | collective-permute-start | bytes 1179656 | tf_op jit(solution)/shard_map/ppermute | solution.py:56
  1170.9 53.0 %collective-permute-start.164 = (bf16[8,48,2304]{2,1,0:T(8,128)(2,1)}, bf16[8,48,2304]{2,1,0:T(8,128)(2,1)}, u32[]{:S(2)}, u32[]{:S(2)}) collective-permute-start(bf16[8,48,2304]{2,1,0:T(8,128)(2,1)} %collective-permute-done.163), channel_id=1, source_target_pairs={{0,8},{1,9},{2,10},{3,11},{4,12},{5,13},{6,14},{7,15},{8,0},{9,1},... | collective-permute-start | bytes 5308424 | tf_op jit(solution)/shard_map/ppermute | solution.py:56
  1182.1 51.6 %collective-permute-start.169 = (bf16[2,280,1600]{2,1,0:T(8,128)(2,1)}, bf16[2,280,1600]{2,1,0:T(8,128)(2,1)}, u32[]{:S(2)}, u32[]{:S(2)}) collective-permute-start(bf16[2,280,1600]{2,1,0:T(8,128)(2,1)} %collective-permute-done.168), channel_id=1, source_target_pairs={{0,8},{1,9},{2,10},{3,11},{4,12},{5,13},{6,14},{7,15},{8,0},{9,1},... | collective-permute-start | bytes 5376008 | tf_op jit(solution)/shard_map/ppermute | solution.py:56
  1419.0 72.4 %collective-permute-start.241 = (f32[1,4,64]{2,1,0:T(4,128)}, f32[1,4,64]{2,1,0:T(4,128)}, u32[]{:S(2)}, u32[]{:S(2)}) collective-permute-start(f32[1,4,64]{2,1,0:T(4,128)} %stack_reshape.66), channel_id=1, source_target_pairs={{0,2},{1,3},{2,0},{3,1},{4,6},{5,7},{6,4},{7,5},{8,10},{9,11},{10,... | collective-permute-start | bytes 3080 | tf_op jit(solution)/shard_map/ppermute | solution.py:60
  1420.4 73.1 %collective-permute-start.240 = (f32[1,4,64]{2,1,0:T(4,128)}, f32[1,4,64]{2,1,0:T(4,128)}, u32[]{:S(2)}, u32[]{:S(2)}) collective-permute-start(f32[1,4,64]{2,1,0:T(4,128)} %stack_reshape.66), channel_id=1, source_target_pairs={{0,1},{1,0},{2,3},{3,2},{4,5},{5,4},{6,7},{7,6},{8,9},{9,8},{10,11... | collective-permute-start | bytes 3080 | tf_op jit(solution)/shard_map/ppermute | solution.py:60
  1684.0 85.6 %collective-permute-start.250 = (bf16[64,768]{1,0:T(8,128)(2,1)}, bf16[64,768]{1,0:T(8,128)(2,1)}, u32[]{:S(2)}, u32[]{:S(2)}) collective-permute-start(bf16[64,768]{1,0:T(8,128)(2,1)} %get-tuple-element.414), channel_id=1, source_target_pairs={{0,1},{1,0},{2,3},{3,2},{4,5},{5,4},{6,7},{7,6},{8,9},{9,8},{10,11... | collective-permute-start | bytes 294920 | tf_op jit(solution)/shard_map/ppermute | solution.py:60
  (905 other events, 9892.3 us)
where the time goes:
time: 1890 us; the launch traced here: 1860 us
  local copies, waits for them, and re-layouts  454 us (24%)
  starting transfers between devices  453 us (24%)
  waiting for transfers between devices  447 us (24%)
  matrix products  367 us (19%)
  other arithmetic  131 us (7%)
    ppermute x205, waiting for transfers between devices, send_rows(): return lax.ppermute(values, AXES[1], pairs)  381 us
    ppermute x205, starting transfers between devices, send_rows(): return lax.ppermute(values, AXES[1], pairs)  288 us
    ppermute x59, starting transfers between devices, send(): return lax.ppermute(values, AXES, pairs)  166 us
    dot_general x86, matrix products, dot(): return jnp.dot(left, right, preferred_element_type=f32)  157 us
    dot_general x104, matrix products, dot_nt(): lax.dot_general(left, right, (((1,), (1,)), ((), ())), preferred_element_...  137 us
    dynamic_update_slice x48, local copies, waits for them, and re-layouts, put(): return lax.dynamic_update_slice(whole, piece[:, None], (0, index, 0, 0))  91.6 us
    ppermute x59, waiting for transfers between devices, send(): return lax.ppermute(values, AXES, pairs)  65.7 us
    concatenate x48, local copies, waits for them, and re-layouts, fetch_columns(): piece = jnp.concatenate(pieces[k % TENSOR] + chosen, 1)  58.9 us
  transfers between devices with their start and end apart: 264, of which 119 were waited for; matrix products, arithmetic and copies ran while one was open for 44% of the time, Pallas kernels for 0%

commit v1 on v0

v1 whole, which is shorter than its diff:
```python
import functools
import math

import jax
import jax.numpy as jnp
from jax import lax
from jax.experimental import pallas as pl
from jax.experimental.pallas import tpu as pltpu
from jax.sharding import PartitionSpec as P

HD = 128
ADAPTER_RANK = 16
TENSOR = 4

AXES = ("o", "c", "z", "y")
epsilon = 1e-06
masked_score = -1e30
f32 = jnp.float32
bf16 = jnp.bfloat16
CHUNK = 256
SUBLANES = 8
BLOCK = 512
VMEM_BYTES = 32 << 20

NEAR = ((0, 0), (0, 1), (0, 2), (0, 4), (0, 5), (0, 6), (0, 8), (1, 3), (1, 7), (1, 8))
HEADS = ((0, 3), (0, 7), (1, 0), (1, 1), (1, 2), (1, 4), (1, 5), (1, 6))


def dot(left, right):
    return jnp.dot(left, right, preferred_element_type=f32)


def dot_nt(left, right):
    return lax.dot_general(left, right, (((1,), (1,)), ((), ())), preferred_element_type=f32)


def dot_tn(left, right):
    return lax.dot_general(left, right, (((0,), (0,)), ((), ())), preferred_element_type=f32)


class Place:
    def __init__(self):
        self.rep = lax.axis_size(AXES[0]) * lax.axis_size(AXES[1])
        self.planes = lax.axis_size(AXES[2])
        self.size = 2 * self.planes
        self.blocks = self.planes // self.rep
        self.shards = self.size // TENSOR
        self.o, self.c, self.z, self.y = [lax.axis_index(axis) for axis in AXES]
        self.g, self.b = self.z // self.blocks, self.z % self.blocks
        self.p = 2 * self.o + self.y

    def send(self, values, move):
        pairs = []
        for index in range(self.rep * self.size):
            rest, y = divmod(index, 2)
            rest, z = divmod(rest, self.planes)
            to = move(*divmod(rest, 2), *divmod(z, self.blocks), y)
            if to is not None:
                o, c, g, b, y = to
                target = ((2 * o + c) * self.planes + g * self.blocks + b) * 2 + y
                pairs.append((index, target))
        return lax.ppermute(values, AXES, pairs)

    def swap(self, values):
        return self.send(values, lambda o, c, g, b, y: (g // 2, g % 2, 2 * o + c, b, y))

    def part(self, values, k):
        return self.send(values, lambda o, c, g, b, y: (o ^ (k // 2), c, g, b, y ^ (k % 2)))

    def other_group(self, values, k):
        return self.send(values, lambda o, c, g, b, y: (o, c, g ^ k, b, y))

    def other_block(self, values, k):
        return self.send(values, lambda o, c, g, b, y: (o, c, g, b ^ k, y))

    def other_core(self, values):
        return self.send(values, lambda o, c, g, b, y: (o, 1 - c, g, b, y))

    def other_outer(self, values):
        return self.send(values, lambda o, c, g, b, y: (1 - o, c, g, b, y))

    def first_index(self, core, block, part):
        plane = (2 * (part // 2) + core) * self.blocks + block
        return 2 * plane + part % 2

    def gather(self, rows):
        cut = rows.shape[1] // 2
        one = self.part(rows, 1)
        two = self.part(rows, 2)
        return (rows, one, two, self.part(one[:, :cut], 2), self.part(two[:, cut:], 1))

    def scatter(self, parts):
        left_near, left_far, right_near, right_far = parts
        count = left_near.shape[0] // 2
        from_one = self.part(left_far, 1)
        from_two = self.part(right_far, 2)
        left = (left_near[count:].astype(f32) + from_one[count:].astype(f32)).astype(bf16)
        right = (right_near[count:].astype(f32) + from_two[count:].astype(f32)).astype(bf16)
        return (
            left_near, from_one, self.part(left, 2), right_near, from_two, self.part(right, 1)
        )

    def arrivals(self, stats):
        return [stats] + [self.part(stats, k) for k in range(1, TENSOR)]

    def spread(self, rows):
        own = [rows] + [self.other_block(rows, k) for k in range(1, self.blocks)]
        return own + [self.other_core(piece) for piece in own]

    def collect(self, pieces):
        total = [(piece,) for piece in pieces[: self.blocks]]
        total = [
            own + (self.other_core(piece.astype(bf16)),)
            for own, piece in zip(total, pieces[self.blocks :])
        ]
        if self.blocks == 1:
            return total[0]
        total = [sum(term.astype(f32) for term in terms) for terms in total]
        result = total[0]
        for k in range(1, self.blocks):
            result = result + self.other_block(total[k].astype(bf16), k).astype(f32)
        return (result,)

    def gather_planes(self, rows):
        return lax.all_gather(rows, (AXES[2], AXES[1]), axis=0, tiled=True)

    def fetch_columns(self, mine, there):
        arrived = self.send(
            there, lambda o, c, g, b, y: (o, c, g, b, 1 - y) if y == c else None
        )
        return jnp.where(self.y == self.c, mine, arrived)

    def fetch_heads(self, whole, first, matrices):
        count, wide = whole.shape[0] // TENSOR, whole.shape[1] - first
        pieces = []
        for k in range(TENSOR):
            piece = lax.dynamic_slice(whole, ((self.p ^ k) * count, first), (count, wide))
            pieces.append(self.part(piece, k) if k else piece)
        planes = self.planes // TENSOR
        rows = count // (planes * 2 * TENSOR)
        if rows % (2 * SUBLANES) == 0:
            return assemble(self.p, pieces, planes, matrices)
        result = jnp.zeros((planes, 2, 2, 2, rows, matrices, TENSOR, wide // matrices), bf16)
        for k, piece in enumerate(pieces):
            piece = piece.reshape(planes, 2, TENSOR, rows, matrices, wide // matrices)
            piece = piece.transpose(0, 1, 3, 4, 2, 5)[:, None, None]
            at = (0, self.y ^ (k % 2), self.o ^ (k // 2)) + (0,) * 5
            result = lax.dynamic_update_slice(result, piece, at)
        return result.reshape(count, TENSOR * wide)

    def in_order(self, pieces):
        whole = jnp.stack(pieces)
        if len(pieces) > 1:
            for k, piece in enumerate(pieces):
                whole = lax.dynamic_update_index_in_dim(whole, piece, self.b ^ k, 0)
        return whole

    def all_blocks(self, piece):
        return self.in_order([piece] + [self.other_block(piece, k) for k in range(1, self.blocks)])


def heads_share(matrices, share, shares):
    number, rows, width = matrices.shape
    piece = lax.dynamic_slice_in_dim(matrices, share * (rows // shares), rows // shares, 1)
    piece = piece.reshape(number, rows // shares, TENSOR, width // TENSOR).transpose(2, 1, 0, 3)
    return piece.reshape(TENSOR * (rows // shares), number * (width // TENSOR))


def assemble_kernel(planes, matrices, part, *refs):
    pieces, out = refs[:TENSOR], refs[TENSOR]
    count, wide = pieces[0].shape
    rows, one = count // (planes * 2 * TENSOR), wide // matrices
    for k, piece in enumerate(pieces):
        owner = part[0] ^ k
        place = (owner % 2) * 2 + owner // 2
        for plane in range(planes):
            for core in range(2):
                start = (plane * TENSOR + place) * 2 + core
                at = pl.ds(pl.multiple_of(start * rows, rows), rows)
                for group in range(TENSOR):
                    source = ((plane * 2 + core) * TENSOR + group) * rows
                    for m in range(matrices):
                        to = (m * TENSOR + group) * one
                        out[at, to : to + one] = piece[
                            source : source + rows, m * one : (m + 1) * one
                        ]


def assemble(part, pieces, planes, matrices):
    count, wide = pieces[0].shape
    return pl.pallas_call(
        functools.partial(assemble_kernel, planes, matrices),
        out_shape=jax.ShapeDtypeStruct((count, TENSOR * wide), bf16),
        in_specs=[pl.BlockSpec(memory_space=m) for m in [pltpu.SMEM] + [pltpu.VMEM] * TENSOR],
        out_specs=pl.BlockSpec(memory_space=pltpu.VMEM),
        compiler_params=pltpu.CompilerParams(vmem_limit_bytes=VMEM_BYTES),
        cost_estimate=pl.CostEstimate(
            flops=0, bytes_accessed=16 * count * wide, transcendentals=0
        ),
    )(part.astype(jnp.int32)[None], *pieces)


def rotary_tables(positions):
    pair_count = HD // 2
    third_part = pair_count // 3
    first_part = pair_count - 2 * third_part
    pieces = []
    for column, amount in ((0, first_part), (1, third_part), (2, third_part)):
        frequency = jnp.power(10000.0, -jnp.arange(amount, dtype=f32) / amount)
        pieces.append(positions[column].astype(f32)[:, None] * frequency[None, :])
    angles = jnp.repeat(jnp.concatenate(pieces, 1), 2, 1)
    sign = jnp.where(jnp.arange(HD) % 2 == 0, -1.0, 1.0)
    return jnp.cos(angles), jnp.sin(angles) * sign


def call(kernel, outs, args, scratch=(), flops=0, anywhere=()):
    outs = [jax.ShapeDtypeStruct(shape, dtype) for shape, dtype in outs]
    moved = sum(v.size * v.dtype.itemsize for v in list(args) + outs)
    space = [pl.ANY if k in anywhere else pltpu.VMEM for k in range(len(args))]
    return pl.pallas_call(
        kernel,
        out_shape=outs,
        in_specs=[pl.BlockSpec(memory_space=m) for m in space],
        out_specs=[pl.BlockSpec(memory_space=pltpu.VMEM) for _ in outs],
        scratch_shapes=list(scratch),
        compiler_params=pltpu.CompilerParams(vmem_limit_bytes=VMEM_BYTES),
        cost_estimate=pl.CostEstimate(flops=flops, bytes_accessed=moved, transcendentals=0),
    )(*args)


def part_shapes(rows, width):
    return [((rows // 2, width // 2), bf16)] * 4


def put_parts(parts, raw, inner, factors):
    count, half = raw.shape[0] // TENSOR, raw.shape[1] // 2
    for at in chunks(raw.shape[1]):
        values = (raw[:, at] + dot(inner, factors[:, at])).astype(bf16)
        right = at.start // half
        to = slice(at.start - right * half, at.stop - right * half)
        order = ((0, 1), (2, 3)) if right else ((0, 2), (1, 3))
        for ref, slots in zip(parts[2:] if right else parts[:2], order):
            for row, slot in enumerate(slots):
                ref[row * count : (row + 1) * count, to] = values[
                    slot * count : (slot + 1) * count
                ]


def join(pieces, full):
    own, one, two, left, right = pieces
    count, width = own.shape
    full[:count] = own[...]
    full[count : 2 * count] = one[...]
    full[2 * count : 3 * count] = two[...]
    full[3 * count :, : width // 2] = left[...]
    full[3 * count :, width // 2 :] = right[...]


def chunks(width):
    return [slice(start, start + CHUNK) for start in range(0, width, CHUNK)]


def turned(values):
    return values.astype(f32).T.astype(bf16)


def narrow(values, mask):
    return (values * mask).astype(bf16)


def row_sums(values):
    ones = jnp.ones((SUBLANES, values.shape[1]), bf16)
    high = values.astype(bf16)
    return dot_nt(ones, high) + dot_nt(ones, (values - high.astype(f32)).astype(bf16))


def as_columns(row, width):
    column = jnp.broadcast_to(row, (HD, row.shape[1])).T
    return jnp.concatenate([column] * (width // HD), 1)


def total_stats(refs):
    total = refs[0][...]
    count = total.shape[1] // TENSOR
    for k, ref in enumerate(refs):
        if k:
            order = [ref[:, (j ^ k) * count : ((j ^ k) + 1) * count] for j in range(TENSOR)]
            total = total + jnp.concatenate(order, 1)
    return total


def stat_rows(total, index):
    return total[index * SUBLANES : index * SUBLANES + 1]


def swap_pairs(values):
    lane = lax.broadcasted_iota(jnp.int32, values.shape, 1)
    return jnp.where(lane % 2 == 0, pltpu.roll(values, HD - 1, 1), pltpu.roll(values, 1, 1))


def rotate(values, cosine, sine):
    heads = [values[:, k : k + HD] for k in range(0, values.shape[1], HD)]
    return jnp.concatenate([v * cosine + swap_pairs(v) * sine for v in heads], 1)


def rotate_back(grad, cosine, sine):
    heads = [grad[:, k : k + HD] for k in range(0, grad.shape[1], HD)]
    return jnp.concatenate([v * cosine + swap_pairs(v * sine) for v in heads], 1)


def gelu_terms(x):
    slope = math.sqrt(2.0 / math.pi)
    square = x * x
    t = jnp.tanh(slope * x * (1.0 + 0.044715 * square))
    value = 0.5 * x * (1.0 + t)
    inner = slope * (1.0 + 3.0 * 0.044715 * square)
    return value, 0.5 * (1.0 + t) + 0.5 * x * (1.0 - t * t) * inner


def sum_terms(terms, count):
    sides = []
    for near, first, far in (terms[:3], terms[3:]):
        total = near[:count].astype(f32) + first[:count].astype(f32) + far[...].astype(f32)
        sides.append(total)
    return jnp.concatenate(sides, 1)


def advance_kernel(*refs):
    terms, (state, factor, scale, shift, new, normed) = refs[:6], refs[6:]
    value = state[...] + factor[...] * sum_terms(terms, state.shape[0])
    new[...] = value
    centred = value - jnp.mean(value, -1, keepdims=True)
    hat = centred * lax.rsqrt(jnp.mean(centred * centred, -1, keepdims=True) + epsilon)
    normed[...] = (hat * scale[...] + shift[...]).astype(bf16)


def advance(terms, state, factor, scale, shift):
    return call(
        advance_kernel, [(state.shape, f32), (state.shape, bf16)],
        (*terms, state, factor, scale, shift), flops=30 * state.size,
    )


def retreat_kernel(*refs):
    terms, (state, grad, scale, factor, new, out) = refs[:6], refs[6:]
    value = state[...]
    centred = value - jnp.mean(value, -1, keepdims=True)
    spread = lax.rsqrt(jnp.mean(centred * centred, -1, keepdims=True) + epsilon)
    hat = centred * spread
    inner = sum_terms(terms, value.shape[0]) * scale[...]
    along = jnp.mean(inner * hat, -1, keepdims=True)
    result = grad[...] + spread * (inner - jnp.mean(inner, -1, keepdims=True) - hat * along)
    new[...] = result
    out[...] = (result * factor[...]).astype(bf16)


def retreat(terms, state, grad, scale, factor):
    return call(
        retreat_kernel, [(state.shape, f32), (state.shape, bf16)],
        (*terms, state, grad, scale, factor), flops=40 * state.size,
    )


def pack_kernel(layer, squares, planes, *refs):
    part, square, wide = refs[:3]
    mine, there, held, sems = refs[3:]
    own = square.shape[3] // TENSOR
    copies = []
    if planes:
        whole = pltpu.make_async_copy(wide.at[layer], held, sems.at[2 * len(squares)])
        whole.start()
    for k, column in enumerate(squares):
        for side, out in enumerate((mine, there)):
            at = pl.ds(pl.multiple_of((part[0] ^ side) * own, own), own)
            copies.append(
                pltpu.make_async_copy(
                    square.at[layer, squares[column], :, at],
                    out.at[:, pl.ds(column, own)],
                    sems.at[2 * k + side],
                )
            )
            copies[-1].start()
    if planes:
        base, stop, count = planes
        one = held.shape[1] // (8 * count)
        step = (stop - base) // (2 * count)
        whole.wait()
        for out in (mine, there) if step > one else ():
            out[:, base:stop] = jnp.zeros((held.shape[0], stop - base), bf16)
        for k in range(TENSOR):

            @pl.when(part[0] == k)
            def _(k=k):
                for side, out in enumerate((mine, there)):
                    o, y = divmod(k ^ side, 2)
                    for z in range(2 * count):
                        at = (((z // 2) * 2 + y) * 4 + o * 2 + z % 2) * one
                        to = base + z * step
                        out[:, to : to + one] = held[:, at : at + one]

    for copy in copies:
        copy.wait()


def pack(part, square, wide, layer, width, squares, planes=None):
    rows = square.shape[2]
    scratch = [
        pltpu.VMEM(wide.shape[1:] if planes else (SUBLANES, HD), bf16),
        pltpu.SemaphoreType.DMA((2 * len(squares) + 1,)),
    ]
    return pl.pallas_call(
        functools.partial(pack_kernel, layer, squares, planes),
        out_shape=[jax.ShapeDtypeStruct((rows, width), bf16)] * 2,
        in_specs=[pl.BlockSpec(memory_space=m) for m in (pltpu.SMEM, pl.ANY, pl.ANY)],
        out_specs=[pl.BlockSpec(memory_space=pltpu.VMEM)] * 2,
        scratch_shapes=scratch,
        compiler_params=pltpu.CompilerParams(vmem_limit_bytes=VMEM_BYTES),
        cost_estimate=pl.CostEstimate(flops=0, bytes_accessed=8 * rows * width, transcendentals=0),
    )(part, square, wide)


def pick_kernel(seqs, near_list, heads_list, *refs):
    adapters, groups, firsts, seconds, wide_firsts, wide_seconds = refs[:6]
    near, heads, cat = refs[6:]
    rank = seqs * ADAPTER_RANK
    per = HD // rank
    layers, _, rows, _ = firsts.shape
    row = lax.broadcasted_iota(jnp.int32, (per * HD, HD), 0)
    column = lax.broadcasted_iota(jnp.int32, (per * HD, HD), 1)

    def one_hot(group):
        wanted = jnp.zeros_like(column)
        for s in range(seqs):
            here = (column // ADAPTER_RANK) % seqs == s
            wanted = jnp.where(here, adapters[group * seqs + s] * ADAPTER_RANK, wanted)
        wanted = wanted + column % ADAPTER_RANK + (column // rank) * HD
        return (row == wanted).astype(f32).astype(bf16)

    hots = [one_hot(groups[k]) for k in range(TENSOR + 2)]

    def blocks(items, count):
        for block in range(-(-len(items) // per)):
            here = items[block * per : (block + 1) * per]
            for k in range(per):
                at = slice(k * HD, (k + 1) * HD)
                if k < len(here):
                    ref, index = here[k]
                    cat[:count, at] = ref[index]
                else:
                    cat[:count, at] = jnp.zeros((count, HD), bf16)
            yield block, cat[:count]

    refs_of = (firsts, seconds)
    items = [(refs_of[w], (layer, i)) for layer in range(layers) for w, i in near_list]
    for block, values in blocks(items, rows):
        for k in range(TENSOR):
            near[k, block * rows : (block + 1) * rows] = dot(values, hots[k]).astype(bf16)
    base = -(-len(items) // per) * rows
    items = [(refs_of[w], (layer, i)) for layer in range(layers) for w, i in heads_list]
    for block, values in blocks(items, rows):
        for k in range(2):
            heads[k, block * rows : (block + 1) * rows] = dot(values, hots[TENSOR + k]).astype(bf16)
    units = wide_firsts.shape[1]
    items = [(ref, (layer,)) for layer in range(layers) for ref in (wide_firsts, wide_seconds)]
    for block, values in blocks(items, units):
        at = base + block * units
        for k in range(TENSOR):
            near[k, at : at + units] = dot(values, hots[k]).astype(bf16)


def pick(adapters, groups, firsts, seconds, wide_firsts, wide_seconds, seqs):
    layers, _, rows, _ = firsts.shape
    units = wide_firsts.shape[1]
    per = HD // (seqs * ADAPTER_RANK)
    near_rows = -(-layers * len(NEAR) // per) * rows + -(-layers * 2 // per) * units
    heads_rows = -(-layers * len(HEADS) // per) * rows
    space = [pltpu.SMEM] * 2 + [pltpu.VMEM] * 4
    return pl.pallas_call(
        functools.partial(pick_kernel, seqs, NEAR, HEADS),
        out_shape=[
            jax.ShapeDtypeStruct((TENSOR, near_rows, HD), bf16),
            jax.ShapeDtypeStruct((2, heads_rows, HD), bf16),
        ],
        in_specs=[pl.BlockSpec(memory_space=m) for m in space],
        out_specs=[pl.BlockSpec(memory_space=pltpu.VMEM)] * 2,
        scratch_shapes=[pltpu.VMEM((max(rows, units), per * HD), bf16)],
        compiler_params=pltpu.CompilerParams(vmem_limit_bytes=VMEM_BYTES),
        cost_estimate=pl.CostEstimate(flops=0, bytes_accessed=8 * near_rows * HD, transcendentals=0),
    )(adapters, groups, firsts, seconds, wide_firsts, wide_seconds)


def picked(ref, place, rank, count=1):
    return ref[place * rank : (place + count) * rank]


def ffn_kernel(places, *refs):
    pieces, (mask, near, far, w_in, w_out), refs = refs[:5], refs[5:10], refs[10:]
    parts, (up_raw, up_inner, down_inner), (full, raw, hidden) = refs[:4], refs[4:7], refs[7:]
    rank = mask.shape[1]
    width = full.shape[1]
    up_a, down_b, down_a, up_b = places
    join(pieces, full)
    raw[:, : w_in.shape[1]] = dot(full[...], w_in[...])
    inner = narrow(dot_nt(full[...], picked(near, up_a, rank)), mask[...])
    up_inner[...] = inner
    factors = picked(far, up_b, rank)
    for at in chunks(w_in.shape[1]):
        values = raw[:, at] + dot(inner, factors[:, at])
        up_raw[:, at] = values.astype(bf16)
        hidden[:, at] = gelu_terms(values)[0].astype(bf16)
    raw[:, :width] = dot(hidden[...], w_out[...])
    inner = narrow(dot_nt(hidden[...], picked(far, down_a, rank)), mask[...])
    down_inner[...] = inner
    put_parts(parts, raw.at[:, :width], inner, picked(near, down_b, rank))


def ffn(pieces, mask, near, far, w_in, w_out, places):
    count, width = pieces[0].shape
    rows, rank = mask.shape
    wide = w_in.shape[1]
    outs = part_shapes(rows, width) + [((rows, wide), bf16), ((rows, rank), bf16)]
    scratch = [
        pltpu.VMEM((rows, width), bf16),
        pltpu.VMEM((rows, max(wide, width)), f32),
        pltpu.VMEM((rows, wide), bf16),
    ]
    outs = call(
        functools.partial(ffn_kernel, places), outs + [((rows, rank), bf16)],
        (*pieces, mask, near, far, w_in, w_out), scratch, 4 * rows * width * wide,
    )
    return outs[:4], tuple(outs[4:])


def ffn_back_kernel(places, *refs):
    grads, inputs, refs = refs[:5], refs[5:10], refs[10:]
    up_raw, up_inner, down_inner, mask, near, far, w_in, w_out = refs[:8]
    parts, (a_down, b_up, a_up, b_down) = refs[8:12], refs[12:16]
    grad, full, raw, grad_up = refs[16:]
    rank = mask.shape[1]
    width = full.shape[1]
    at_up_a, at_down_b, at_down_a, at_up_b = places
    join(grads, grad)
    join(inputs, full)
    raw[:, : w_out.shape[0]] = dot_nt(grad[...], w_out[...])
    down_back = narrow(dot_nt(grad[...], picked(near, at_down_b, rank)), mask[...])
    down_turned = turned(down_back)
    up_turned = turned(up_inner[...])
    factors = picked(far, at_down_a, rank)
    for at in chunks(up_raw.shape[1]):
        hidden_grad = raw[:, at] + dot(down_back, factors[:, at])
        value, slope = gelu_terms(up_raw[:, at].astype(f32))
        raw_grad = (hidden_grad * slope).astype(bf16)
        grad_up[:, at] = raw_grad
        a_down[:, at] = dot(down_turned, value.astype(bf16)).astype(bf16)
        b_up[:, at] = dot(up_turned, raw_grad).astype(bf16)
    up_back = narrow(dot_nt(grad_up[...], picked(far, at_up_b, rank)), mask[...])
    raw[:, :width] = dot_nt(grad_up[...], w_in[...])
    put_parts(parts, raw.at[:, :width], up_back, picked(near, at_up_a, rank))
    a_up[...] = dot(turned(up_back), full[...]).astype(bf16)
    b_down[...] = dot(turned(down_inner[...]), grad[...]).astype(bf16)


def ffn_back(grads, inputs, saved, mask, near, far, w_in, w_out, places):
    count, width = grads[0].shape
    rows, rank = mask.shape
    wide = w_in.shape[1]
    outs = part_shapes(rows, width) + [((rank, n), bf16) for n in (wide, wide, width, width)]
    scratch = [
        pltpu.VMEM((rows, width), bf16),
        pltpu.VMEM((rows, width), bf16),
        pltpu.VMEM((rows, max(wide, width)), f32),
        pltpu.VMEM((rows, wide), bf16),
    ]
    outs = call(
        functools.partial(ffn_back_kernel, places), outs,
        (*grads, *inputs, *saved, mask, near, far, w_in, w_out), scratch,
        4 * rows * width * wide,
    )
    return outs[:4], outs[4:]


def project_kernel(start, count, normed, *refs):
    pieces, (mask, weights, near, heads), refs = refs[:5], refs[5:9], refs[9:]
    raws, (inner, stats, full, together) = refs[:count], refs[count:]
    own = raws[0].shape[1]
    rank = mask.shape[1]
    base, near_at, heads_at = start
    join(pieces, full)
    together[...] = dot(full[...], weights[:, base : base + count * own])
    inner[...] = narrow(
        dot_nt(full[...], picked(near, near_at, rank, count)),
        jnp.concatenate([mask[...]] * count, 1),
    )
    for k, raw in enumerate(raws):
        values = together[:, k * own : (k + 1) * own] + dot(
            inner[:, k * rank : (k + 1) * rank], picked(heads, heads_at + k, rank)
        )
        raw[...] = values.astype(raw.dtype)
        if k < normed:
            stats[k * SUBLANES : (k + 1) * SUBLANES] = row_sums(values * values)


def project(pieces, mask, weights, near, heads, start, count, normed):
    rows, rank = mask.shape
    own = heads.shape[1]
    outs = [((rows, own), f32 if k < normed else bf16) for k in range(count)]
    outs += [((rows, count * rank), bf16), ((normed * SUBLANES, rows), f32)]
    outs = call(
        functools.partial(project_kernel, start, count, normed), outs,
        (*pieces, mask, weights, near, heads),
        [pltpu.VMEM((rows, pieces[0].shape[1]), bf16), pltpu.VMEM((rows, count * own), f32)],
        2 * rows * weights.shape[0] * own * count,
    )
    return outs[:count], outs[count], outs[count + 1]


def scales_of(total, index, width, own):
    return as_columns(lax.rsqrt(stat_rows(total, index) / width + epsilon), own)


def normalize_kernel(count, turning, valued, width, *refs):
    raws, gains, refs = refs[:count], refs[count : 2 * count], refs[2 * count :]
    tables, refs = refs[: 2 * turning], refs[2 * turning :]
    value, refs = refs[:valued], refs[valued:]
    stats, outs, total = refs[: -count - 1], refs[-count - 1 : -1], refs[-1]
    total[...] = total_stats(stats)
    own = raws[0].shape[1]
    for k in range(count):
        values = raws[k][...] * scales_of(total, k, width, own) * gains[k][...]
        if turning:
            values = rotate(values, tables[0][...], tables[1][...])
        outs[k][:, :own] = values.astype(bf16)
    if valued:
        outs[-1][:, own:] = value[0][...]


def normalize(raws, gains, stats, width, tables=(), value=()):
    shape = raws[0].shape
    outs = [(shape, bf16) for _ in raws]
    if value:
        outs[-1] = ((shape[0], 2 * shape[1]), bf16)
    outs.append((stats[0].shape, f32))
    outs = call(
        functools.partial(normalize_kernel, len(raws), len(tables) // 2, len(value), width), outs,
        (*raws, *gains, *tables, *value, *stats), flops=20 * len(raws) * raws[0].size,
    )
    return outs[:-1], outs[-1]


def attend_kernel(count, start, *refs):
    query, marks, refs = refs[0], refs[1], refs[2:]
    pairs, key_marks, refs = refs[:count], refs[count : 2 * count], refs[2 * count :]
    mask, weights, near, heads = refs[:4]
    parts, result, inner, raw = refs[4:8], refs[8], refs[9], refs[10]
    rows, own = query.shape
    width, rank = near.shape[1], mask.shape[1]
    base, near_at, heads_at = start
    scale = 1.0 / math.sqrt(HD)
    block = min(BLOCK, rows)

    @pl.loop(0, rows // block)
    def _(index):
        at = pl.ds(pl.multiple_of(index * block, block), block)
        allowed = [marks[at] == key_mark[...] for key_mark in key_marks]
        for head in range(0, own, HD):
            scores = [
                jnp.where(
                    ok, dot_nt(query[at, head : head + HD], pair[:, head : head + HD]) * scale,
                    masked_score,
                )
                for ok, pair in zip(allowed, pairs)
            ]
            peak = functools.reduce(
                jnp.maximum, [jnp.max(s, -1, keepdims=True) for s in scores]
            )
            weighed = [jnp.exp(s - peak) for s in scores]
            total = sum(jnp.sum(w, -1, keepdims=True) for w in weighed)
            summed = sum(
                dot(w.astype(bf16), pair[:, own + head : own + head + HD])
                for w, pair in zip(weighed, pairs)
            )
            result[at, head : head + HD] = (summed / total).astype(bf16)

    raw[...] = dot(result[...], weights[:, base : base + width])
    inner[...] = narrow(dot_nt(result[...], picked(heads, heads_at, rank)), mask[...])
    put_parts(parts, raw, inner[...], picked(near, near_at, rank))


def attend(query, marks, pairs, key_marks, mask, weights, near, heads, start):
    rows, own = query.shape
    width, rank = near.shape[1], mask.shape[1]
    outs = part_shapes(rows, width) + [((rows, own), bf16), ((rows, rank), bf16)]
    keys = sum(pair.shape[0] for pair in pairs)
    outs = call(
        functools.partial(attend_kernel, len(pairs), start), outs,
        (query, marks, *pairs, *key_marks, mask, weights, near, heads),
        [pltpu.VMEM((rows, width), f32)], 4 * rows * keys * own + 2 * rows * own * width,
    )
    return outs[:4], outs[4], outs[5]


def attend_back_kernel(count, start, *refs):
    grads, (query, marks), refs = refs[:5], refs[5:7], refs[7:]
    pairs, key_marks, refs = refs[:count], refs[count : 2 * count], refs[2 * count :]
    (result, inner, mask, weights, near, heads), refs = refs[:6], refs[6:]
    base, near_at, heads_at = start
    grad_query, pair_grads, refs = refs[0], refs[1 : 1 + count], refs[1 + count :]
    a_grad, b_grad, grad, grad_out, raw = refs
    rows, own = query.shape
    rank = mask.shape[1]
    scale = 1.0 / math.sqrt(HD)
    block = min(BLOCK, rows)
    join(grads, grad)
    back = narrow(dot_nt(grad[...], picked(near, near_at, rank)), mask[...])
    raw[...] = dot_nt(grad[...], weights[:, base : base + grad.shape[1]])
    grad_out[...] = (raw[...] + dot(back, picked(heads, heads_at, rank))).astype(bf16)
    a_grad[...] = dot(turned(back), result[...]).astype(bf16)
    b_grad[...] = dot(turned(inner[...]), grad[...]).astype(bf16)
    for head in range(0, own, HD):
        here, there = slice(head, head + HD), slice(own + head, own + head + HD)
        keys_turned = [turned(pair[:, here]) for pair in pairs]
        for start in range(0, rows, block):
            at = slice(start, start + block)
            q, g = query[at, here], grad_out[at, here]
            scores = [
                jnp.where(
                    key_mark[...] == marks[:, at], dot_nt(pair[:, here], q) * scale, masked_score
                )
                for key_mark, pair in zip(key_marks, pairs)
            ]
            peak = functools.reduce(jnp.maximum, [jnp.max(s, 0, keepdims=True) for s in scores])
            weighed = [jnp.exp(s - peak) for s in scores]
            inverse = 1.0 / sum(jnp.sum(w, 0, keepdims=True) for w in weighed)
            probs = [w * inverse for w in weighed]
            along = [dot_nt(pair[:, there], g) for pair in pairs]
            delta = sum(jnp.sum(p * d, 0, keepdims=True) for p, d in zip(probs, along))
            turned_grad = 0.0
            for k in range(count):
                score_grad = (probs[k] * (along[k] - delta)).astype(bf16)
                key_grad = dot(score_grad, q) * scale
                value_grad = dot(probs[k].astype(bf16), g)
                if start:
                    key_grad = key_grad + pair_grads[k][:, here]
                    value_grad = value_grad + pair_grads[k][:, there]
                pair_grads[k][:, here] = key_grad
                pair_grads[k][:, there] = value_grad
                turned_grad = turned_grad + dot(keys_turned[k], score_grad)
            grad_query[at, here] = (turned_grad * scale).T


def attend_back(
    grads, query, marks, pairs, key_marks, result, inner, mask, weights, near, heads, start
):
    rows, own = query.shape
    width, rank = near.shape[1], mask.shape[1]
    outs = [((rows, own), f32)] + [(pair.shape, f32) for pair in pairs]
    outs += [((rank, own), bf16), ((rank, width), bf16)]
    keys = sum(pair.shape[0] for pair in pairs)
    outs = call(
        functools.partial(attend_back_kernel, len(pairs), start), outs,
        (*grads, query, marks, *pairs, *key_marks, result, inner, mask, weights, near, heads),
        [
            pltpu.VMEM((rows, width), bf16), pltpu.VMEM((rows, own), bf16),
            pltpu.VMEM((rows, own), f32),
        ],
        10 * rows * keys * own + 2 * rows * own * width,
    )
    return outs[0], outs[1:-2], outs[-2], outs[-1]


def back_stats_kernel(counts, turning, valued, width, *refs):
    number = len(counts)
    terms = []
    for count in counts:
        terms.append(refs[:count])
        refs = refs[count:]
    raws, gains, refs = refs[:number], refs[number : 2 * number], refs[2 * number :]
    tables, refs = refs[: 2 * turning], refs[2 * turning :]
    total, outs, stats = refs[0], refs[1:-1], refs[-1]
    own = raws[0].shape[1]
    for k in range(number):
        grad = sum(term[:, :own].astype(f32) for term in terms[k])
        if turning:
            grad = rotate_back(grad, tables[0][...], tables[1][...])
        grad = grad * gains[k][...]
        outs[k][...] = grad
        hat = raws[k][...] * scales_of(total, k, width, own)
        stats[k * SUBLANES : (k + 1) * SUBLANES] = row_sums(hat * grad)
    if valued:
        outs[-1][...] = sum(term[:, own:].astype(f32) for term in terms[-1]).astype(bf16)


def back_stats(terms, raws, gains, total, width, tables=(), valued=False):
    shape = raws[0].shape
    outs = [(shape, f32) for _ in raws] + [(shape, bf16)] * valued + [(total.shape, f32)]
    outs = call(
        functools.partial(
            back_stats_kernel, tuple(len(t) for t in terms), len(tables) // 2, int(valued), width
        ),
        outs, (*[term for t in terms for term in t], *raws, *gains, *tables, total),
        flops=30 * len(raws) * raws[0].size,
    )
    return outs[:-1], outs[-1]


def project_back_kernel(start, count, normed, parted, *refs):
    scaled, raws, refs = refs[:count], refs[count : count + normed], refs[count + normed :]
    total, (inner, mask, weights, near, heads), refs = refs[0], refs[1:6], refs[6:]
    inputs, refs = refs[:5], refs[5:]
    split = 4 if parted else 1
    stats, refs = refs[: -6 - split], refs[-6 - split :]
    outs, (a_grad, b_grad, full, grads, back, raw) = refs[:split], refs[split:]
    own = scaled[0].shape[1]
    width = full.shape[1]
    rank = mask.shape[1]
    base, near_at, heads_at = start
    join(inputs, full)
    along = total_stats(stats)
    for k in range(count):
        if k < normed:
            scale = scales_of(total, k, width, own)
            hat = raws[k][...] * scale
            mean = as_columns(stat_rows(along, k) / width, own)
            grads[:, k * own : (k + 1) * own] = (scale * (scaled[k][...] - hat * mean)).astype(bf16)
        else:
            grads[:, k * own : (k + 1) * own] = scaled[k][...]
    inner_turned = turned(inner[...])
    for k in range(count):
        at = slice(k * rank, (k + 1) * rank)
        grad = grads[:, k * own : (k + 1) * own]
        back[:, at] = narrow(dot_nt(grad, picked(heads, heads_at + k, rank)), mask[...])
        b_grad[at] = dot(inner_turned[at], grad).astype(bf16)
    a_grad[...] = dot(turned(back[...]), full[...]).astype(bf16)
    raw[...] = dot_nt(grads[...], weights[:, base : base + count * own])
    factors = picked(near, near_at, rank, count)
    if parted:
        put_parts(outs, raw, back[...], factors)
    else:
        for at in chunks(width):
            outs[0][:, at] = raw[:, at] + dot(back[...], factors[:, at])


def project_back(
    scaled, raws, total, stats, inner, mask, weights, near, heads, inputs, start, parted=True
):
    count, normed = len(scaled), len(raws)
    rows, own = scaled[0].shape
    width, rank = weights.shape[0], mask.shape[1]
    outs = part_shapes(rows, width) if parted else [((rows, width), f32)]
    split = len(outs)
    outs = outs + [((count * rank, width), bf16), ((count * rank, own), bf16)]
    scratch = [
        pltpu.VMEM((rows, width), bf16),
        pltpu.VMEM((rows, count * own), bf16),
        pltpu.VMEM((rows, count * rank), bf16),
        pltpu.VMEM((rows, width), f32),
    ]
    outs = call(
        functools.partial(project_back_kernel, start, count, normed, parted), outs,
        (*scaled, *raws, total, inner, mask, weights, near, heads, *inputs, *stats), scratch,
        2 * rows * width * own * count,
    )
    return outs[:split], outs[split], outs[split + 1]


def on_device(
    tokens,
    context,
    cotangent,
    positions,
    sequence_lengths,
    sequence_adapter,
    text_token_count,
    timestep_modulation,
    modulation,
    gains,
    query_key_value_weight,
    output_weight,
    up_weight,
    down_weight,
    first_factors,
    down_first_factor,
    second_factors,
    up_second_factor,
):
    place = Place()
    rows, width = tokens.shape
    seq_count, text_local = context.shape[:2]
    layers = query_key_value_weight.shape[0]
    columns = first_factors.shape[3]
    rank = seq_count * ADAPTER_RANK
    own = width // TENSOR
    wide = up_weight.shape[2] // TENSOR
    padded = -(-wide // CHUNK) * CHUNK
    set_rows = TENSOR * rows

    numbers = jnp.concatenate([positions.reshape(-1), sequence_lengths, text_token_count])
    numbers = place.swap(numbers)
    state = place.swap(tokens).astype(f32)
    times = place.swap(timestep_modulation)
    positions = numbers[: 3 * rows].reshape(3, rows)
    lengths, counts = [
        numbers[3 * rows + k * seq_count : 3 * rows + (k + 1) * seq_count] for k in range(2)
    ]

    bounds = jnp.cumsum(lengths)

    def token_segments(index):
        packed = jnp.arange(rows, dtype=jnp.int32) * place.size + index
        return jnp.sum((packed[:, None] >= bounds[None, :]).astype(jnp.int32), 1)

    def text_marks(index):
        at = index * text_local + jnp.arange(text_local)
        marks = jnp.where(at[None, :] < counts[:, None], jnp.arange(seq_count)[:, None], -1)
        return marks.reshape(-1)

    def over_set(function, core, block):
        return jnp.concatenate(
            [function(place.first_index(core, block, place.p ^ k)) for k in range(TENSOR)]
        )

    def over_group(function):
        return [
            over_set(function, core, place.b ^ k)
            for core in (place.c, 1 - place.c)
            for k in range(place.blocks)
        ]

    segment = over_set(token_segments, place.c, place.b)
    sequence = jnp.minimum(segment, seq_count - 1)
    self_marks = over_group(token_segments)
    cross_marks = over_group(text_marks)
    column_sequence = jnp.arange(rank) // ADAPTER_RANK
    mask = (sequence[:, None] == column_sequence[None, :]) & (segment < seq_count)[:, None]
    mask = mask.astype(f32)
    text_sequence = jnp.tile(jnp.repeat(jnp.arange(seq_count), text_local), TENSOR)
    text_mask = (text_sequence[:, None] == column_sequence[None, :]).astype(f32)
    valid = (segment[:rows] < seq_count).astype(f32)[:, None]

    def mods_of(layer):
        table = modulation[layer][None] + times
        chosen = [table[0, k][None] for k in range(6)]
        for s in range(1, seq_count):
            here = (sequence[:rows] == s)[:, None]
            chosen = [jnp.where(here, table[s, k][None], chosen[k]) for k in range(6)]
        return chosen

    def own_gain(layer, index):
        return lax.dynamic_slice_in_dim(gains[layer, index], place.p * own, own, 0)[None]

    table = jnp.zeros((place.rep, seq_count), jnp.int32)
    for k in range(2):
        arrived = sequence_adapter if k == 0 else place.other_outer(sequence_adapter)
        for m, values in enumerate((arrived, place.other_core(arrived))):
            here = jnp.arange(place.rep) == 2 * (place.o ^ k) + (place.c ^ m)
            table = jnp.where(here[:, None], values[None], table)
    half_units = down_first_factor.shape[1] // 2
    wanted = [place.g ^ k for k in range(TENSOR)] + [place.p, place.p ^ 1]
    near_share, heads_pick = pick(
        table.reshape(-1),
        jnp.stack(wanted).astype(jnp.int32),
        first_factors,
        second_factors.transpose(0, 1, 3, 2),
        lax.dynamic_slice_in_dim(down_first_factor, place.o * half_units, half_units, 1),
        lax.dynamic_slice_in_dim(
            up_second_factor.transpose(0, 2, 1), place.o * half_units, half_units, 1
        ),
        seq_count,
    )
    shard_rows = first_factors.shape[2]
    wide_blocks = -(-layers * 2 * rank // HD)
    near_rows = near_share.shape[1] - wide_blocks * half_units
    from_groups = [near_share[0]]
    from_groups += [place.other_group(near_share[k], k) for k in range(1, TENSOR)]
    from_groups = [place.all_blocks(piece) for piece in from_groups]
    own_rows = jnp.stack([piece[:, :near_rows] for piece in from_groups])
    other_rows = place.part(own_rows, 1)
    near = jnp.zeros((place.rep, 2) + own_rows.shape[1:], bf16)
    far = jnp.zeros((place.rep, place.blocks, wide_blocks * half_units, HD), bf16)
    for k in range(TENSOR):
        for rows_of, y in ((own_rows, place.y), (other_rows, 1 - place.y)):
            near = lax.dynamic_update_slice(
                near, rows_of[k][None, None], (place.g ^ k, y, 0, 0, 0)
            )
        far = lax.dynamic_update_slice(
            far, from_groups[k][None, :, near_rows:], (place.g ^ k, 0, 0, 0)
        )
    near = near.reshape(place.rep, 2, place.blocks, -1, shard_rows, HD)
    near = near.transpose(0, 2, 1, 4, 3, 5).reshape(width, -1).T
    far = far.reshape(place.planes, wide_blocks, half_units, HD).transpose(0, 2, 1, 3)
    far = far.reshape(wide, wide_blocks * HD)
    far = far.reshape(place.size, -1, wide_blocks * HD)
    far = jnp.pad(far, ((0, 0), (0, (padded - wide) // place.size), (0, 0))).reshape(padded, -1).T
    arrived = place.part(heads_pick[1], 1)
    heads_pick = jnp.where(
        place.y == 0, jnp.stack([heads_pick[0], arrived]), jnp.stack([arrived, heads_pick[0]])
    )
    heads_pick = place.send(
        heads_pick, lambda o, c, g, b, y: (g // 2, c, 2 * o + y, b, g % 2)
    )
    heads_pick = place.all_blocks(heads_pick).reshape(place.blocks, 2, -1, shard_rows, HD)
    far_heads = heads_pick.transpose(0, 1, 3, 2, 4).reshape(own, -1).T

    up_at = 6 * own
    part = place.p.astype(jnp.int32)[None]
    share = 2 * place.o + place.c

    def tied(value, after):
        return value if after is None else lax.optimization_barrier((value, after))[0]

    def fetch_self(layer, after, ready=None):
        mine, there = pack(
            tied(part, after), query_key_value_weight, up_weight, layer, 3 * own,
            {k * own: k for k in range(3)},
        )
        rows = place.fetch_columns(mine, there)
        piece = heads_share(output_weight[layer], share, place.rep)
        whole = place.gather_planes(tied(jnp.concatenate([rows, piece], 1), ready))
        return whole, place.fetch_heads(whole, 3 * own, 2)

    def fetch_others(layer, after):
        mine, there = pack(
            tied(part, after), query_key_value_weight, up_weight, layer, 3 * own + padded,
            {k * own: 3 + k for k in range(3)}, (3 * own, 3 * own + padded, place.planes),
        )
        rows = place.fetch_columns(mine, there)
        cross = place.gather_planes(rows[:, : 3 * own])
        up = place.gather_planes(rows[:, 3 * own :])
        count = down_weight.shape[1] // place.rep
        piece = lax.dynamic_slice(
            down_weight, (layer, share * count, 0), (1, count, width)
        )[0]
        piece = jnp.pad(piece, ((0, padded // place.size - count), (0, 0)))
        return cross, up, place.gather_planes(tied(piece, rows))

    positions = jnp.stack([positions] + [place.part(positions, k) for k in range(1, TENSOR)], 1)
    tables = rotary_tables(positions.reshape(3, set_rows))

    def arrivals(stats):
        arrived = place.arrivals(stats)
        count = stats.shape[1] // TENSOR
        if count % HD == 0:
            return arrived
        pieces = [v.reshape(-1, TENSOR, count) for v in arrived]
        total = sum(
            jnp.stack([v[:, j ^ k] for j in range(TENSOR)], 1) for k, v in enumerate(pieces)
        )
        return [total.reshape(stats.shape)]

    columns_of = [v.reshape(-1, 1) for v in (segment, sequence)]
    rows_of = [v.reshape(1, -1) for v in (segment, sequence)]
    self_rows, cross_rows = [[v.reshape(1, -1) for v in m] for m in (self_marks, cross_marks)]
    self_columns, cross_columns = [
        [v.reshape(-1, 1) for v in m] for m in (self_marks, cross_marks)
    ]
    zero_row = jnp.zeros((1, width), f32)
    starts = []
    for layer in range(layers):
        one, two, three = layer * len(NEAR), layer * len(HEADS), 2 * layer
        starts.append(
            (
                (0, one, two + 2), (0, one + 7, two), (0, one + 3, two + 5), (own, one + 4, two + 6),
                (width, one + 8, two + 1), (one + 6, one + 9, three, three + 1),
            )
        )

    saved = []
    factors = []
    for layer in range(layers):
        shift_one, scale_one, gate_one, shift_two, scale_two, gate_two = mods_of(layer)
        factors.append((valid * gate_one, valid * gate_two, 1.0 + scale_one, 1.0 + scale_two))
        factors[-1] += (shift_one, shift_two)
    valid_rows = jnp.broadcast_to(valid, (rows, width))
    centred = state - jnp.mean(state, -1, keepdims=True)
    hat = centred * lax.rsqrt(jnp.mean(centred * centred, -1, keepdims=True) + epsilon)
    normed = (hat * factors[0][2] + factors[0][4]).astype(bf16)
    fetched = []
    coming = fetch_self(0, None, (state, numbers, times, from_groups))
    others = None
    for layer in range(layers):
        gate_one, gate_two, scale_one, scale_two, shift_one, shift_two = factors[layer]
        in_at, out_at, cross_at, text_at, crossed_at, ffn_at = starts[layer]
        self_in, heads = coming
        self_pieces = place.gather(normed)
        if layer == 0:
            others = fetch_others(layer, self_pieces[3])
            text = tied(context.reshape(seq_count * text_local, width), self_pieces[3])
            text = place.gather(place.swap(text))
        cross_in, ffn_in, ffn_out = others
        raws, self_inner, stats = project(self_pieces, mask, self_in, near, far_heads, in_at, 3, 2)
        gain = [own_gain(layer, k) for k in range(4)]
        (query, pair), self_total = normalize(
            raws[:2], gain[:2], arrivals(stats), width, tables, raws[2:]
        )
        pairs = place.spread(pair)
        if layer + 1 < layers:
            coming = fetch_self(layer + 1, query)
        parts, attended, out_inner = attend(
            query, columns_of[0], pairs, self_rows, mask, heads, near, far_heads, out_at
        )
        self_saved = (self_pieces, raws, self_inner, self_total, query, pairs, attended, out_inner)
        state_one, normed = advance(
            place.scatter(parts), state, gate_one, gains[layer, 4][None], zero_row
        )

        text_raws, text_inner, stats = project(
            text, text_mask, cross_in, near, far_heads, text_at, 2, 1
        )
        (pair,), text_total = normalize(
            text_raws[:1], gain[3:], arrivals(stats), width, (), text_raws[1:]
        )
        pairs = place.spread(pair)
        cross_pieces = place.gather(normed)
        if layer + 1 < layers:
            others = fetch_others(layer + 1, cross_pieces[3])
        else:
            cotangent = place.swap(tied(cotangent, cross_pieces[3]))
        raws, cross_inner, stats = project(
            cross_pieces, mask, cross_in, near, far_heads, cross_at, 1, 1
        )
        (query,), cross_total = normalize(raws, gain[2:3], arrivals(stats), width)
        parts, crossed, crossed_inner = attend(
            query, columns_of[1], pairs, cross_rows, mask, heads, near, far_heads, crossed_at
        )
        cross_saved = (
            cross_pieces, raws, cross_inner, cross_total, query, pairs, crossed, crossed_inner
        )
        state_two, normed = advance(
            place.scatter(parts), state_one, valid_rows, scale_two, shift_two
        )

        ffn_pieces = place.gather(normed)
        parts, ffn_saved = ffn(ffn_pieces, mask, near, far, ffn_in, ffn_out, ffn_at)
        fetched.append((self_in, heads, cross_in, ffn_in, ffn_out))
        saved.append(
            (
                (state, state_one, state_two), self_saved, cross_saved,
                (text_raws, text_inner, text_total), (ffn_pieces, ffn_saved), gain,
            )
        )
        following = factors[min(layer + 1, layers - 1)]
        state, normed = advance(
            place.scatter(parts), state_two, gate_two, following[2], following[4]
        )

    grad = cotangent.astype(f32)
    out = (grad * factors[-1][1]).astype(bf16)
    grad_text = 0.0
    whole_grads, part_grads, wide_grads = [], [], []
    for layer in reversed(range(layers)):
        self_in, heads, cross_in, ffn_in, ffn_out = fetched[layer]
        gate_one, gate_two, scale_one, scale_two, shift_one, shift_two = factors[layer]
        (
            (state_zero, state_one, state_two), self_saved, cross_saved,
            (text_raws, text_inner, text_total), (ffn_pieces, ffn_saved), gain,
        ) = saved[layer]
        in_at, out_at, cross_at, text_at, crossed_at, ffn_at = starts[layer]
        parts, (down_a, up_b, up_a, down_b) = ffn_back(
            place.gather(out), ffn_pieces, ffn_saved, mask, near, far, ffn_in, ffn_out, ffn_at
        )
        grad, out = retreat(place.scatter(parts), state_two, grad, scale_two, valid_rows)

        pieces, raws, inner, total, query, pairs, result, result_inner = cross_saved
        grad_query, pair_grads, cross_out_a, cross_out_b = attend_back(
            place.gather(out), query, rows_of[1], pairs, cross_columns, result, result_inner,
            mask, heads, near, far_heads, crossed_at,
        )
        scaled, stats = back_stats([(grad_query,)], raws, gain[2:3], total, width)
        parts, cross_a, cross_b = project_back(
            scaled, raws, total, arrivals(stats), inner, mask, cross_in, near, far_heads, pieces,
            cross_at,
        )
        terms = place.collect(pair_grads)
        scaled, stats = back_stats([terms], text_raws[:1], gain[3:], text_total, width, (), True)
        (text_grad,), text_a, text_b = project_back(
            scaled, text_raws[:1], text_total, arrivals(stats), text_inner, text_mask, cross_in,
            near, far_heads, text, text_at, False,
        )
        grad_text = grad_text + text_grad
        grad, out = retreat(
            place.scatter(parts), state_one, grad, gains[layer, 4][None], gate_one
        )

        pieces, raws, inner, total, query, pairs, result, result_inner = self_saved
        grad_query, pair_grads, self_out_a, self_out_b = attend_back(
            place.gather(out), query, rows_of[0], pairs, self_columns, result, result_inner,
            mask, heads, near, far_heads, out_at,
        )
        terms = place.collect(pair_grads)
        scaled, stats = back_stats(
            [(grad_query,), terms], raws[:2], gain[:2], total, width, tables, True
        )
        parts, self_a, self_b = project_back(
            scaled, raws[:2], total, arrivals(stats), inner, mask, self_in, near, far_heads, pieces,
            in_at,
        )
        gate = factors[max(layer - 1, 0)][1]
        grad, out = retreat(place.scatter(parts), state_zero, grad, scale_one, gate)

        whole_grads.append(
            jnp.concatenate([self_a, cross_a, text_a, up_a, self_out_b, cross_out_b, down_b], 0)
        )
        part_grads.append(
            jnp.concatenate([self_out_a, cross_out_a, self_b, cross_b, text_b], 0)
        )
        wide_grad = jnp.concatenate([down_a, up_b], 0).reshape(2 * rank, place.size, -1)
        wide_grads.append(wide_grad[:, :, : wide // place.size].reshape(2 * rank, wide))

    def flat(lists):
        return jnp.concatenate(lists[::-1], 0).T

    grad_text = grad_text.astype(bf16)
    count, half = grad_text.shape[0] // TENSOR, width // 2
    slots = [grad_text[k * count : (k + 1) * count] for k in range(TENSOR)]
    text_parts = [
        jnp.concatenate([v[:, at] for v in pair], 0)
        for at, pair in (
            (slice(0, half), (slots[0], slots[2])),
            (slice(0, half), (slots[1], slots[3])),
            (slice(half, width), (slots[0], slots[1])),
            (slice(half, width), (slots[2], slots[3])),
        )
    ]

    def added(terms):
        left, one, two, right, three, four = [v.astype(f32) for v in terms]
        count = two.shape[0]
        return jnp.concatenate(
            [left[:count] + one[:count] + two, right[:count] + three[:count] + four], 1
        )

    whole_all = flat(whole_grads)
    whole_wide = whole_all.shape[1]
    whole_all = whole_all.reshape(place.planes, 2, 2, -1, whole_wide)
    slots = [
        lax.dynamic_slice(
            whole_all,
            (0, (place.p ^ k) % 2, (place.p ^ k) // 2, 0, 0),
            (place.planes, 1, 1) + whole_all.shape[3:],
        ).reshape(-1, whole_wide)
        for k in range(TENSOR)
    ]
    count, half = slots[0].shape[0], whole_wide // 2
    from_parts = added(
        place.scatter(
            [
                jnp.concatenate([v[:, at] for v in pair], 0)
                for at, pair in (
                    (slice(0, half), (slots[0], slots[2])),
                    (slice(0, half), (slots[1], slots[3])),
                    (slice(half, whole_wide), (slots[0], slots[1])),
                    (slice(half, whole_wide), (slots[2], slots[3])),
                )
            ]
        )
    )

    def sum_set(values):
        values = values.astype(f32) + place.other_core(values.astype(bf16)).astype(f32)
        result = values
        for k in range(1, place.blocks):
            result = result + place.other_block(values.astype(bf16), k).astype(f32)
        return result.astype(bf16)

    def to_owner(values):
        planes = values.reshape(place.planes, -1, values.shape[1])
        pieces = []
        for k in range(place.rep):
            plane = (place.g ^ k) * place.blocks + place.b
            piece = lax.dynamic_index_in_dim(planes, plane, 0, False)
            pieces.append(place.other_group(piece, k) if k else piece)
        near = jnp.concatenate(pieces, 1)
        other = place.other_outer(near)
        low = jnp.where(place.o == 0, near, other)
        high = jnp.where(place.o == 0, other, near)
        return jnp.split(jnp.concatenate([low, high], 0), place.rep, 1)

    def heads_to_owner(values):
        planes = values.reshape(place.blocks, -1, values.shape[1])
        mine = lax.dynamic_index_in_dim(planes, place.b, 0, False)
        mine = place.send(mine, lambda o, c, g, b, y: (g // 2, c, 2 * o + y, b, g % 2))
        mine = mine.reshape(2, -1, values.shape[1])
        pieces = []
        for k in range(TENSOR):
            piece = lax.dynamic_index_in_dim(mine, (place.y ^ k) % 2, 0, False)
            pieces.append(place.part(piece, k) if k else piece)
        return pieces

    whole_pieces = to_owner(sum_set(from_parts))
    part_pieces = heads_to_owner(sum_set(flat(part_grads)))
    wide_pieces = to_owner(sum_set(flat(wide_grads)))

    def chooser(adapters):
        column = (adapters[:, None] * ADAPTER_RANK + jnp.arange(ADAPTER_RANK)[None, :]).reshape(-1)
        return (jnp.arange(columns)[:, None] == column[None, :]).astype(bf16)

    def choosers(first):
        return jnp.concatenate(
            [
                chooser(lax.dynamic_index_in_dim(table, first ^ k, 0, False))
                for k in range(place.rep)
            ],
            1,
        )

    choose_near = choosers(place.g)
    choose_heads = choosers(place.p)

    def of_index(pieces, index):
        return jnp.concatenate([p[:, index * rank : (index + 1) * rank] for p in pieces], 1)

    whole_count, part_count = 10, 8
    lora_a, lora_b, lora_a_down, lora_b_up = [], [], [], []
    for layer in range(layers):
        near = [of_index(whole_pieces, layer * whole_count + k) for k in range(whole_count)]
        far = [of_index(part_pieces, layer * part_count + k) for k in range(part_count)]
        q_a, k_a, v_a, cq_a, ck_a, cv_a, up_a, o_b, co_b, down_b = near
        o_a, co_a, q_b, k_b, v_b, cq_b, ck_b, cv_b = far
        a_all = [(v, choose_near) for v in (q_a, k_a, v_a, cq_a, ck_a, cv_a, up_a)]
        a_all = a_all[:3] + [(o_a, choose_heads)] + a_all[3:6] + [(co_a, choose_heads)] + a_all[6:]
        b_all = [(v, choose_heads) for v in (q_b, k_b, v_b, cq_b, ck_b, cv_b)]
        b_all = b_all[:3] + [(o_b, choose_near)] + b_all[3:]
        b_all = b_all + [(co_b, choose_near), (down_b, choose_near)]
        lora_a.append(jnp.stack([dot_nt(v, chosen) for v, chosen in a_all]))
        lora_b.append(jnp.stack([dot_nt(chosen, v) for v, chosen in b_all]))
        lora_a_down.append(dot_nt(of_index(wide_pieces, 2 * layer), choose_near))
        lora_b_up.append(dot_nt(choose_near, of_index(wide_pieces, 2 * layer + 1)))

    grad_text = added(place.scatter(text_parts))
    grad_text = place.swap(grad_text.astype(bf16)).astype(f32)
    return (
        place.swap(state.astype(bf16)),
        place.swap(grad.astype(bf16)).astype(f32),
        grad_text.reshape(context.shape),
        jnp.stack(lora_a),
        jnp.stack(lora_a_down),
        jnp.stack(lora_b),
        jnp.stack(lora_b_up),
    )


def solution(mesh):
    rep, fsdp = AXES[:2], AXES[2:]
    sizes = (mesh.shape["rep"] // 2, 2, mesh.shape["fsdp"] // 2, 2)
    mesh = jax.sharding.Mesh(mesh.devices.reshape(sizes), AXES)
    in_specs = (
        P(AXES, None),
        P(rep, fsdp, None),
        P(AXES, None),
        P(None, AXES),
        P(rep),
        P(rep),
        P(rep),
        P(rep, None, None),
        P(),
        P(),
        P(None, None, fsdp, None),
        P(None, None, fsdp, None),
        P(None, fsdp, None),
        P(None, fsdp, None),
        P(None, None, fsdp, None),
        P(None, fsdp, None),
        P(None, None, None, fsdp),
        P(None, None, fsdp),
    )
    out_specs = (
        P(AXES, None),
        P(AXES, None),
        P(rep, fsdp, None),
        P(None, None, fsdp, None),
        P(None, fsdp, None),
        P(None, None, None, fsdp),
        P(None, None, fsdp),
    )
    return jax.shard_map(
        on_device, mesh=mesh, in_specs=in_specs, out_specs=out_specs, check_vma=False
    )
```

time: 1890 us -> 1280 us (0.68)
  matrix products: 367 us -> 21.4 us
  Pallas kernels: 0 us -> 183 us
  local copies, waits for them, and re-layouts: 454 us -> 316 us
  starting transfers between devices: 453 us -> 321 us
  waiting for transfers between devices: 447 us -> 322 us
  other arithmetic: 131 us -> 71.4 us
    ppermute x205 -> x0, waiting for transfers between devices: 381 us -> none  [send_rows(): return lax.ppermute(values, AXES[1], pairs)]
    ppermute x205 -> x0, starting transfers between devices: 288 us -> none  [send_rows(): return lax.ppermute(values, AXES[1], pairs)]
    ppermute x59 -> x197, waiting for transfers between devices: 65.7 us -> 322 us  [send(): return lax.ppermute(values, AXES, pairs)]
    dot_general x172 -> x0, matrix products: 229 us -> none  [the longest x86 157 us: dot(): return jnp.dot(left, right, preferred_element_type=f32)]
    pallas_call x0 -> x55, Pallas kernels: none -> 183 us  [the longest x48 172 us: call(): pl.pallas_call(kernel, out_shape=outs, in_specs=[pl.BlockSpec(memory_spac...]
    ppermute x59 -> x197, starting transfers between devices: 166 us -> 320 us  [send(): return lax.ppermute(values, AXES, pairs)]
    unnamed x1359 -> x1118, local copies, waits for them, and re-layouts: 48.4 us -> 188 us
    dynamic_update_slice x108 -> x12, local copies, waits for them, and re-layouts: 149 us -> 13.9 us  [the longest x8 10.2 us: on_device(): lax.dynamic_update_slice(near, rows_of[k][None, None], (place.g ^ k, y, 0...]
  transfers between devices with their start and end apart: 264 -> 205, of which waited for: 119 -> 83; matrix products, arithmetic and copies ran while one was open for 44% -> 18% of each run, Pallas kernels for 0% -> 9%
where the time goes in v1:
time: 1280 us; the launch traced here: 1260 us
  waiting for transfers between devices  322 us (25%)
  starting transfers between devices  321 us (25%)
  local copies, waits for them, and re-layouts  316 us (25%)
  Pallas kernels  183 us (14%)
  other arithmetic  71.4 us (6%)
  between operations  27.6 us (2%)
  matrix products  21.4 us (2%)
    ppermute x197, waiting for transfers between devices, send(): return lax.ppermute(values, AXES, pairs)  322 us
    ppermute x197, starting transfers between devices, send(): return lax.ppermute(values, AXES, pairs)  320 us
    unnamed x1118, local copies, waits for them, and re-layouts  188 us
    pallas_call x48, Pallas kernels, call(): pl.pallas_call(kernel, out_shape=outs, in_specs=[pl.BlockSpec(memory_spac...  172 us
  transfers between devices with their start and end apart: 205, of which 83 were waited for; matrix products, arithmetic and copies ran while one was open for 18% of the time, Pallas kernels for 9%

profile of v1, /device:TPU:1, one launch (start us, length us, event | category | flops | bytes accessed | tf_op | source)
XLA Modules:
  0.0 1262.7 jit_solution(4013637577435685667)
XLA Ops:
  60.5 11.0 collective-permute-done.13
  78.1 8.5 collective-permute-done.2.refs_1_.refs_12_
  102.1 17.6 %collective-permute-done.35 = bf16[192,3456]{1,0:T(8,128)(2,1)S(1)} collective-permute-done((bf16[192,3456]{1,0:T(8,128)(2,1)S(1)}, bf16[192,3456]{1,0:T(8,128)(2,1)S(1)}, u32[]{:S(2)}, u32[]{:S(2)}) %collective-permute-start.35) | collective-permute-done | bytes 1327136 | tf_op jit(solution)/shard_map/ppermute | solution.py:62
  151.0 23.7 %collective-permute-start.5 = (bf16[128,768]{1,0:T(8,128)(2,1)S(1)}, bf16[128,768]{1,0:T(8,128)(2,1)S(1)}, u32[]{:S(2)}, u32[]{:S(2)}) collective-permute-start(bf16[128,768]{1,0:T(8,128)(2,1)S(1)} %slice.1601), channel_id=1, source_target_pairs={{0,1},{1,0},{2,3},{3,2},{4,5},{5,4},{6,7},{7,6},{8,9},{9,8},{10,11... | collective-permute-start | bytes 589832 | tf_op jit(solution)/shard_map/ppermute | solution.py:62
  230.0 7.0 collective-permute-done.64
  253.0 10.5 collective-permute-done.24.refs_1_
  264.4 12.7 %collective-permute-done.26.refs_3_ = bf16[384,768]{1,0:T(8,128)(2,1)} collective-permute-done((bf16[384,768]{1,0:T(8,128)(2,1)}, bf16[384,768]{1,0:T(8,128)(2,1)}, u32[]{:S(2)}, u32[]{:S(2)}) %collective-permute-start.26) | collective-permute-done | bytes 589856 | tf_op jit(solution)/shard_map/ppermute | solution.py:62
  290.3 6.5 collective-permute-done.27.refs_1_
  305.9 7.5 collective-permute-done.31.refs_1_.refs_9_
  324.6 17.2 %collective-permute-done.80 = bf16[192,3456]{1,0:T(8,128)(2,1)S(1)} collective-permute-done((bf16[192,3456]{1,0:T(8,128)(2,1)S(1)}, bf16[192,3456]{1,0:T(8,128)(2,1)S(1)}, u32[]{:S(2)}, u32[]{:S(2)}) %collective-permute-start.80) | collective-permute-done | bytes 1327136 | tf_op jit(solution)/shard_map/ppermute | solution.py:62
  350.1 10.7 collective-permute-start.39
  362.6 10.8 collective-permute-done.39.refs_0_.refs_9_
  408.5 10.1 collective-permute-start.47
  483.2 11.6 shard_map.239
  512.6 6.5 collective-permute-done.60.refs_1_.refs_12_
  546.9 11.9 collective-permute-start.68
  572.8 17.9 %collective-permute-done.86 = f32[8,256]{1,0:T(8,128)S(1)} collective-permute-done((f32[8,256]{1,0:T(8,128)}, f32[8,256]{1,0:T(8,128)S(1)}, u32[]{:S(2)}, u32[]{:S(2)}) %collective-permute-start.86) | collective-permute-done | bytes 8224 | tf_op jit(solution)/shard_map/ppermute | solution.py:62
  596.0 7.9 shard_map.245
  610.3 6.4 collective-permute-done.72.refs_1_
  662.8 8.7 collective-permute-start.101
  672.4 8.6 collective-permute-done.89.refs_2_
  714.7 10.4 shard_map.254
  725.1 17.7 %shard_map.256 = (bf16[256,768]{1,0:T(8,128)(2,1)S(1)}, bf16[256,768]{1,0:T(8,128)(2,1)S(1)}, bf16[256,768]{1,0:T(8,128)(2,1)S(1)}, bf16[256,768]{1,0:T(8,128)(2...) custom-call(bf16[128,1536]{1,0:T(8,128)(2,1)S(1)} %copy-done.235, ...), custom_call_target="tpu_custom_call" | custom-call | flops 7247757312 | bytes 23314432 | tf_op jit(solution)/shard_map/pallas_call | solution.py:220
  758.8 8.8 collective-permute-done.110.refs_1_
  784.9 6.4 shard_map.258
  826.7 8.4 collective-permute-done.121.refs_1_
  854.0 9.5 shard_map.262
  864.2 23.7 %collective-permute-start.125 = (bf16[512,768]{1,0:T(8,128)(2,1)S(1)}, bf16[512,768]{1,0:T(8,128)(2,1)S(1)}, u32[]{:S(2)}, u32[]{:S(2)}) collective-permute-start(bf16[512,768]{1,0:T(8,128)(2,1)S(1)} %convert_element_type.565), channel_id=1, source_target_pairs={{0,8},{1,9},{2,10},{3,11},{4,12},{5,13},{6,14},{7,15},{8,0},{9,1},... | collective-permute-start | bytes 2359304 | tf_op jit(solution)/shard_map/ppermute | solution.py:62
  910.4 9.1 collective-permute-done.99.refs_5_
  978.0 18.3 %shard_map.266 = (bf16[256,768]{1,0:T(8,128)(2,1)S(1)}, bf16[256,768]{1,0:T(8,128)(2,1)}, bf16[256,768]{1,0:T(8,128)(2,1)S(1)}, bf16[256,768]{1,0:T(8,128)(2,1)}...) custom-call(bf16[128,1536]{1,0:T(8,128)(2,1)S(1)} %copy-done.409, ...), custom_call_target="tpu_custom_call" | custom-call | flops 7247757312 | bytes 23314432 | tf_op jit(solution)/shard_map/pallas_call | solution.py:220
  1126.1 7.3 collective-permute-start.177
  1133.6 9.2 shard_map.272
  (1908 shorter events, 873.2 us)
Async XLA Ops:
  7.2 186.3 %all-gather.9.cloned.1.call-start = ((), (), s32[]{:S(2)}) async-start(), calls=%async_computation | async-start | bytes 6635520 | tf_op jit(solution)/shard_map/all_gather | solution.py:125
  7.2 27.2 %collective-permute-start.10 = (s32[1]{0:T(128)}, s32[1]{0:T(128)}, u32[]{:S(2)}, u32[]{:S(2)}) collective-permute-start(s32[1]{0:T(128)} %param.23), channel_id=1, source_target_pairs={{0,8},{1,9},{2,10},{3,11},{4,12},{5,13},{6,14},{7,15},{8,0},{9,1},... | collective-permute-start | bytes 20 | tf_op jit(solution)/shard_map/ppermute | solution.py:62
  7.4 28.4 %collective-permute-start.8 = (s32[1]{0:T(128)}, s32[1]{0:T(128)}, u32[]{:S(2)}, u32[]{:S(2)}) collective-permute-start(s32[1]{0:T(128)} %param.23), channel_id=1, source_target_pairs={{0,16},{1,17},{2,18},{3,19},{4,20},{5,21},{6,22},{7,23},{8,24},{9,... | collective-permute-start | bytes 20 | tf_op jit(solution)/shard_map/ppermute | solution.py:62
  10.0 37.3 %collective-permute-start = (bf16[128,1536]{1,0:T(8,128)(2,1)}, bf16[128,1536]{1,0:T(8,128)(2,1)}, u32[]{:S(2)}, u32[]{:S(2)}) collective-permute-start(bf16[128,1536]{1,0:T(8,128)(2,1)} %param.18), channel_id=1, source_target_pairs={{0,0},{1,1},{2,8},{3,9},{4,16},{5,17},{6,24},{7,25},{8,2},{9,3},{1... | collective-permute-start | bytes 1179656 | tf_op jit(solution)/shard_map/ppermute | solution.py:62
  13.5 40.9 %collective-permute-start.1 = (f32[1,6,1536]{2,0,1:T(1,128)}, f32[1,6,1536]{2,0,1:T(1,128)}, u32[]{:S(2)}, u32[]{:S(2)}) collective-permute-start(f32[1,6,1536]{2,0,1:T(1,128)} %param.25), channel_id=1, source_target_pairs={{0,0},{1,1},{2,8},{3,9},{4,16},{5,17},{6,24},{7,25},{8,2},{9,3},{1... | collective-permute-start | bytes 110600 | tf_op jit(solution)/shard_map/ppermute | solution.py:62
  17.6 36.7 %collective-permute-start.6 = (s32[386]{0:T(512)S(1)}, s32[386]{0:T(512)S(1)}, u32[]{:S(2)}, u32[]{:S(2)}) collective-permute-start(s32[386]{0:T(512)S(1)} %pad_add_fusion.3), channel_id=1, source_target_pairs={{0,0},{1,1},{2,8},{3,9},{4,16},{5,17},{6,24},{7,25},{8,2},{9,3},{1... | collective-permute-start | bytes 4640 | tf_op jit(solution)/shard_map/ppermute | solution.py:62
  71.5 314.4 %all-gather.11.cloned.1.call-start = ((), (), s32[]{:S(2)}) async-start(), calls=%async_computation.1 | async-start | bytes 3981312 | tf_op jit(solution)/shard_map/all_gather | solution.py:125
  121.8 351.2 %all-gather.13.cloned.1.call-start = ((), (), s32[]{:S(2)}) async-start(), calls=%async_computation.2 | async-start | bytes 7962624 | tf_op jit(solution)/shard_map/all_gather | solution.py:125
  124.1 348.9 %all-gather.15.cloned.1.call-start = ((), (), s32[]{:S(2)}) async-start(), calls=%async_computation.3 | async-start | bytes 7962624 | tf_op jit(solution)/shard_map/all_gather | solution.py:125
  127.6 399.3 %all-gather.17.cloned.1.call-start = ((), (), s32[]{:S(2)}) async-start(), calls=%async_computation.4 | async-start | bytes 6635520 | tf_op jit(solution)/shard_map/all_gather | solution.py:125
  139.6 35.1 %collective-permute-start.14 = (bf16[4,1,576,128]{3,2,1,0:T(8,128)(2,1)}, bf16[4,1,576,128]{3,2,1,0:T(8,128)(2,1)}, u32[]{:S(2)}, u32[]{:S(2)}) collective-permute-start(bf16[4,1,576,128]{3,2,1,0:T(8,128)(2,1)} %pad_maximum_fusion.6), channel_id=1, source_target_pairs={{0,1},{1,0},{2,3},{3,2},{4,5},{5,4},{6,7},{7,6},{8,9},{9,8},{10,11... | collective-permute-start | bytes 1769480 | tf_op jit(solution)/shard_map/ppermute | solution.py:62
  151.0 41.8 %collective-permute-start.5 = (bf16[128,768]{1,0:T(8,128)(2,1)S(1)}, bf16[128,768]{1,0:T(8,128)(2,1)S(1)}, u32[]{:S(2)}, u32[]{:S(2)}) collective-permute-start(bf16[128,768]{1,0:T(8,128)(2,1)S(1)} %slice.1601), channel_id=1, source_target_pairs={{0,1},{1,0},{2,3},{3,2},{4,5},{5,4},{6,7},{7,6},{8,9},{9,8},{10,11... | collective-permute-start | bytes 589832 | tf_op jit(solution)/shard_map/ppermute | solution.py:62
  239.1 325.6 %all-gather.19.cloned.1.call-start = ((), (), s32[]{:S(2)}) async-start(), calls=%async_computation.5 | async-start | bytes 3981312 | tf_op jit(solution)/shard_map/all_gather | solution.py:125
  239.5 39.4 %collective-permute-start.23 = (bf16[512,768]{1,0:T(8,128)(2,1)}, bf16[512,768]{1,0:T(8,128)(2,1)}, u32[]{:S(2)}, u32[]{:S(2)}) collective-permute-start(bf16[512,768]{1,0:T(8,128)(2,1)} %get-tuple-element.217.refs_2_.refs_7_), channel_id=1, source_target_pairs={{0,8},{1,9},{2,10},{3,11},{4,12},{5,13},{6,14},{7,15},{8,0},{9,1},... | collective-permute-start | bytes 2359304 | tf_op jit(solution)/shard_map/ppermute | solution.py:62
  250.6 26.6 %collective-permute-start.26 = (bf16[384,768]{1,0:T(8,128)(2,1)}, bf16[384,768]{1,0:T(8,128)(2,1)}, u32[]{:S(2)}, u32[]{:S(2)}) collective-permute-start(bf16[384,768]{1,0:T(8,128)(2,1)} %get-tuple-element.423), channel_id=1, source_target_pairs={{0,17},{1,16},{2,19},{3,18},{4,21},{5,20},{6,23},{7,22},{8,25},{9,... | collective-permute-start | bytes 1769480 | tf_op jit(solution)/shard_map/ppermute | solution.py:62
  343.9 358.8 %all-gather.21.cloned.1.call-start = ((), (), s32[]{:S(2)}) async-start(), calls=%async_computation.6 | async-start | bytes 7962624 | tf_op jit(solution)/shard_map/all_gather | solution.py:125
  346.2 356.6 %all-gather.23.cloned.1.call-start = ((), (), s32[]{:S(2)}) async-start(), calls=%async_computation.7 | async-start | bytes 7962624 | tf_op jit(solution)/shard_map/all_gather | solution.py:125
  408.5 28.3 %collective-permute-start.47 = (bf16[256,768]{1,0:T(8,128)(2,1)S(1)}, bf16[256,768]{1,0:T(8,128)(2,1)S(1)}, u32[]{:S(2)}, u32[]{:S(2)}) collective-permute-start(bf16[256,768]{1,0:T(8,128)(2,1)S(1)} %get-tuple-element.233.refs_2_.refs_7_), channel_id=1, source_target_pairs={{0,8},{1,9},{2,10},{3,11},{4,12},{5,13},{6,14},{7,15},{8,0},{9,1},... | collective-permute-start | bytes 1179656 | tf_op jit(solution)/shard_map/ppermute | solution.py:62
  546.9 49.0 %collective-permute-start.68 = (bf16[512,768]{1,0:T(8,128)(2,1)}, bf16[512,768]{1,0:T(8,128)(2,1)}, u32[]{:S(2)}, u32[]{:S(2)}) collective-permute-start(bf16[512,768]{1,0:T(8,128)(2,1)} %get-tuple-element.255.refs_2_.refs_7_), channel_id=1, source_target_pairs={{0,8},{1,9},{2,10},{3,11},{4,12},{5,13},{6,14},{7,15},{8,0},{9,1},... | collective-permute-start | bytes 2359304 | tf_op jit(solution)/shard_map/ppermute | solution.py:62
  561.9 30.1 %collective-permute-start.69 = (bf16[384,768]{1,0:T(8,128)(2,1)}, bf16[384,768]{1,0:T(8,128)(2,1)}, u32[]{:S(2)}, u32[]{:S(2)}) collective-permute-start(bf16[384,768]{1,0:T(8,128)(2,1)} %get-tuple-element.421), channel_id=1, source_target_pairs={{0,1},{1,0},{2,3},{3,2},{4,5},{5,4},{6,7},{7,6},{8,9},{9,8},{10,11... | collective-permute-start | bytes 1769480 | tf_op jit(solution)/shard_map/ppermute | solution.py:62
  562.2 30.9 %collective-permute-start.70 = (bf16[384,768]{1,0:T(8,128)(2,1)}, bf16[384,768]{1,0:T(8,128)(2,1)}, u32[]{:S(2)}, u32[]{:S(2)}) collective-permute-start(bf16[384,768]{1,0:T(8,128)(2,1)} %get-tuple-element.420), channel_id=1, source_target_pairs={{0,16},{1,17},{2,18},{3,19},{4,20},{5,21},{6,22},{7,23},{8,24},{9,... | collective-permute-start | bytes 1769480 | tf_op jit(solution)/shard_map/ppermute | solution.py:62
  563.7 29.5 %collective-permute-start.71 = (bf16[384,768]{1,0:T(8,128)(2,1)}, bf16[384,768]{1,0:T(8,128)(2,1)}, u32[]{:S(2)}, u32[]{:S(2)}) collective-permute-start(bf16[384,768]{1,0:T(8,128)(2,1)} %get-tuple-element.419), channel_id=1, source_target_pairs={{0,17},{1,16},{2,19},{3,18},{4,21},{5,20},{6,23},{7,22},{8,25},{9,... | collective-permute-start | bytes 1769480 | tf_op jit(solution)/shard_map/ppermute | solution.py:62
  695.2 29.9 %collective-permute-start.104 = (bf16[128,768]{1,0:T(8,128)(2,1)}, bf16[128,768]{1,0:T(8,128)(2,1)}, u32[]{:S(2)}, u32[]{:S(2)}) collective-permute-start(bf16[128,768]{1,0:T(8,128)(2,1)} %slice.1673), channel_id=1, source_target_pairs={{0,16},{1,17},{2,18},{3,19},{4,20},{5,21},{6,22},{7,23},{8,24},{9,... | collective-permute-start | bytes 589832 | tf_op jit(solution)/shard_map/ppermute | solution.py:62
  699.9 25.2 %collective-permute-start.105 = (bf16[128,768]{1,0:T(8,128)(2,1)}, bf16[128,768]{1,0:T(8,128)(2,1)}, u32[]{:S(2)}, u32[]{:S(2)}) collective-permute-start(bf16[128,768]{1,0:T(8,128)(2,1)} %slice.1674), channel_id=1, source_target_pairs={{0,1},{1,0},{2,3},{3,2},{4,5},{5,4},{6,7},{7,6},{8,9},{9,8},{10,11... | collective-permute-start | bytes 589832 | tf_op jit(solution)/shard_map/ppermute | solution.py:62
  864.2 27.4 %collective-permute-start.125 = (bf16[512,768]{1,0:T(8,128)(2,1)S(1)}, bf16[512,768]{1,0:T(8,128)(2,1)S(1)}, u32[]{:S(2)}, u32[]{:S(2)}) collective-permute-start(bf16[512,768]{1,0:T(8,128)(2,1)S(1)} %convert_element_type.565), channel_id=1, source_target_pairs={{0,8},{1,9},{2,10},{3,11},{4,12},{5,13},{6,14},{7,15},{8,0},{9,1},... | collective-permute-start | bytes 2359304 | tf_op jit(solution)/shard_map/ppermute | solution.py:62
  937.2 26.2 %collective-permute-start.166 = (f32[8,256]{1,0:T(8,128)S(1)}, f32[8,256]{1,0:T(8,128)S(1)}, u32[]{:S(2)}, u32[]{:S(2)}) collective-permute-start(f32[8,256]{1,0:T(8,128)S(1)} %get-tuple-element.369), channel_id=1, source_target_pairs={{0,1},{1,0},{2,3},{3,2},{4,5},{5,4},{6,7},{7,6},{8,9},{9,8},{10,11... | collective-permute-start | bytes 24584 | tf_op jit(solution)/shard_map/ppermute | solution.py:62
  1072.3 32.2 %collective-permute-start.148 = (bf16[256,768]{1,0:T(8,128)(2,1)}, bf16[256,768]{1,0:T(8,128)(2,1)}, u32[]{:S(2)}, u32[]{:S(2)}) collective-permute-start(bf16[256,768]{1,0:T(8,128)(2,1)} %get-tuple-element.341), channel_id=1, source_target_pairs={{0,1},{1,0},{2,3},{3,2},{4,5},{5,4},{6,7},{7,6},{8,9},{9,8},{10,11... | collective-permute-start | bytes 1179656 | tf_op jit(solution)/shard_map/ppermute | solution.py:62
  1072.4 34.4 %collective-permute-start.150 = (bf16[256,768]{1,0:T(8,128)(2,1)}, bf16[256,768]{1,0:T(8,128)(2,1)}, u32[]{:S(2)}, u32[]{:S(2)}) collective-permute-start(bf16[256,768]{1,0:T(8,128)(2,1)} %get-tuple-element.343), channel_id=1, source_target_pairs={{0,16},{1,17},{2,18},{3,19},{4,20},{5,21},{6,22},{7,23},{8,24},{9,... | collective-permute-start | bytes 1179656 | tf_op jit(solution)/shard_map/ppermute | solution.py:62
  1159.8 27.9 %collective-permute-start.160 = (bf16[256,768]{1,0:T(8,128)(2,1)}, bf16[256,768]{1,0:T(8,128)(2,1)S(1)}, u32[]{:S(2)}, u32[]{:S(2)}) collective-permute-start(bf16[256,768]{1,0:T(8,128)(2,1)} %get-tuple-element.358), channel_id=1, source_target_pairs={{0,1},{1,0},{2,3},{3,2},{4,5},{5,4},{6,7},{7,6},{8,9},{9,8},{10,11... | collective-permute-start | bytes 1179656 | tf_op jit(solution)/shard_map/ppermute | solution.py:62
  1160.5 29.3 %collective-permute-start.162 = (bf16[256,768]{1,0:T(8,128)(2,1)}, bf16[256,768]{1,0:T(8,128)(2,1)S(1)}, u32[]{:S(2)}, u32[]{:S(2)}) collective-permute-start(bf16[256,768]{1,0:T(8,128)(2,1)} %get-tuple-element.360), channel_id=1, source_target_pairs={{0,16},{1,17},{2,18},{3,19},{4,20},{5,21},{6,22},{7,23},{8,24},{9,... | collective-permute-start | bytes 1179656 | tf_op jit(solution)/shard_map/ppermute | solution.py:62
  1188.4 39.5 %collective-permute-start.161 = (bf16[128,768]{1,0:T(8,128)(2,1)}, bf16[128,768]{1,0:T(8,128)(2,1)S(1)}, u32[]{:S(2)}, u32[]{:S(2)}) collective-permute-start(bf16[128,768]{1,0:T(8,128)(2,1)} %add_convert_fusion.8), channel_id=1, source_target_pairs={{0,16},{1,17},{2,18},{3,19},{4,20},{5,21},{6,22},{7,23},{8,24},{9,... | collective-permute-start | bytes 589832 | tf_op jit(solution)/shard_map/ppermute | solution.py:62
  1190.6 37.4 %collective-permute-start.163 = (bf16[128,768]{1,0:T(8,128)(2,1)}, bf16[128,768]{1,0:T(8,128)(2,1)}, u32[]{:S(2)}, u32[]{:S(2)}) collective-permute-start(bf16[128,768]{1,0:T(8,128)(2,1)} %add_convert_fusion.7), channel_id=1, source_target_pairs={{0,1},{1,0},{2,3},{3,2},{4,5},{5,4},{6,7},{7,6},{8,9},{9,8},{10,11... | collective-permute-start | bytes 589832 | tf_op jit(solution)/shard_map/ppermute | solution.py:62
  (717 other events, 7553.4 us)
Sparse Core Ops, SparseCore 0:
  71.7 67.8 all-gather.8
  141.2 51.7 all-gather.10
  195.2 70.5 all-gather.12
  267.9 69.8 all-gather.14
  339.3 68.2 all-gather.16
  409.0 40.1 all-gather.18
  451.4 70.1 all-gather.20
  523.8 69.8 all-gather.22

commit v2 on v1

--- a/solution.py
+++ b/solution.py
@@ -20,7 +20,7 @@
 CHUNK = 256
 SUBLANES = 8
 BLOCK = 512
-VMEM_BYTES = 32 << 20
+VMEM_BYTES = 56 << 20
 
 NEAR = ((0, 0), (0, 1), (0, 2), (0, 4), (0, 5), (0, 6), (0, 8), (1, 3), (1, 7), (1, 8))
 HEADS = ((0, 3), (0, 7), (1, 0), (1, 1), (1, 2), (1, 4), (1, 5), (1, 6))
@@ -62,7 +62,10 @@
         return lax.ppermute(values, AXES, pairs)
 
     def swap(self, values):
-        return self.send(values, lambda o, c, g, b, y: (g // 2, g % 2, 2 * o + c, b, y))
+        return self.send(values, lambda o, c, g, b, y: (g % 2, g // 2, 2 * o + c, b, y))
+
+    def swap_back(self, values):
+        return self.send(values, lambda o, c, g, b, y: (g // 2, g % 2, 2 * c + o, b, y))
 
     def part(self, values, k):
         return self.send(values, lambda o, c, g, b, y: (o ^ (k // 2), c, g, b, y ^ (k % 2)))
@@ -80,7 +83,7 @@
         return self.send(values, lambda o, c, g, b, y: (1 - o, c, g, b, y))
 
     def first_index(self, core, block, part):
-        plane = (2 * (part // 2) + core) * self.blocks + block
+        plane = (2 * core + part // 2) * self.blocks + block
         return 2 * plane + part % 2
 
     def gather(self, rows):
@@ -130,46 +133,56 @@
         )
         return jnp.where(self.y == self.c, mine, arrived)
 
-    def fetch_heads(self, whole, first, matrices):
+    def fetch_heads(self, whole, first, widths):
         count, wide = whole.shape[0] // TENSOR, whole.shape[1] - first
-        pieces = []
-        for k in range(TENSOR):
-            piece = lax.dynamic_slice(whole, ((self.p ^ k) * count, first), (count, wide))
-            pieces.append(self.part(piece, k) if k else piece)
         planes = self.planes // TENSOR
+        half = count // (2 * planes)
+
+        def rows_of(part):
+            return lax.dynamic_slice(whole, (part * count, first), (count, wide))
+
+        def core_rows(part):
+            piece = rows_of(part).reshape(planes, 2, half, wide)
+            return lax.dynamic_index_in_dim(piece, self.c, 1, False).reshape(planes * half, wide)
+
+        halves = [self.part(core_rows(self.p ^ k), k) for k in range(1, TENSOR)]
+        mine = jnp.stack(halves)
+        other = self.other_core(mine)
+        both = jnp.where(
+            self.c == 0, jnp.stack([mine, other], 1), jnp.stack([other, mine], 1)
+        ).reshape(TENSOR - 1, 2, planes, half, wide)
+        pieces = [rows_of(self.p)]
+        pieces += [both[k].transpose(1, 0, 2, 3).reshape(count, wide) for k in range(TENSOR - 1)]
         rows = count // (planes * 2 * TENSOR)
         if rows % (2 * SUBLANES) == 0:
-            return assemble(self.p, pieces, planes, matrices)
-        result = jnp.zeros((planes, 2, 2, 2, rows, matrices, TENSOR, wide // matrices), bf16)
-        for k, piece in enumerate(pieces):
-            piece = piece.reshape(planes, 2, TENSOR, rows, matrices, wide // matrices)
-            piece = piece.transpose(0, 1, 3, 4, 2, 5)[:, None, None]
-            at = (0, self.y ^ (k % 2), self.o ^ (k // 2)) + (0,) * 5
-            result = lax.dynamic_update_slice(result, piece, at)
-        return result.reshape(count, TENSOR * wide)
-
-    def in_order(self, pieces):
-        whole = jnp.stack(pieces)
-        if len(pieces) > 1:
+            return assemble(self.p, pieces, planes, widths)
+        parts, start = [], 0
+        for one in widths:
+            result = jnp.zeros((planes, 2, 2, 2, rows, TENSOR, one), bf16)
             for k, piece in enumerate(pieces):
-                whole = lax.dynamic_update_index_in_dim(whole, piece, self.b ^ k, 0)
-        return whole
-
-    def all_blocks(self, piece):
-        return self.in_order([piece] + [self.other_block(piece, k) for k in range(1, self.blocks)])
+                piece = piece[:, start : start + one].reshape(planes, 2, TENSOR, rows, one)
+                piece = piece.transpose(0, 1, 3, 2, 4)[:, None, None]
+                at = (0, self.y ^ (k % 2), self.o ^ (k // 2)) + (0,) * 4
+                result = lax.dynamic_update_slice(result, piece, at)
+            parts.append(result.reshape(count, TENSOR * one))
+            start += one
+        return jnp.concatenate(parts, 1)
 
 
 def heads_share(matrices, share, shares):
-    number, rows, width = matrices.shape
-    piece = lax.dynamic_slice_in_dim(matrices, share * (rows // shares), rows // shares, 1)
-    piece = piece.reshape(number, rows // shares, TENSOR, width // TENSOR).transpose(2, 1, 0, 3)
-    return piece.reshape(TENSOR * (rows // shares), number * (width // TENSOR))
-
-
-def assemble_kernel(planes, matrices, part, *refs):
+    pieces = []
+    for matrix in matrices:
+        rows, width = matrix.shape[0] // shares, matrix.shape[1] // TENSOR
+        piece = lax.dynamic_slice_in_dim(matrix, share * rows, rows, 0)
+        piece = piece.reshape(rows, TENSOR, width).transpose(1, 0, 2)
+        pieces.append(piece.reshape(TENSOR * rows, width))
+    return jnp.concatenate(pieces, 1)
+
+
+def assemble_kernel(planes, widths, part, *refs):
     pieces, out = refs[:TENSOR], refs[TENSOR]
-    count, wide = pieces[0].shape
-    rows, one = count // (planes * 2 * TENSOR), wide // matrices
+    count = pieces[0].shape[0]
+    rows = count // (planes * 2 * TENSOR)
     for k, piece in enumerate(pieces):
         owner = part[0] ^ k
         place = (owner % 2) * 2 + owner // 2
@@ -179,17 +192,19 @@
                 at = pl.ds(pl.multiple_of(start * rows, rows), rows)
                 for group in range(TENSOR):
                     source = ((plane * 2 + core) * TENSOR + group) * rows
-                    for m in range(matrices):
-                        to = (m * TENSOR + group) * one
+                    first = 0
+                    for one in widths:
+                        to = first * TENSOR + group * one
                         out[at, to : to + one] = piece[
-                            source : source + rows, m * one : (m + 1) * one
+                            source : source + rows, first : first + one
                         ]
-
-
-def assemble(part, pieces, planes, matrices):
+                        first += one
+
+
+def assemble(part, pieces, planes, widths):
     count, wide = pieces[0].shape
     return pl.pallas_call(
-        functools.partial(assemble_kernel, planes, matrices),
+        functools.partial(assemble_kernel, planes, widths),
         out_shape=jax.ShapeDtypeStruct((count, TENSOR * wide), bf16),
         in_specs=[pl.BlockSpec(memory_space=m) for m in [pltpu.SMEM] + [pltpu.VMEM] * TENSOR],
         out_specs=pl.BlockSpec(memory_space=pltpu.VMEM),
@@ -244,6 +259,12 @@
                 ref[row * count : (row + 1) * count, to] = values[
                     slot * count : (slot + 1) * count
                 ]
+
+
+def start_copy(source, held, sem):
+    copy = pltpu.make_async_copy(source, held, sem)
+    copy.start()
+    return copy
 
 
 def join(pieces, full):
@@ -419,96 +440,31 @@
     )(part, square, wide)
 
 
-def pick_kernel(seqs, near_list, heads_list, *refs):
-    adapters, groups, firsts, seconds, wide_firsts, wide_seconds = refs[:6]
-    near, heads, cat = refs[6:]
-    rank = seqs * ADAPTER_RANK
-    per = HD // rank
-    layers, _, rows, _ = firsts.shape
-    row = lax.broadcasted_iota(jnp.int32, (per * HD, HD), 0)
-    column = lax.broadcasted_iota(jnp.int32, (per * HD, HD), 1)
-
-    def one_hot(group):
-        wanted = jnp.zeros_like(column)
-        for s in range(seqs):
-            here = (column // ADAPTER_RANK) % seqs == s
-            wanted = jnp.where(here, adapters[group * seqs + s] * ADAPTER_RANK, wanted)
-        wanted = wanted + column % ADAPTER_RANK + (column // rank) * HD
-        return (row == wanted).astype(f32).astype(bf16)
-
-    hots = [one_hot(groups[k]) for k in range(TENSOR + 2)]
-
-    def blocks(items, count):
-        for block in range(-(-len(items) // per)):
-            here = items[block * per : (block + 1) * per]
-            for k in range(per):
-                at = slice(k * HD, (k + 1) * HD)
-                if k < len(here):
-                    ref, index = here[k]
-                    cat[:count, at] = ref[index]
-                else:
-                    cat[:count, at] = jnp.zeros((count, HD), bf16)
-            yield block, cat[:count]
-
-    refs_of = (firsts, seconds)
-    items = [(refs_of[w], (layer, i)) for layer in range(layers) for w, i in near_list]
-    for block, values in blocks(items, rows):
-        for k in range(TENSOR):
-            near[k, block * rows : (block + 1) * rows] = dot(values, hots[k]).astype(bf16)
-    base = -(-len(items) // per) * rows
-    items = [(refs_of[w], (layer, i)) for layer in range(layers) for w, i in heads_list]
-    for block, values in blocks(items, rows):
-        for k in range(2):
-            heads[k, block * rows : (block + 1) * rows] = dot(values, hots[TENSOR + k]).astype(bf16)
-    units = wide_firsts.shape[1]
-    items = [(ref, (layer,)) for layer in range(layers) for ref in (wide_firsts, wide_seconds)]
-    for block, values in blocks(items, units):
-        at = base + block * units
-        for k in range(TENSOR):
-            near[k, at : at + units] = dot(values, hots[k]).astype(bf16)
-
-
-def pick(adapters, groups, firsts, seconds, wide_firsts, wide_seconds, seqs):
-    layers, _, rows, _ = firsts.shape
-    units = wide_firsts.shape[1]
-    per = HD // (seqs * ADAPTER_RANK)
-    near_rows = -(-layers * len(NEAR) // per) * rows + -(-layers * 2 // per) * units
-    heads_rows = -(-layers * len(HEADS) // per) * rows
-    space = [pltpu.SMEM] * 2 + [pltpu.VMEM] * 4
-    return pl.pallas_call(
-        functools.partial(pick_kernel, seqs, NEAR, HEADS),
-        out_shape=[
-            jax.ShapeDtypeStruct((TENSOR, near_rows, HD), bf16),
-            jax.ShapeDtypeStruct((2, heads_rows, HD), bf16),
-        ],
-        in_specs=[pl.BlockSpec(memory_space=m) for m in space],
-        out_specs=[pl.BlockSpec(memory_space=pltpu.VMEM)] * 2,
-        scratch_shapes=[pltpu.VMEM((max(rows, units), per * HD), bf16)],
-        compiler_params=pltpu.CompilerParams(vmem_limit_bytes=VMEM_BYTES),
-        cost_estimate=pl.CostEstimate(flops=0, bytes_accessed=8 * near_rows * HD, transcendentals=0),
-    )(adapters, groups, firsts, seconds, wide_firsts, wide_seconds)
-
-
 def picked(ref, place, rank, count=1):
     return ref[place * rank : (place + count) * rank]
 
 
 def ffn_kernel(places, *refs):
     pieces, (mask, near, far, w_in, w_out), refs = refs[:5], refs[5:10], refs[10:]
-    parts, (up_raw, up_inner, down_inner), (full, raw, hidden) = refs[:4], refs[4:7], refs[7:]
+    parts, (up_raw, up_inner, down_inner), refs = refs[:4], refs[4:7], refs[7:]
+    full, raw, hidden, held_in, held_out, sems = refs
     rank = mask.shape[1]
     width = full.shape[1]
     up_a, down_b, down_a, up_b = places
+    first = start_copy(w_in, held_in, sems.at[0])
+    second = start_copy(w_out.at[:, pl.ds(0, full.shape[1])], held_out, sems.at[1])
     join(pieces, full)
-    raw[:, : w_in.shape[1]] = dot(full[...], w_in[...])
     inner = narrow(dot_nt(full[...], picked(near, up_a, rank)), mask[...])
     up_inner[...] = inner
+    first.wait()
+    raw[:, : held_in.shape[1]] = dot(full[...], held_in[...])
     factors = picked(far, up_b, rank)
-    for at in chunks(w_in.shape[1]):
+    for at in chunks(held_in.shape[1]):
         values = raw[:, at] + dot(inner, factors[:, at])
         up_raw[:, at] = values.astype(bf16)
         hidden[:, at] = gelu_terms(values)[0].astype(bf16)
-    raw[:, :width] = dot(hidden[...], w_out[...])
+    second.wait()
+    raw[:, :width] = dot(hidden[...], held_out[...])
     inner = narrow(dot_nt(hidden[...], picked(far, down_a, rank)), mask[...])
     down_inner[...] = inner
     put_parts(parts, raw.at[:, :width], inner, picked(near, down_b, rank))
@@ -523,10 +479,13 @@
         pltpu.VMEM((rows, width), bf16),
         pltpu.VMEM((rows, max(wide, width)), f32),
         pltpu.VMEM((rows, wide), bf16),
+        pltpu.VMEM(w_in.shape, bf16),
+        pltpu.VMEM((w_out.shape[0], width), bf16),
+        pltpu.SemaphoreType.DMA((2,)),
     ]
     outs = call(
         functools.partial(ffn_kernel, places), outs + [((rows, rank), bf16)],
-        (*pieces, mask, near, far, w_in, w_out), scratch, 4 * rows * width * wide,
+        (*pieces, mask, near, far, w_in, w_out), scratch, 4 * rows * width * wide, (8, 9),
     )
     return outs[:4], tuple(outs[4:])
 
@@ -535,17 +494,20 @@
     grads, inputs, refs = refs[:5], refs[5:10], refs[10:]
     up_raw, up_inner, down_inner, mask, near, far, w_in, w_out = refs[:8]
     parts, (a_down, b_up, a_up, b_down) = refs[8:12], refs[12:16]
-    grad, full, raw, grad_up = refs[16:]
+    grad, full, raw, grad_up, held_in, held_out, sems = refs[16:]
     rank = mask.shape[1]
     width = full.shape[1]
     at_up_a, at_down_b, at_down_a, at_up_b = places
+    second = start_copy(w_out.at[:, pl.ds(0, full.shape[1])], held_out, sems.at[1])
+    first = start_copy(w_in, held_in, sems.at[0])
     join(grads, grad)
     join(inputs, full)
-    raw[:, : w_out.shape[0]] = dot_nt(grad[...], w_out[...])
     down_back = narrow(dot_nt(grad[...], picked(near, at_down_b, rank)), mask[...])
     down_turned = turned(down_back)
     up_turned = turned(up_inner[...])
     factors = picked(far, at_down_a, rank)
+    second.wait()
+    raw[:, : held_out.shape[0]] = dot_nt(grad[...], held_out[...])
     for at in chunks(up_raw.shape[1]):
         hidden_grad = raw[:, at] + dot(down_back, factors[:, at])
         value, slope = gelu_terms(up_raw[:, at].astype(f32))
@@ -554,7 +516,8 @@
         a_down[:, at] = dot(down_turned, value.astype(bf16)).astype(bf16)
         b_up[:, at] = dot(up_turned, raw_grad).astype(bf16)
     up_back = narrow(dot_nt(grad_up[...], picked(far, at_up_b, rank)), mask[...])
-    raw[:, :width] = dot_nt(grad_up[...], w_in[...])
+    first.wait()
+    raw[:, :width] = dot_nt(grad_up[...], held_in[...])
     put_parts(parts, raw.at[:, :width], up_back, picked(near, at_up_a, rank))
     a_up[...] = dot(turned(up_back), full[...]).astype(bf16)
     b_down[...] = dot(turned(down_inner[...]), grad[...]).astype(bf16)
@@ -570,27 +533,32 @@
         pltpu.VMEM((rows, width), bf16),
         pltpu.VMEM((rows, max(wide, width)), f32),
         pltpu.VMEM((rows, wide), bf16),
+        pltpu.VMEM(w_in.shape, bf16),
+        pltpu.VMEM((w_out.shape[0], width), bf16),
+        pltpu.SemaphoreType.DMA((2,)),
     ]
     outs = call(
         functools.partial(ffn_back_kernel, places), outs,
         (*grads, *inputs, *saved, mask, near, far, w_in, w_out), scratch,
-        4 * rows * width * wide,
+        4 * rows * width * wide, (16, 17),
     )
     return outs[:4], outs[4:]
 
 
 def project_kernel(start, count, normed, *refs):
     pieces, (mask, weights, near, heads), refs = refs[:5], refs[5:9], refs[9:]
-    raws, (inner, stats, full, together) = refs[:count], refs[count:]
+    raws, (inner, stats, full, together, held, sems) = refs[:count], refs[count:]
     own = raws[0].shape[1]
     rank = mask.shape[1]
     base, near_at, heads_at = start
+    copy = start_copy(weights.at[:, pl.ds(base, count * own)], held, sems.at[0])
     join(pieces, full)
-    together[...] = dot(full[...], weights[:, base : base + count * own])
     inner[...] = narrow(
         dot_nt(full[...], picked(near, near_at, rank, count)),
         jnp.concatenate([mask[...]] * count, 1),
     )
+    copy.wait()
+    together[...] = dot(full[...], held[...])
     for k, raw in enumerate(raws):
         values = together[:, k * own : (k + 1) * own] + dot(
             inner[:, k * rank : (k + 1) * rank], picked(heads, heads_at + k, rank)
@@ -608,8 +576,11 @@
     outs = call(
         functools.partial(project_kernel, start, count, normed), outs,
         (*pieces, mask, weights, near, heads),
-        [pltpu.VMEM((rows, pieces[0].shape[1]), bf16), pltpu.VMEM((rows, count * own), f32)],
-        2 * rows * weights.shape[0] * own * count,
+        [
+            pltpu.VMEM((rows, pieces[0].shape[1]), bf16), pltpu.VMEM((rows, count * own), f32),
+            pltpu.VMEM((weights.shape[0], count * own), bf16), pltpu.SemaphoreType.DMA((1,)),
+        ],
+        2 * rows * weights.shape[0] * own * count, (6,),
     )
     return outs[:count], outs[count], outs[count + 1]
 
@@ -651,10 +622,11 @@
     query, marks, refs = refs[0], refs[1], refs[2:]
     pairs, key_marks, refs = refs[:count], refs[count : 2 * count], refs[2 * count :]
     mask, weights, near, heads = refs[:4]
-    parts, result, inner, raw = refs[4:8], refs[8], refs[9], refs[10]
+    parts, (result, inner, raw, held, sems) = refs[4:8], refs[8:]
     rows, own = query.shape
     width, rank = near.shape[1], mask.shape[1]
     base, near_at, heads_at = start
+    copy = start_copy(weights.at[:, pl.ds(base, width)], held, sems.at[0])
     scale = 1.0 / math.sqrt(HD)
     block = min(BLOCK, rows)
 
@@ -681,7 +653,8 @@
             )
             result[at, head : head + HD] = (summed / total).astype(bf16)
 
-    raw[...] = dot(result[...], weights[:, base : base + width])
+    copy.wait()
+    raw[...] = dot(result[...], held[...])
     inner[...] = narrow(dot_nt(result[...], picked(heads, heads_at, rank)), mask[...])
     put_parts(parts, raw, inner[...], picked(near, near_at, rank))
 
@@ -694,7 +667,11 @@
     outs = call(
         functools.partial(attend_kernel, len(pairs), start), outs,
         (query, marks, *pairs, *key_marks, mask, weights, near, heads),
-        [pltpu.VMEM((rows, width), f32)], 4 * rows * keys * own + 2 * rows * own * width,
+        [
+            pltpu.VMEM((rows, width), f32), pltpu.VMEM((own, width), bf16),
+            pltpu.SemaphoreType.DMA((1,)),
+        ],
+        4 * rows * keys * own + 2 * rows * own * width, (3 + 2 * len(pairs),),
     )
     return outs[:4], outs[4], outs[5]
 
@@ -705,17 +682,19 @@
     (result, inner, mask, weights, near, heads), refs = refs[:6], refs[6:]
     base, near_at, heads_at = start
     grad_query, pair_grads, refs = refs[0], refs[1 : 1 + count], refs[1 + count :]
-    a_grad, b_grad, grad, grad_out, raw = refs
+    a_grad, b_grad, grad, grad_out, raw, held, sems = refs
     rows, own = query.shape
     rank = mask.shape[1]
     scale = 1.0 / math.sqrt(HD)
     block = min(BLOCK, rows)
+    copy = start_copy(weights.at[:, pl.ds(base, grad.shape[1])], held, sems.at[0])
     join(grads, grad)
     back = narrow(dot_nt(grad[...], picked(near, near_at, rank)), mask[...])
-    raw[...] = dot_nt(grad[...], weights[:, base : base + grad.shape[1]])
+    b_grad[...] = dot(turned(inner[...]), grad[...]).astype(bf16)
+    copy.wait()
+    raw[...] = dot_nt(grad[...], held[...])
     grad_out[...] = (raw[...] + dot(back, picked(heads, heads_at, rank))).astype(bf16)
     a_grad[...] = dot(turned(back), result[...]).astype(bf16)
-    b_grad[...] = dot(turned(inner[...]), grad[...]).astype(bf16)
     for head in range(0, own, HD):
         here, there = slice(head, head + HD), slice(own + head, own + head + HD)
         keys_turned = [turned(pair[:, here]) for pair in pairs]
@@ -761,9 +740,10 @@
         (*grads, query, marks, *pairs, *key_marks, result, inner, mask, weights, near, heads),
         [
             pltpu.VMEM((rows, width), bf16), pltpu.VMEM((rows, own), bf16),
-            pltpu.VMEM((rows, own), f32),
+            pltpu.VMEM((rows, own), f32), pltpu.VMEM((own, width), bf16),
+            pltpu.SemaphoreType.DMA((1,)),
         ],
-        10 * rows * keys * own + 2 * rows * own * width,
+        10 * rows * keys * own + 2 * rows * own * width, (10 + 2 * len(pairs),),
     )
     return outs[0], outs[1:-2], outs[-2], outs[-1]
 
@@ -808,12 +788,13 @@
     total, (inner, mask, weights, near, heads), refs = refs[0], refs[1:6], refs[6:]
     inputs, refs = refs[:5], refs[5:]
     split = 4 if parted else 1
-    stats, refs = refs[: -6 - split], refs[-6 - split :]
-    outs, (a_grad, b_grad, full, grads, back, raw) = refs[:split], refs[split:]
+    stats, refs = refs[: -8 - split], refs[-8 - split :]
+    outs, (a_grad, b_grad, full, grads, back, raw, held, sems) = refs[:split], refs[split:]
     own = scaled[0].shape[1]
     width = full.shape[1]
     rank = mask.shape[1]
     base, near_at, heads_at = start
+    copy = start_copy(weights.at[:, pl.ds(base, count * own)], held, sems.at[0])
     join(inputs, full)
     along = total_stats(stats)
     for k in range(count):
@@ -831,7 +812,8 @@
         back[:, at] = narrow(dot_nt(grad, picked(heads, heads_at + k, rank)), mask[...])
         b_grad[at] = dot(inner_turned[at], grad).astype(bf16)
     a_grad[...] = dot(turned(back[...]), full[...]).astype(bf16)
-    raw[...] = dot_nt(grads[...], weights[:, base : base + count * own])
+    copy.wait()
+    raw[...] = dot_nt(grads[...], held[...])
     factors = picked(near, near_at, rank, count)
     if parted:
         put_parts(outs, raw, back[...], factors)
@@ -854,11 +836,13 @@
         pltpu.VMEM((rows, count * own), bf16),
         pltpu.VMEM((rows, count * rank), bf16),
         pltpu.VMEM((rows, width), f32),
+        pltpu.VMEM((width, count * own), bf16),
+        pltpu.SemaphoreType.DMA((1,)),
     ]
     outs = call(
         functools.partial(project_back_kernel, start, count, normed, parted), outs,
         (*scaled, *raws, total, inner, mask, weights, near, heads, *inputs, *stats), scratch,
-        2 * rows * width * own * count,
+        2 * rows * width * own * count, (count + normed + 3,),
     )
     return outs[:split], outs[split], outs[split + 1]
 
@@ -896,7 +880,10 @@
 
     numbers = jnp.concatenate([positions.reshape(-1), sequence_lengths, text_token_count])
     numbers = place.swap(numbers)
-    state = place.swap(tokens).astype(f32)
+    moved = place.swap(
+        jnp.concatenate([tokens, context.reshape(seq_count * text_local, width)], 0)
+    )
+    state = moved[:rows].astype(f32)
     times = place.swap(timestep_modulation)
     positions = numbers[: 3 * rows].reshape(3, rows)
     lengths, counts = [
@@ -954,84 +941,82 @@
         for m, values in enumerate((arrived, place.other_core(arrived))):
             here = jnp.arange(place.rep) == 2 * (place.o ^ k) + (place.c ^ m)
             table = jnp.where(here[:, None], values[None], table)
-    half_units = down_first_factor.shape[1] // 2
-    wanted = [place.g ^ k for k in range(TENSOR)] + [place.p, place.p ^ 1]
-    near_share, heads_pick = pick(
-        table.reshape(-1),
-        jnp.stack(wanted).astype(jnp.int32),
-        first_factors,
-        second_factors.transpose(0, 1, 3, 2),
-        lax.dynamic_slice_in_dim(down_first_factor, place.o * half_units, half_units, 1),
-        lax.dynamic_slice_in_dim(
-            up_second_factor.transpose(0, 2, 1), place.o * half_units, half_units, 1
-        ),
-        seq_count,
-    )
-    shard_rows = first_factors.shape[2]
-    wide_blocks = -(-layers * 2 * rank // HD)
-    near_rows = near_share.shape[1] - wide_blocks * half_units
-    from_groups = [near_share[0]]
-    from_groups += [place.other_group(near_share[k], k) for k in range(1, TENSOR)]
-    from_groups = [place.all_blocks(piece) for piece in from_groups]
-    own_rows = jnp.stack([piece[:, :near_rows] for piece in from_groups])
-    other_rows = place.part(own_rows, 1)
-    near = jnp.zeros((place.rep, 2) + own_rows.shape[1:], bf16)
-    far = jnp.zeros((place.rep, place.blocks, wide_blocks * half_units, HD), bf16)
-    for k in range(TENSOR):
-        for rows_of, y in ((own_rows, place.y), (other_rows, 1 - place.y)):
-            near = lax.dynamic_update_slice(
-                near, rows_of[k][None, None], (place.g ^ k, y, 0, 0, 0)
-            )
-        far = lax.dynamic_update_slice(
-            far, from_groups[k][None, :, near_rows:], (place.g ^ k, 0, 0, 0)
-        )
-    near = near.reshape(place.rep, 2, place.blocks, -1, shard_rows, HD)
-    near = near.transpose(0, 2, 1, 4, 3, 5).reshape(width, -1).T
-    far = far.reshape(place.planes, wide_blocks, half_units, HD).transpose(0, 2, 1, 3)
-    far = far.reshape(wide, wide_blocks * HD)
-    far = far.reshape(place.size, -1, wide_blocks * HD)
-    far = jnp.pad(far, ((0, 0), (0, (padded - wide) // place.size), (0, 0))).reshape(padded, -1).T
-    arrived = place.part(heads_pick[1], 1)
-    heads_pick = jnp.where(
-        place.y == 0, jnp.stack([heads_pick[0], arrived]), jnp.stack([arrived, heads_pick[0]])
-    )
-    heads_pick = place.send(
-        heads_pick, lambda o, c, g, b, y: (g // 2, c, 2 * o + y, b, g % 2)
-    )
-    heads_pick = place.all_blocks(heads_pick).reshape(place.blocks, 2, -1, shard_rows, HD)
-    far_heads = heads_pick.transpose(0, 1, 3, 2, 4).reshape(own, -1).T
+    def tied(value, after):
+        return value if after is None else lax.optimization_barrier((value, after))[0]
+
+    wanted = (table[:, :, None] * ADAPTER_RANK + jnp.arange(ADAPTER_RANK)).reshape(-1)
+    choose = (jnp.arange(columns)[:, None] == wanted[None, :]).astype(bf16)
+    firsts = jnp.einsum("lkdj,jr->lkdr", first_factors, choose).astype(bf16)
+    seconds = jnp.einsum("lkjd,jr->lkdr", second_factors, choose).astype(bf16)
+
+    def own_columns(values, count):
+        column = jnp.arange(count * rank * place.rep)
+        kept = jnp.arange(count * rank)
+        here = (column // (rank * place.rep))[:, None] == (kept // rank)[None, :]
+        here &= (column % (rank * place.rep))[:, None] == (place.g * rank + kept % rank)[None, :]
+        return lax.dot_general(
+            here.astype(bf16), values, (((0,), (1,)), ((), ())), preferred_element_type=f32
+        ).astype(bf16)
+
+    factor_rows = [
+        jnp.concatenate([(firsts, seconds)[w][layer, k] for w, k in NEAR], 1)
+        for layer in range(layers)
+    ]
+    factor_rows = jnp.concatenate(factor_rows, 1)
+    factor_rows = place.fetch_columns(factor_rows, factor_rows)
+    factor_width = factor_rows.shape[1] // layers
+
+    def fetch_factors(layer, after):
+        whole = factor_rows[:, layer * factor_width : (layer + 1) * factor_width]
+        return own_columns(place.gather_planes(tied(whole, after)), len(NEAR))
 
     up_at = 6 * own
     part = place.p.astype(jnp.int32)[None]
     share = 2 * place.o + place.c
 
-    def tied(value, after):
-        return value if after is None else lax.optimization_barrier((value, after))[0]
-
-    def fetch_self(layer, after, ready=None):
+    def self_rows_of(layer, after):
         mine, there = pack(
             tied(part, after), query_key_value_weight, up_weight, layer, 3 * own,
             {k * own: k for k in range(3)},
         )
-        rows = place.fetch_columns(mine, there)
-        piece = heads_share(output_weight[layer], share, place.rep)
-        whole = place.gather_planes(tied(jnp.concatenate([rows, piece], 1), ready))
-        return whole, place.fetch_heads(whole, 3 * own, 2)
-
-    def fetch_others(layer, after):
+        factors = [(firsts, seconds)[w][layer, k] for w, k in HEADS]
+        piece = heads_share(
+            [output_weight[layer, 0], output_weight[layer, 1], jnp.concatenate(factors, 1)],
+            share, place.rep,
+        )
+        return jnp.concatenate([place.fetch_columns(mine, there), piece], 1)
+
+    def fetch_self(rows, after):
+        whole = place.gather_planes(tied(rows, after))
+        widths = (own, own, len(HEADS) * rank * place.rep // TENSOR)
+        heads = place.fetch_heads(whole, 3 * own, widths)
+        return whole, heads, own_columns(heads[:, 2 * width :], len(HEADS))
+
+    def other_rows_of(layer, after):
         mine, there = pack(
             tied(part, after), query_key_value_weight, up_weight, layer, 3 * own + padded,
             {k * own: 3 + k for k in range(3)}, (3 * own, 3 * own + padded, place.planes),
         )
-        rows = place.fetch_columns(mine, there)
+        return place.fetch_columns(mine, there)
+
+    def fetch_others(layer, rows, after):
+        rows = tied(rows, after)
         cross = place.gather_planes(rows[:, : 3 * own])
         up = place.gather_planes(rows[:, 3 * own :])
         count = down_weight.shape[1] // place.rep
         piece = lax.dynamic_slice(
             down_weight, (layer, share * count, 0), (1, count, width)
         )[0]
+        factors = [
+            dot(lax.dynamic_slice_in_dim(down_first_factor[layer], share * count, count, 0), choose),
+            dot_tn(
+                lax.dynamic_slice_in_dim(up_second_factor[layer], share * count, count, 1), choose
+            ),
+        ]
+        piece = jnp.concatenate([piece] + [v.astype(bf16) for v in factors], 1)
         piece = jnp.pad(piece, ((0, padded // place.size - count), (0, 0)))
-        return cross, up, place.gather_planes(tied(piece, rows))
+        down = place.gather_planes(tied(piece, rows))
+        return cross, up, down, own_columns(down[:, width:], 2)
 
     positions = jnp.stack([positions] + [place.part(positions, k) for k in range(1, TENSOR)], 1)
     tables = rotary_tables(positions.reshape(3, set_rows))
@@ -1054,15 +1039,8 @@
         [v.reshape(-1, 1) for v in m] for m in (self_marks, cross_marks)
     ]
     zero_row = jnp.zeros((1, width), f32)
-    starts = []
-    for layer in range(layers):
-        one, two, three = layer * len(NEAR), layer * len(HEADS), 2 * layer
-        starts.append(
-            (
-                (0, one, two + 2), (0, one + 7, two), (0, one + 3, two + 5), (own, one + 4, two + 6),
-                (width, one + 8, two + 1), (one + 6, one + 9, three, three + 1),
-            )
-        )
+    in_at, out_at, cross_at, text_at = (0, 0, 2), (0, 7, 0), (0, 3, 5), (own, 4, 6)
+    crossed_at, ffn_at = (width, 8, 1), (6, 9, 0, 1)
 
     saved = []
     factors = []
@@ -1075,18 +1053,23 @@
     hat = centred * lax.rsqrt(jnp.mean(centred * centred, -1, keepdims=True) + epsilon)
     normed = (hat * factors[0][2] + factors[0][4]).astype(bf16)
     fetched = []
-    coming = fetch_self(0, None, (state, numbers, times, from_groups))
+    coming = fetch_self(self_rows_of(0, None), (moved, numbers, times))
+    picked_now = fetch_factors(0, None)
     others = None
     for layer in range(layers):
         gate_one, gate_two, scale_one, scale_two, shift_one, shift_two = factors[layer]
-        in_at, out_at, cross_at, text_at, crossed_at, ffn_at = starts[layer]
-        self_in, heads = coming
+        self_in, heads, far_heads = coming
+        near = picked_now
         self_pieces = place.gather(normed)
         if layer == 0:
-            others = fetch_others(layer, self_pieces[3])
-            text = tied(context.reshape(seq_count * text_local, width), self_pieces[3])
-            text = place.gather(place.swap(text))
-        cross_in, ffn_in, ffn_out = others
+            first_rows = other_rows_of(layer, self_pieces[3])
+            others = fetch_others(layer, first_rows, None)
+            prepared = [
+                (self_rows_of(k, first_rows), other_rows_of(k, first_rows))
+                for k in range(1, layers)
+            ]
+            text = place.gather(tied(moved[rows:], self_pieces[3]))
+        cross_in, ffn_in, ffn_out, far = others
         raws, self_inner, stats = project(self_pieces, mask, self_in, near, far_heads, in_at, 3, 2)
         gain = [own_gain(layer, k) for k in range(4)]
         (query, pair), self_total = normalize(
@@ -1094,7 +1077,8 @@
         )
         pairs = place.spread(pair)
         if layer + 1 < layers:
-            coming = fetch_self(layer + 1, query)
+            coming = fetch_self(prepared[layer][0], query)
+            picked_now = fetch_factors(layer + 1, query)
         parts, attended, out_inner = attend(
             query, columns_of[0], pairs, self_rows, mask, heads, near, far_heads, out_at
         )
@@ -1112,9 +1096,9 @@
         pairs = place.spread(pair)
         cross_pieces = place.gather(normed)
         if layer + 1 < layers:
-            others = fetch_others(layer + 1, cross_pieces[3])
+            others = fetch_others(layer + 1, prepared[layer][1], cross_pieces[3])
         else:
-            cotangent = place.swap(tied(cotangent, cross_pieces[3]))
+            cotangent = place.swap(tied(cotangent, ffn_out[:SUBLANES]))
         raws, cross_inner, stats = project(
             cross_pieces, mask, cross_in, near, far_heads, cross_at, 1, 1
         )
@@ -1130,8 +1114,9 @@
         )
 
         ffn_pieces = place.gather(normed)
-        parts, ffn_saved = ffn(ffn_pieces, mask, near, far, ffn_in, ffn_out, ffn_at)
-        fetched.append((self_in, heads, cross_in, ffn_in, ffn_out))
+        ready = mask if layer + 1 == layers else tied(mask, coming[1])
+        parts, ffn_saved = ffn(ffn_pieces, ready, near, far, ffn_in, ffn_out, ffn_at)
+        fetched.append((self_in, heads, cross_in, ffn_in, ffn_out, near, far, far_heads))
         saved.append(
             (
                 (state, state_one, state_two), self_saved, cross_saved,
@@ -1148,13 +1133,12 @@
     grad_text = 0.0
     whole_grads, part_grads, wide_grads = [], [], []
     for layer in reversed(range(layers)):
-        self_in, heads, cross_in, ffn_in, ffn_out = fetched[layer]
+        self_in, heads, cross_in, ffn_in, ffn_out, near, far, far_heads = fetched[layer]
         gate_one, gate_two, scale_one, scale_two, shift_one, shift_two = factors[layer]
         (
             (state_zero, state_one, state_two), self_saved, cross_saved,
             (text_raws, text_inner, text_total), (ffn_pieces, ffn_saved), gain,
         ) = saved[layer]
-        in_at, out_at, cross_at, text_at, crossed_at, ffn_at = starts[layer]
         parts, (down_a, up_b, up_a, down_b) = ffn_back(
             place.gather(out), ffn_pieces, ffn_saved, mask, near, far, ffn_in, ffn_out, ffn_at
         )
@@ -1327,10 +1311,10 @@
         lora_b_up.append(dot_nt(choose_near, of_index(wide_pieces, 2 * layer + 1)))
 
     grad_text = added(place.scatter(text_parts))
-    grad_text = place.swap(grad_text.astype(bf16)).astype(f32)
+    grad_text = place.swap_back(grad_text.astype(bf16)).astype(f32)
     return (
-        place.swap(state.astype(bf16)),
-        place.swap(grad.astype(bf16)).astype(f32),
+        place.swap_back(state.astype(bf16)),
+        place.swap_back(grad.astype(bf16)).astype(f32),
         grad_text.reshape(context.shape),
         jnp.stack(lora_a),
         jnp.stack(lora_a_down),

time: 1280 us -> 1170 us (0.914)
  local copies, waits for them, and re-layouts: 316 us -> 106 us
  Pallas kernels: 183 us -> 323 us
  starting transfers between devices: 321 us -> 244 us
  waiting for transfers between devices: 322 us -> 346 us
    unnamed x1118 -> x566, local copies, waits for them, and re-layouts: 188 us -> 36.6 us
    pallas_call x48, Pallas kernels: 172 us -> 303 us  [call(): pl.pallas_call(kernel, out_shape=outs, in_specs=[pl.BlockSpec(memory_spac...]
    ppermute x197 -> x193, starting transfers between devices: 320 us -> 243 us  [send(): return lax.ppermute(values, AXES, pairs)]
    all_gather x8 -> x10, waiting for transfers between devices: 0.01 us -> 35 us  [gather_planes(): return lax.all_gather(rows, (AXES[2], AXES[1]), axis=0, tiled=True)]
    dot_general x0 -> x12, matrix products: none -> 22 us  [the longest x6 15.6 us: own_columns(): lax.dot_general(here.astype(bf16), values, (((0,), (1,)), ((), ())), pref...]
    dynamic_update_slice x12 -> x0, local copies, waits for them, and re-layouts: 13.9 us -> none  [the longest x8 10.2 us: on_device(): lax.dynamic_update_slice(near, rows_of[k][None, None], (place.g ^ k, y, 0...]
    ppermute x197 -> x193, waiting for transfers between devices: 322 us -> 311 us  [send(): return lax.ppermute(values, AXES, pairs)]
  transfers between devices with their start and end apart: 205 -> 203, of which waited for: 83 -> 91; matrix products, arithmetic and copies ran while one was open for 18% -> 16% of each run, Pallas kernels for 9% -> 20%
where the time goes in v2:
time: 1170 us; the launch traced here: 1160 us
  waiting for transfers between devices  346 us (30%)
  Pallas kernels  323 us (28%)
  starting transfers between devices  244 us (21%)
  local copies, waits for them, and re-layouts  106 us (9%)
  other arithmetic  82.1 us (7%)
  matrix products  34 us (3%)
  between operations  25.3 us (2%)
    ppermute x193, waiting for transfers between devices, send(): return lax.ppermute(values, AXES, pairs)  311 us
    pallas_call x48, Pallas kernels, call(): pl.pallas_call(kernel, out_shape=outs, in_specs=[pl.BlockSpec(memory_spac...  303 us
    ppermute x193, starting transfers between devices, send(): return lax.ppermute(values, AXES, pairs)  243 us
    unnamed x566, local copies, waits for them, and re-layouts  36.6 us
    all_gather x10, waiting for transfers between devices, gather_planes(): return lax.all_gather(rows, (AXES[2], AXES[1]), axis=0, tiled=True)  35 us
  transfers between devices with their start and end apart: 203, of which 91 were waited for; matrix products, arithmetic and copies ran while one was open for 16% of the time, Pallas kernels for 20%

profile of v2, /device:TPU:1, one launch (start us, length us, event | category | flops | bytes accessed | tf_op | source)
XLA Modules:
  0.0 1160.9 jit_solution(5738697835901696149)
XLA Ops:
  57.3 11.1 collective-permute-done.2.refs_1_.refs_12_
  80.8 16.9 %collective-permute-done.31 = bf16[192,3456]{1,0:T(8,128)(2,1)S(1)} collective-permute-done((bf16[192,3456]{1,0:T(8,128)(2,1)}, bf16[192,3456]{1,0:T(8,128)(2,1)S(1)}, u32[]{:S(2)}, u32[]{:S(2)}) %collective-permute-start.31) | collective-permute-done | bytes 1327136 | tf_op jit(solution)/shard_map/ppermute | solution.py:62
  158.5 8.0 shard_map.227
  202.4 7.8 shard_map.229
  211.3 29.4 %collective-permute-done.97 = bf16[128,1536]{1,0:T(8,128)(2,1)S(1)} collective-permute-done((bf16[128,1536]{1,0:T(8,128)(2,1)}, bf16[128,1536]{1,0:T(8,128)(2,1)S(1)}, u32[]{:S(2)}, u32[]{:S(2)}) %collective-permute-start.97) | collective-permute-done | bytes 393248 | tf_op jit(solution)/shard_map/ppermute | solution.py:62
  253.4 14.5 %collective-permute-done.26.refs_5_ = bf16[128,768]{1,0:T(8,128)(2,1)S(1)} collective-permute-done((bf16[128,768]{1,0:T(8,128)(2,1)S(1)}, bf16[128,768]{1,0:T(8,128)(2,1)S(1)}, u32[]{:S(2)}, u32[]{:S(2)}) %collective-permute-start.26) | collective-permute-done | bytes 196640 | tf_op jit(solution)/shard_map/ppermute | solution.py:62
  271.9 7.2 collective-permute-done.27.refs_1_.refs_9_
  367.1 7.7 collective-permute-done.43.refs_1_
  403.6 8.2 all-gather.21.cloned.1.call-done.refs_8_.refs_16_
  411.8 17.3 %shard_map.240 = (bf16[256,768]{1,0:T(8,128)(2,1)}, bf16[256,768]{1,0:T(8,128)(2,1)}, bf16[256,768]{1,0:T(8,128)(2,1)}, bf16[256,768]{1,0:T(8,128)(2,1)}, bf16[5...) custom-call(bf16[128,1536]{1,0:T(8,128)(2,1)} %get-tuple-element.237.refs_0_.refs_5_, ...), custom_call_target="tpu_custom_call" | custom-call | flops 7247757312 | bytes 20955136 | tf_op jit(solution)/shard_map/pallas_call | solution.py:235
  431.6 8.2 collective-permute-done.56.refs_1_
  468.9 8.1 shard_map.242
  503.1 7.9 shard_map.244
  513.2 8.1 collective-permute-done.68.refs_1_
  592.2 8.2 collective-permute-done.88.refs_1_.refs_6_
  605.1 26.8 %all-gather.29.cloned.1.call-done.refs_8_.refs_16_ = bf16[1536,2304]{1,0:T(8,128)(2,1)} async-done(((bf16[192,2304]{1,0:T(8,128)(2,1)}), bf16[1536,2304]{1,0:T(8,128)(2,1)}) %all-gather.29.cloned.1.call-update) | async-done | bytes 7077904 | tf_op jit(solution)/shard_map/all_gather | solution.py:128
  633.3 17.0 %shard_map.253 = (bf16[256,768]{1,0:T(8,128)(2,1)}, bf16[256,768]{1,0:T(8,128)(2,1)}, bf16[256,768]{1,0:T(8,128)(2,1)}, bf16[256,768]{1,0:T(8,128)(2,1)}, bf16[5...) custom-call(bf16[128,1536]{1,0:T(8,128)(2,1)} %get-tuple-element.278.refs_0_.refs_5_, ...), custom_call_target="tpu_custom_call" | custom-call | flops 7247757312 | bytes 20955136 | tf_op jit(solution)/shard_map/pallas_call | solution.py:235
  651.1 20.9 %shard_map.255 = (bf16[256,768]{1,0:T(8,128)(2,1)}, bf16[256,768]{1,0:T(8,128)(2,1)}, bf16[256,768]{1,0:T(8,128)(2,1)}, bf16[256,768]{1,0:T(8,128)(2,1)}, bf16[1...) custom-call(bf16[128,1536]{1,0:T(8,128)(2,1)} %get-tuple-element.724.refs_0_, ...), custom_call_target="tpu_custom_call" | custom-call | flops 7247757312 | bytes 22773760 | tf_op jit(solution)/shard_map/pallas_call | solution.py:235
  674.5 8.3 collective-permute-done.102.refs_1_
  711.1 9.3 shard_map.257
  769.8 12.6 %shard_map.261 = (f32[512,384]{1,0:T(8,128)}, f32[512,768]{1,0:T(8,128)}, f32[512,768]{1,0:T(8,128)}, bf16[16,384]{1,0:T(8,128)(2,1)}, bf16[16,1536]{1,0:T(8,128)(2,1)}) custom-call(bf16[128,1536]{1,0:T(8,128)(2,1)} %get-tuple-element.306.refs_0_, bf16[128,1536]{1,0:T(8,128)(2,1)} %copy-done.164, bf16[128,1536]{1,0:T(8,128)(2,1)} %copy-done.165, ...), custom_call_target="tpu_custom_call" | custom-call | flops 2617245696 | bytes 11323392 | tf_op jit(solution)/shard_map/pallas_call | solution.py:235
  784.0 11.6 %collective-permute-start.121 = (bf16[512,768]{1,0:T(8,128)(2,1)S(1)}, bf16[512,768]{1,0:T(8,128)(2,1)S(1)}, u32[]{:S(2)}, u32[]{:S(2)}) collective-permute-start(bf16[512,768]{1,0:T(8,128)(2,1)S(1)} %convert_element_type.610), channel_id=1, source_target_pairs={{0,8},{1,9},{2,10},{3,11},{4,12},{5,13},{6,14},{7,15},{8,0},{9,1},... | collective-permute-start | bytes 2359304 | tf_op jit(solution)/shard_map/ppermute | solution.py:62
  810.6 8.5 shard_map.263
  821.4 10.6 collective-permute-done.95.refs_5_
  865.3 7.4 collective-permute-done.129.refs_1_
  880.5 21.1 %shard_map.265 = (bf16[256,768]{1,0:T(8,128)(2,1)}, bf16[256,768]{1,0:T(8,128)(2,1)}, bf16[256,768]{1,0:T(8,128)(2,1)}, bf16[256,768]{1,0:T(8,128)(2,1)}, bf16[1...) custom-call(bf16[128,1536]{1,0:T(8,128)(2,1)} %get-tuple-element.323.refs_0_, ...), custom_call_target="tpu_custom_call" | custom-call | flops 7247757312 | bytes 22773760 | tf_op jit(solution)/shard_map/pallas_call | solution.py:235
  940.9 8.9 shard_map.267
  977.1 7.6 collective-permute-done.167
  1017.1 9.5 collective-permute-start.173
  1027.4 12.4 %shard_map.271 = (f32[512,384]{1,0:T(8,128)}, f32[512,768]{1,0:T(8,128)}, f32[512,768]{1,0:T(8,128)}, bf16[16,384]{1,0:T(8,128)(2,1)}, bf16[16,1536]{1,0:T(8,128)(2,1)}) custom-call(bf16[128,1536]{1,0:T(8,128)(2,1)} %get-tuple-element.345.refs_0_, bf16[128,1536]{1,0:T(8,128)(2,1)} %copy-done.158, bf16[128,1536]{1,0:T(8,128)(2,1)} %copy-done.159, ...), custom_call_target="tpu_custom_call" | custom-call | flops 2617245696 | bytes 11323392 | tf_op jit(solution)/shard_map/pallas_call | solution.py:235
  1058.3 8.6 shard_map.273
  1132.5 7.4 collective-permute-start.160
  (1378 shorter events, 758.5 us)
Async XLA Ops:
  7.2 105.8 %all-gather.11.cloned.1.call-start = ((), (), s32[]{:S(2)}) async-start(), calls=%async_computation | async-start | bytes 7077888 | tf_op jit(solution)/shard_map/all_gather | solution.py:128
  7.4 26.4 %collective-permute-start.8 = (s32[1]{0:T(128)}, s32[1]{0:T(128)}, u32[]{:S(2)}, u32[]{:S(2)}) collective-permute-start(s32[1]{0:T(128)} %param.23), channel_id=1, source_target_pairs={{0,16},{1,17},{2,18},{3,19},{4,20},{5,21},{6,22},{7,23},{8,24},{9,... | collective-permute-start | bytes 20 | tf_op jit(solution)/shard_map/ppermute | solution.py:62
  10.0 35.2 %collective-permute-start.1 = (f32[1,6,1536]{2,0,1:T(1,128)}, f32[1,6,1536]{2,0,1:T(1,128)S(1)}, u32[]{:S(2)}, u32[]{:S(2)}) collective-permute-start(f32[1,6,1536]{2,0,1:T(1,128)} %param.25), channel_id=1, source_target_pairs={{0,0},{1,1},{2,16},{3,17},{4,8},{5,9},{6,24},{7,25},{8,2},{9,3},{1... | collective-permute-start | bytes 110600 | tf_op jit(solution)/shard_map/ppermute | solution.py:62
  15.4 29.9 %collective-permute-start = (bf16[192,1536]{1,0:T(8,128)(2,1)}, bf16[192,1536]{1,0:T(8,128)(2,1)S(1)}, u32[]{:S(2)}, u32[]{:S(2)}) collective-permute-start(bf16[192,1536]{1,0:T(8,128)(2,1)} %pad_maximum_fusion.8), channel_id=1, source_target_pairs={{0,0},{1,1},{2,16},{3,17},{4,8},{5,9},{6,24},{7,25},{8,2},{9,3},{1... | collective-permute-start | bytes 1769480 | tf_op jit(solution)/shard_map/ppermute | solution.py:62
  19.4 25.8 %collective-permute-start.6 = (s32[386]{0:T(512)S(1)}, s32[386]{0:T(512)S(1)}, u32[]{:S(2)}, u32[]{:S(2)}) collective-permute-start(s32[386]{0:T(512)S(1)} %pad_add_fusion.3), channel_id=1, source_target_pairs={{0,0},{1,1},{2,16},{3,17},{4,8},{5,9},{6,24},{7,25},{8,2},{9,3},{1... | collective-permute-start | bytes 4640 | tf_op jit(solution)/shard_map/ppermute | solution.py:62
  45.3 99.0 %all-gather.13.cloned.1.call-start = ((), (), s32[]{:S(2)}) async-start(), calls=%async_computation.1 | async-start | bytes 2211840 | tf_op jit(solution)/shard_map/all_gather | solution.py:128
  56.4 250.1 %all-gather.15.cloned.1.call-start = ((), (), s32[]{:S(2)}) async-start(), calls=%async_computation.2 | async-start | bytes 3981312 | tf_op jit(solution)/shard_map/all_gather | solution.py:128
  98.7 246.4 %all-gather.17.cloned.1.call-start = ((), (), s32[]{:S(2)}) async-start(), calls=%async_computation.3 | async-start | bytes 7077888 | tf_op jit(solution)/shard_map/all_gather | solution.py:128
  177.3 209.5 %all-gather.19.cloned.1.call-start = ((), (), s32[]{:S(2)}) async-start(), calls=%async_computation.4 | async-start | bytes 8626176 | tf_op jit(solution)/shard_map/all_gather | solution.py:128
  190.3 221.5 %all-gather.21.cloned.1.call-start = ((), (), s32[]{:S(2)}) async-start(), calls=%async_computation.5 | async-start | bytes 7962624 | tf_op jit(solution)/shard_map/all_gather | solution.py:128
  191.3 262.9 %all-gather.23.cloned.1.call-start = ((), (), s32[]{:S(2)}) async-start(), calls=%async_computation.6 | async-start | bytes 2211840 | tf_op jit(solution)/shard_map/all_gather | solution.py:128
  194.9 45.8 %collective-permute-start.97 = (bf16[128,1536]{1,0:T(8,128)(2,1)}, bf16[128,1536]{1,0:T(8,128)(2,1)S(1)}, u32[]{:S(2)}, u32[]{:S(2)}) collective-permute-start(bf16[128,1536]{1,0:T(8,128)(2,1)} %param.20), channel_id=1, source_target_pairs={{0,0},{1,1},{2,16},{3,17},{4,8},{5,9},{6,24},{7,25},{8,2},{9,3},{1... | collective-permute-start | bytes 1179656 | tf_op jit(solution)/shard_map/ppermute | solution.py:62
  198.3 294.2 %all-gather.25.cloned.1.call-start = ((), (), s32[]{:S(2)}) async-start(), calls=%async_computation.7 | async-start | bytes 3981312 | tf_op jit(solution)/shard_map/all_gather | solution.py:128
  210.3 38.1 %collective-permute-start.23 = (bf16[256,768]{1,0:T(8,128)(2,1)}, bf16[256,768]{1,0:T(8,128)(2,1)S(1)}, u32[]{:S(2)}, u32[]{:S(2)}) collective-permute-start(bf16[256,768]{1,0:T(8,128)(2,1)} %get-tuple-element.217), channel_id=1, source_target_pairs={{0,1},{1,0},{2,3},{3,2},{4,5},{5,4},{6,7},{7,6},{8,9},{9,8},{10,11... | collective-permute-start | bytes 1179656 | tf_op jit(solution)/shard_map/ppermute | solution.py:62
  210.3 38.2 %collective-permute-start.25 = (bf16[256,768]{1,0:T(8,128)(2,1)}, bf16[256,768]{1,0:T(8,128)(2,1)S(1)}, u32[]{:S(2)}, u32[]{:S(2)}) collective-permute-start(bf16[256,768]{1,0:T(8,128)(2,1)} %get-tuple-element.219), channel_id=1, source_target_pairs={{0,16},{1,17},{2,18},{3,19},{4,20},{5,21},{6,22},{7,23},{8,24},{9,... | collective-permute-start | bytes 1179656 | tf_op jit(solution)/shard_map/ppermute | solution.py:62
  247.1 32.2 %collective-permute-start.76 = (bf16[192,3456]{1,0:T(8,128)(2,1)}, bf16[192,3456]{1,0:T(8,128)(2,1)S(1)}, u32[]{:S(2)}, u32[]{:S(2)}) collective-permute-start(bf16[192,3456]{1,0:T(8,128)(2,1)} %get-tuple-element.264), channel_id=1, source_target_pairs={{0,1},{2,3},{4,5},{6,7},{9,8},{11,10},{13,12},{15,14},{16,17},{18,... | collective-permute-start | bytes 3981320 | tf_op jit(solution)/shard_map/ppermute | solution.py:62
  285.0 318.0 %all-gather.27.cloned.1.call-start = ((), (), s32[]{:S(2)}) async-start(), calls=%async_computation.8 | async-start | bytes 8626176 | tf_op jit(solution)/shard_map/all_gather | solution.py:128
  291.2 340.8 %all-gather.29.cloned.1.call-start = ((), (), s32[]{:S(2)}) async-start(), calls=%async_computation.9 | async-start | bytes 7962624 | tf_op jit(solution)/shard_map/all_gather | solution.py:128
  366.5 30.1 %collective-permute-start.55 = (bf16[3,192,896]{2,1,0:T(8,128)(2,1)S(1)}, bf16[3,192,896]{2,1,0:T(8,128)(2,1)}, u32[]{:S(2)}, u32[]{:S(2)}) collective-permute-start(bf16[3,192,896]{2,1,0:T(8,128)(2,1)S(1)} %get-tuple-element.442), channel_id=1, source_target_pairs={{0,8},{1,9},{2,10},{3,11},{4,12},{5,13},{6,14},{7,15},{8,0},{9,1},... | collective-permute-start | bytes 3096584 | tf_op jit(solution)/shard_map/ppermute | solution.py:62
  591.4 59.0 %collective-permute-start.100 = (bf16[128,768]{1,0:T(8,128)(2,1)S(1)}, bf16[128,768]{1,0:T(8,128)(2,1)S(1)}, u32[]{:S(2)}, u32[]{:S(2)}) collective-permute-start(bf16[128,768]{1,0:T(8,128)(2,1)S(1)} %slice.1870), channel_id=1, source_target_pairs={{0,16},{1,17},{2,18},{3,19},{4,20},{5,21},{6,22},{7,23},{8,24},{9,... | collective-permute-start | bytes 589832 | tf_op jit(solution)/shard_map/ppermute | solution.py:62
  591.6 58.8 %collective-permute-start.101 = (bf16[128,768]{1,0:T(8,128)(2,1)S(1)}, bf16[128,768]{1,0:T(8,128)(2,1)S(1)}, u32[]{:S(2)}, u32[]{:S(2)}) collective-permute-start(bf16[128,768]{1,0:T(8,128)(2,1)S(1)} %slice.1871), channel_id=1, source_target_pairs={{0,1},{1,0},{2,3},{3,2},{4,5},{5,4},{6,7},{7,6},{8,9},{9,8},{10,11... | collective-permute-start | bytes 589832 | tf_op jit(solution)/shard_map/ppermute | solution.py:62
  600.4 31.6 %collective-permute-start.90 = (bf16[128,768]{1,0:T(8,128)(2,1)S(1)}, bf16[128,768]{1,0:T(8,128)(2,1)S(1)}, u32[]{:S(2)}, u32[]{:S(2)}) collective-permute-start(bf16[128,768]{1,0:T(8,128)(2,1)S(1)} %slice.1864), channel_id=1, source_target_pairs={{0,16},{1,17},{2,18},{3,19},{4,20},{5,21},{6,22},{7,23},{8,24},{9,... | collective-permute-start | bytes 589832 | tf_op jit(solution)/shard_map/ppermute | solution.py:62
  600.7 31.3 %collective-permute-start.91 = (bf16[128,768]{1,0:T(8,128)(2,1)S(1)}, bf16[128,768]{1,0:T(8,128)(2,1)S(1)}, u32[]{:S(2)}, u32[]{:S(2)}) collective-permute-start(bf16[128,768]{1,0:T(8,128)(2,1)S(1)} %slice.1865), channel_id=1, source_target_pairs={{0,1},{1,0},{2,3},{3,2},{4,5},{5,4},{6,7},{7,6},{8,9},{9,8},{10,11... | collective-permute-start | bytes 589832 | tf_op jit(solution)/shard_map/ppermute | solution.py:62
  807.9 35.1 %collective-permute-start.161 = (bf16[256,768]{1,0:T(8,128)(2,1)S(1)}, bf16[256,768]{1,0:T(8,128)(2,1)S(1)}, u32[]{:S(2)}, u32[]{:S(2)}) collective-permute-start(bf16[256,768]{1,0:T(8,128)(2,1)S(1)} %convert_element_type.638), channel_id=1, source_target_pairs={{0,8},{1,9},{2,10},{3,11},{4,12},{5,13},{6,14},{7,15},{8,0},{9,1},... | collective-permute-start | bytes 1179656 | tf_op jit(solution)/shard_map/ppermute | solution.py:62
  819.1 29.0 %collective-permute-start.125 = (bf16[256,768]{1,0:T(8,128)(2,1)}, bf16[256,768]{1,0:T(8,128)(2,1)S(1)}, u32[]{:S(2)}, u32[]{:S(2)}) collective-permute-start(bf16[256,768]{1,0:T(8,128)(2,1)} %get-tuple-element.319), channel_id=1, source_target_pairs={{0,1},{1,0},{2,3},{3,2},{4,5},{5,4},{6,7},{7,6},{8,9},{9,8},{10,11... | collective-permute-start | bytes 1179656 | tf_op jit(solution)/shard_map/ppermute | solution.py:62
  820.8 28.5 %collective-permute-start.127 = (bf16[256,768]{1,0:T(8,128)(2,1)}, bf16[256,768]{1,0:T(8,128)(2,1)S(1)}, u32[]{:S(2)}, u32[]{:S(2)}) collective-permute-start(bf16[256,768]{1,0:T(8,128)(2,1)} %get-tuple-element.321), channel_id=1, source_target_pairs={{0,16},{1,17},{2,18},{3,19},{4,20},{5,21},{6,22},{7,23},{8,24},{9,... | collective-permute-start | bytes 1179656 | tf_op jit(solution)/shard_map/ppermute | solution.py:62
  930.7 26.4 %collective-permute-start.192 = (bf16[560,256]{0,1:T(8,128)(2,1)S(1)}, bf16[560,256]{0,1:T(8,128)(2,1)S(1)}, u32[]{:S(2)}, u32[]{:S(2)}) collective-permute-start(bf16[560,256]{0,1:T(8,128)(2,1)S(1)} %pad_maximum_fusion.12), channel_id=1, source_target_pairs={{0,16},{1,17},{2,18},{3,19},{4,20},{5,21},{6,22},{7,23},{8,24},{9,... | collective-permute-start | bytes 860168 | tf_op jit(solution)/shard_map/ppermute | solution.py:62
  1017.1 27.6 %collective-permute-start.173 = (bf16[64,1536]{1,0:T(8,128)(2,1)S(1)}, bf16[64,1536]{1,0:T(8,128)(2,1)S(1)}, u32[]{:S(2)}, u32[]{:S(2)}) collective-permute-start(bf16[64,1536]{1,0:T(8,128)(2,1)S(1)} %pad_maximum_fusion.14), channel_id=1, source_target_pairs={{0,0},{1,1},{2,8},{3,9},{4,16},{5,17},{6,24},{7,25},{8,4},{9,5},{1... | collective-permute-start | bytes 589832 | tf_op jit(solution)/shard_map/ppermute | solution.py:62
  1066.9 28.1 %collective-permute-start.156 = (bf16[256,768]{1,0:T(8,128)(2,1)}, bf16[256,768]{1,0:T(8,128)(2,1)}, u32[]{:S(2)}, u32[]{:S(2)}) collective-permute-start(bf16[256,768]{1,0:T(8,128)(2,1)} %get-tuple-element.358), channel_id=1, source_target_pairs={{0,1},{1,0},{2,3},{3,2},{4,5},{5,4},{6,7},{7,6},{8,9},{9,8},{10,11... | collective-permute-start | bytes 1179656 | tf_op jit(solution)/shard_map/ppermute | solution.py:62
  1067.3 30.5 %collective-permute-start.158 = (bf16[256,768]{1,0:T(8,128)(2,1)}, bf16[256,768]{1,0:T(8,128)(2,1)}, u32[]{:S(2)}, u32[]{:S(2)}) collective-permute-start(bf16[256,768]{1,0:T(8,128)(2,1)} %get-tuple-element.360), channel_id=1, source_target_pairs={{0,16},{1,17},{2,18},{3,19},{4,20},{5,21},{6,22},{7,23},{8,24},{9,... | collective-permute-start | bytes 1179656 | tf_op jit(solution)/shard_map/ppermute | solution.py:62
  1096.7 29.9 %collective-permute-start.157 = (bf16[128,768]{1,0:T(8,128)(2,1)}, bf16[128,768]{1,0:T(8,128)(2,1)S(1)}, u32[]{:S(2)}, u32[]{:S(2)}) collective-permute-start(bf16[128,768]{1,0:T(8,128)(2,1)} %add_convert_fusion.8), channel_id=1, source_target_pairs={{0,16},{1,17},{2,18},{3,19},{4,20},{5,21},{6,22},{7,23},{8,24},{9,... | collective-permute-start | bytes 589832 | tf_op jit(solution)/shard_map/ppermute | solution.py:62
  1099.5 27.2 %collective-permute-start.159 = (bf16[128,768]{1,0:T(8,128)(2,1)}, bf16[128,768]{1,0:T(8,128)(2,1)S(1)}, u32[]{:S(2)}, u32[]{:S(2)}) collective-permute-start(bf16[128,768]{1,0:T(8,128)(2,1)} %add_convert_fusion.7), channel_id=1, source_target_pairs={{0,1},{1,0},{2,3},{3,2},{4,5},{5,4},{6,7},{7,6},{8,9},{9,8},{10,11... | collective-permute-start | bytes 589832 | tf_op jit(solution)/shard_map/ppermute | solution.py:62
  (431 other events, 3180.3 us)
Sparse Core Ops, SparseCore 0:
  45.4 64.7 all-gather.10
  111.9 26.6 all-gather.12
  140.2 41.8 all-gather.14
  183.6 80.0 all-gather.16
  265.7 74.6 all-gather.18
  341.9 69.7 all-gather.20
  413.4 26.6 all-gather.22
  441.7 41.0 all-gather.24
  485.0 74.9 all-gather.26
  562.1 69.8 all-gather.28

commit v3 on v2

--- a/solution.py
+++ b/solution.py
@@ -134,7 +134,7 @@
         return jnp.where(self.y == self.c, mine, arrived)
 
     def fetch_heads(self, whole, first, widths):
-        count, wide = whole.shape[0] // TENSOR, whole.shape[1] - first
+        count, wide = whole.shape[0] // TENSOR, sum(widths)
         planes = self.planes // TENSOR
         half = count // (2 * planes)
 
@@ -444,6 +444,10 @@
     return ref[place * rank : (place + count) * rank]
 
 
+def last_columns(ref, held):
+    return ref.at[:, pl.ds(ref.shape[1] - held.shape[1], held.shape[1])]
+
+
 def ffn_kernel(places, *refs):
     pieces, (mask, near, far, w_in, w_out), refs = refs[:5], refs[5:10], refs[10:]
     parts, (up_raw, up_inner, down_inner), refs = refs[:4], refs[4:7], refs[7:]
@@ -451,7 +455,7 @@
     rank = mask.shape[1]
     width = full.shape[1]
     up_a, down_b, down_a, up_b = places
-    first = start_copy(w_in, held_in, sems.at[0])
+    first = start_copy(last_columns(w_in, held_in), held_in, sems.at[0])
     second = start_copy(w_out.at[:, pl.ds(0, full.shape[1])], held_out, sems.at[1])
     join(pieces, full)
     inner = narrow(dot_nt(full[...], picked(near, up_a, rank)), mask[...])
@@ -473,13 +477,13 @@
 def ffn(pieces, mask, near, far, w_in, w_out, places):
     count, width = pieces[0].shape
     rows, rank = mask.shape
-    wide = w_in.shape[1]
+    wide = w_out.shape[0]
     outs = part_shapes(rows, width) + [((rows, wide), bf16), ((rows, rank), bf16)]
     scratch = [
         pltpu.VMEM((rows, width), bf16),
         pltpu.VMEM((rows, max(wide, width)), f32),
         pltpu.VMEM((rows, wide), bf16),
-        pltpu.VMEM(w_in.shape, bf16),
+        pltpu.VMEM((width, wide), bf16),
         pltpu.VMEM((w_out.shape[0], width), bf16),
         pltpu.SemaphoreType.DMA((2,)),
     ]
@@ -499,7 +503,7 @@
     width = full.shape[1]
     at_up_a, at_down_b, at_down_a, at_up_b = places
     second = start_copy(w_out.at[:, pl.ds(0, full.shape[1])], held_out, sems.at[1])
-    first = start_copy(w_in, held_in, sems.at[0])
+    first = start_copy(last_columns(w_in, held_in), held_in, sems.at[0])
     join(grads, grad)
     join(inputs, full)
     down_back = narrow(dot_nt(grad[...], picked(near, at_down_b, rank)), mask[...])
@@ -526,14 +530,14 @@
 def ffn_back(grads, inputs, saved, mask, near, far, w_in, w_out, places):
     count, width = grads[0].shape
     rows, rank = mask.shape
-    wide = w_in.shape[1]
+    wide = w_out.shape[0]
     outs = part_shapes(rows, width) + [((rank, n), bf16) for n in (wide, wide, width, width)]
     scratch = [
         pltpu.VMEM((rows, width), bf16),
         pltpu.VMEM((rows, width), bf16),
         pltpu.VMEM((rows, max(wide, width)), f32),
         pltpu.VMEM((rows, wide), bf16),
-        pltpu.VMEM(w_in.shape, bf16),
+        pltpu.VMEM((width, wide), bf16),
         pltpu.VMEM((w_out.shape[0], width), bf16),
         pltpu.SemaphoreType.DMA((2,)),
     ]
@@ -966,9 +970,8 @@
     factor_rows = place.fetch_columns(factor_rows, factor_rows)
     factor_width = factor_rows.shape[1] // layers
 
-    def fetch_factors(layer, after):
-        whole = factor_rows[:, layer * factor_width : (layer + 1) * factor_width]
-        return own_columns(place.gather_planes(tied(whole, after)), len(NEAR))
+    def factors_of(layer):
+        return factor_rows[:, layer * factor_width : (layer + 1) * factor_width]
 
     up_at = 6 * own
     part = place.p.astype(jnp.int32)[None]
@@ -990,7 +993,9 @@
         whole = place.gather_planes(tied(rows, after))
         widths = (own, own, len(HEADS) * rank * place.rep // TENSOR)
         heads = place.fetch_heads(whole, 3 * own, widths)
-        return whole, heads, own_columns(heads[:, 2 * width :], len(HEADS))
+        near = whole[:, 3 * own + sum(widths) :]
+        near = own_columns(near, len(NEAR)) if near.shape[1] else None
+        return whole, heads, own_columns(heads[:, 2 * width :], len(HEADS)), near
 
     def other_rows_of(layer, after):
         mine, there = pack(
@@ -1001,8 +1006,7 @@
 
     def fetch_others(layer, rows, after):
         rows = tied(rows, after)
-        cross = place.gather_planes(rows[:, : 3 * own])
-        up = place.gather_planes(rows[:, 3 * own :])
+        cross_up = place.gather_planes(rows)
         count = down_weight.shape[1] // place.rep
         piece = lax.dynamic_slice(
             down_weight, (layer, share * count, 0), (1, count, width)
@@ -1016,7 +1020,7 @@
         piece = jnp.concatenate([piece] + [v.astype(bf16) for v in factors], 1)
         piece = jnp.pad(piece, ((0, padded // place.size - count), (0, 0)))
         down = place.gather_planes(tied(piece, rows))
-        return cross, up, down, own_columns(down[:, width:], 2)
+        return cross_up, down, own_columns(down[:, width:], 2), piece
 
     positions = jnp.stack([positions] + [place.part(positions, k) for k in range(1, TENSOR)], 1)
     tables = rotary_tables(positions.reshape(3, set_rows))
@@ -1054,12 +1058,12 @@
     normed = (hat * factors[0][2] + factors[0][4]).astype(bf16)
     fetched = []
     coming = fetch_self(self_rows_of(0, None), (moved, numbers, times))
-    picked_now = fetch_factors(0, None)
+    first_near = own_columns(place.gather_planes(factors_of(0)), len(NEAR))
     others = None
     for layer in range(layers):
         gate_one, gate_two, scale_one, scale_two, shift_one, shift_two = factors[layer]
-        self_in, heads, far_heads = coming
-        near = picked_now
+        self_in, heads, far_heads, near = coming
+        near = first_near if near is None else near
         self_pieces = place.gather(normed)
         if layer == 0:
             first_rows = other_rows_of(layer, self_pieces[3])
@@ -1069,16 +1073,13 @@
                 for k in range(1, layers)
             ]
             text = place.gather(tied(moved[rows:], self_pieces[3]))
-        cross_in, ffn_in, ffn_out, far = others
+        cross_in, ffn_out, far, down_piece = others
         raws, self_inner, stats = project(self_pieces, mask, self_in, near, far_heads, in_at, 3, 2)
         gain = [own_gain(layer, k) for k in range(4)]
         (query, pair), self_total = normalize(
             raws[:2], gain[:2], arrivals(stats), width, tables, raws[2:]
         )
         pairs = place.spread(pair)
-        if layer + 1 < layers:
-            coming = fetch_self(prepared[layer][0], query)
-            picked_now = fetch_factors(layer + 1, query)
         parts, attended, out_inner = attend(
             query, columns_of[0], pairs, self_rows, mask, heads, near, far_heads, out_at
         )
@@ -1086,6 +1087,10 @@
         state_one, normed = advance(
             place.scatter(parts), state, gate_one, gains[layer, 4][None], zero_row
         )
+        if layer + 1 < layers:
+            following = jnp.concatenate([prepared[layer][0], factors_of(layer + 1)], 1)
+            following = tied(following, down_piece)
+            coming = fetch_self(following, normed)
 
         text_raws, text_inner, stats = project(
             text, text_mask, cross_in, near, far_heads, text_at, 2, 1
@@ -1115,8 +1120,8 @@
 
         ffn_pieces = place.gather(normed)
         ready = mask if layer + 1 == layers else tied(mask, coming[1])
-        parts, ffn_saved = ffn(ffn_pieces, ready, near, far, ffn_in, ffn_out, ffn_at)
-        fetched.append((self_in, heads, cross_in, ffn_in, ffn_out, near, far, far_heads))
+        parts, ffn_saved = ffn(ffn_pieces, ready, near, far, cross_in, ffn_out, ffn_at)
+        fetched.append((self_in, heads, cross_in, ffn_out, near, far, far_heads))
         saved.append(
             (
                 (state, state_one, state_two), self_saved, cross_saved,
@@ -1133,14 +1138,14 @@
     grad_text = 0.0
     whole_grads, part_grads, wide_grads = [], [], []
     for layer in reversed(range(layers)):
-        self_in, heads, cross_in, ffn_in, ffn_out, near, far, far_heads = fetched[layer]
+        self_in, heads, cross_in, ffn_out, near, far, far_heads = fetched[layer]
         gate_one, gate_two, scale_one, scale_two, shift_one, shift_two = factors[layer]
         (
             (state_zero, state_one, state_two), self_saved, cross_saved,
             (text_raws, text_inner, text_total), (ffn_pieces, ffn_saved), gain,
         ) = saved[layer]
         parts, (down_a, up_b, up_a, down_b) = ffn_back(
-            place.gather(out), ffn_pieces, ffn_saved, mask, near, far, ffn_in, ffn_out, ffn_at
+            place.gather(out), ffn_pieces, ffn_saved, mask, near, far, cross_in, ffn_out, ffn_at
         )
         grad, out = retreat(place.scatter(parts), state_two, grad, scale_two, valid_rows)
 

time: 1170 us -> 1160 us (level)
  starting transfers between devices: 244 us -> 263 us
  waiting for transfers between devices: 346 us -> 327 us
    ppermute x193, starting transfers between devices: 243 us -> 262 us  [send(): return lax.ppermute(values, AXES, pairs)]
    ppermute x193, waiting for transfers between devices: 311 us -> 292 us  [send(): return lax.ppermute(values, AXES, pairs)]
    all_gather x10 -> x7, waiting for transfers between devices: 35 us -> 33.5 us  [gather_planes(): return lax.all_gather(rows, (AXES[2], AXES[1]), axis=0, tiled=True)]
    unnamed x566 -> x554, local copies, waits for them, and re-layouts: 36.6 us -> 37.6 us
  transfers between devices with their start and end apart: 203 -> 200, of which waited for: 91 -> 86; matrix products, arithmetic and copies ran while one was open for 16% -> 16% of each run, Pallas kernels for 20% -> 20%
where the time goes in v3:
time: 1160 us; the launch traced here: 1150 us
  waiting for transfers between devices  327 us (28%)
  Pallas kernels  323 us (28%)
  starting transfers between devices  263 us (23%)
  local copies, waits for them, and re-layouts  96.6 us (8%)
  other arithmetic  86.2 us (7%)
  matrix products  31.9 us (3%)
  between operations  25.5 us (2%)
    pallas_call x48, Pallas kernels, call(): pl.pallas_call(kernel, out_shape=outs, in_specs=[pl.BlockSpec(memory_spac...  302 us
    ppermute x193, waiting for transfers between devices, send(): return lax.ppermute(values, AXES, pairs)  292 us
    ppermute x193, starting transfers between devices, send(): return lax.ppermute(values, AXES, pairs)  262 us
    unnamed x554, local copies, waits for them, and re-layouts  37.6 us
    all_gather x7, waiting for transfers between devices, gather_planes(): return lax.all_gather(rows, (AXES[2], AXES[1]), axis=0, tiled=True)  33.5 us
  transfers between devices with their start and end apart: 200, of which 86 were waited for; matrix products, arithmetic and copies ran while one was open for 16% of the time, Pallas kernels for 20%

profile of v3, /device:TPU:1, one launch (start us, length us, event | category | flops | bytes accessed | tf_op | source)
XLA Modules:
  0.0 1152.7 jit_solution(10004122360213897885)
XLA Ops:
  49.5 9.1 collective-permute-done.2.refs_1_.refs_12_
  74.5 14.1 %collective-permute-done.31 = bf16[192,3456]{1,0:T(8,128)(2,1)} collective-permute-done((bf16[192,3456]{1,0:T(8,128)(2,1)}, bf16[192,3456]{1,0:T(8,128)(2,1)}, u32[]{:S(2)}, u32[]{:S(2)}) %collective-permute-start.31) | collective-permute-done | bytes 1327136 | tf_op jit(solution)/shard_map/ppermute | solution.py:62
  95.8 7.3 collective-permute-done.51
  131.5 7.8 collective-permute-done.16
  139.3 8.3 collective-permute-start.97
  159.6 7.5 collective-permute-done.3.refs_2_.refs_13_
  181.8 8.2 shard_map.227
  210.5 7.8 shard_map.229
  248.7 24.0 %collective-permute-done.27.refs_1_.refs_9_ = bf16[128,1536]{1,0:T(8,128)(2,1)S(1)} collective-permute-done((bf16[128,1536]{1,0:T(8,128)(2,1)}, bf16[128,1536]{1,0:T(8,128)(2,1)S(1)}, u32[]{:S(2)}, u32[]{:S(2)}) %collective-permute-start.27) | collective-permute-done | bytes 393248 | tf_op jit(solution)/shard_map/ppermute | solution.py:62
  357.9 6.9 collective-permute-done.43.refs_1_
  378.2 33.4 %all-gather.16.cloned.1.call-done.refs_9_.refs_17_ = bf16[2304,1664]{1,0:T(8,128)(2,1)} async-done(((bf16[288,1664]{1,0:T(8,128)(2,1)}), bf16[2304,1664]{1,0:T(8,128)(2,1)}) %all-gather.16.cloned.1.call-update) | async-done | bytes 7667728 | tf_op jit(solution)/shard_map/all_gather | solution.py:128
  424.9 17.4 %shard_map.240 = (bf16[256,768]{1,0:T(8,128)(2,1)}, bf16[256,768]{1,0:T(8,128)(2,1)}, bf16[256,768]{1,0:T(8,128)(2,1)}, bf16[256,768]{1,0:T(8,128)(2,1)}, bf16[5...) custom-call(bf16[128,1536]{1,0:T(8,128)(2,1)} %get-tuple-element.237.refs_0_.refs_5_, ...), custom_call_target="tpu_custom_call" | custom-call | flops 7247757312 | bytes 24494080 | tf_op jit(solution)/shard_map/pallas_call | solution.py:235
  442.9 9.7 collective-permute-done.56.refs_1_
  479.5 8.0 shard_map.242
  508.3 7.9 shard_map.244
  516.7 10.2 collective-permute-done.68.refs_1_
  617.8 17.1 %shard_map.253 = (bf16[256,768]{1,0:T(8,128)(2,1)}, bf16[256,768]{1,0:T(8,128)(2,1)}, bf16[256,768]{1,0:T(8,128)(2,1)}, bf16[256,768]{1,0:T(8,128)(2,1)}, bf16[5...) custom-call(bf16[128,1536]{1,0:T(8,128)(2,1)} %get-tuple-element.278.refs_0_.refs_5_, ...), custom_call_target="tpu_custom_call" | custom-call | flops 7247757312 | bytes 24494080 | tf_op jit(solution)/shard_map/pallas_call | solution.py:235
  635.7 20.9 %shard_map.255 = (bf16[256,768]{1,0:T(8,128)(2,1)}, bf16[256,768]{1,0:T(8,128)(2,1)}, bf16[256,768]{1,0:T(8,128)(2,1)}, bf16[256,768]{1,0:T(8,128)(2,1)}, bf16[1...) custom-call(bf16[128,1536]{1,0:T(8,128)(2,1)} %get-tuple-element.736.refs_0_, ...), custom_call_target="tpu_custom_call" | custom-call | flops 7247757312 | bytes 26312704 | tf_op jit(solution)/shard_map/pallas_call | solution.py:235
  680.8 6.7 collective-permute-done.106.refs_1_
  693.6 9.4 shard_map.257
  753.6 12.6 %shard_map.261 = (f32[512,384]{1,0:T(8,128)}, f32[512,768]{1,0:T(8,128)}, f32[512,768]{1,0:T(8,128)}, bf16[16,384]{1,0:T(8,128)(2,1)}, bf16[16,1536]{1,0:T(8,128)(2,1)}) custom-call(bf16[128,1536]{1,0:T(8,128)(2,1)} %get-tuple-element.306.refs_0_, bf16[128,1536]{1,0:T(8,128)(2,1)} %copy-done.162, bf16[128,1536]{1,0:T(8,128)(2,1)} %copy-done.163, ...), custom_call_target="tpu_custom_call" | custom-call | flops 2617245696 | bytes 11323392 | tf_op jit(solution)/shard_map/pallas_call | solution.py:235
  767.8 19.9 %collective-permute-start.121 = (bf16[512,768]{1,0:T(8,128)(2,1)S(1)}, bf16[512,768]{1,0:T(8,128)(2,1)S(1)}, u32[]{:S(2)}, u32[]{:S(2)}) collective-permute-start(bf16[512,768]{1,0:T(8,128)(2,1)S(1)} %convert_element_type.610), channel_id=1, source_target_pairs={{0,8},{1,9},{2,10},{3,11},{4,12},{5,13},{6,14},{7,15},{8,0},{9,1},... | collective-permute-start | bytes 2359304 | tf_op jit(solution)/shard_map/ppermute | solution.py:62
  802.8 8.5 shard_map.263
  813.9 10.2 collective-permute-done.95.refs_5_
  857.4 7.7 collective-permute-done.129.refs_1_
  872.9 21.2 %shard_map.265 = (bf16[256,768]{1,0:T(8,128)(2,1)}, bf16[256,768]{1,0:T(8,128)(2,1)}, bf16[256,768]{1,0:T(8,128)(2,1)}, bf16[256,768]{1,0:T(8,128)(2,1)}, bf16[1...) custom-call(bf16[128,1536]{1,0:T(8,128)(2,1)} %get-tuple-element.323.refs_0_, ...), custom_call_target="tpu_custom_call" | custom-call | flops 7247757312 | bytes 26312704 | tf_op jit(solution)/shard_map/pallas_call | solution.py:235
  933.0 8.9 shard_map.267
  969.4 7.2 collective-permute-done.167
  1009.2 10.1 collective-permute-start.173
  1020.1 12.4 %shard_map.271 = (f32[512,384]{1,0:T(8,128)}, f32[512,768]{1,0:T(8,128)}, f32[512,768]{1,0:T(8,128)}, bf16[16,384]{1,0:T(8,128)(2,1)}, bf16[16,1536]{1,0:T(8,128)(2,1)}) custom-call(bf16[128,1536]{1,0:T(8,128)(2,1)} %get-tuple-element.345.refs_0_, bf16[128,1536]{1,0:T(8,128)(2,1)} %copy-done.156, bf16[128,1536]{1,0:T(8,128)(2,1)} %copy-done.157, ...), custom_call_target="tpu_custom_call" | custom-call | flops 2617245696 | bytes 11323392 | tf_op jit(solution)/shard_map/pallas_call | solution.py:235
  1049.7 8.6 shard_map.273
  1124.5 7.2 collective-permute-start.160
  (1352 shorter events, 750.9 us)
Async XLA Ops:
  7.2 115.0 %all-gather.8.cloned.1.call-start = ((), (), s32[]{:S(2)}) async-start(), calls=%async_computation | async-start | bytes 7077888 | tf_op jit(solution)/shard_map/all_gather | solution.py:128
  7.2 23.7 %collective-permute-start.10 = (s32[1]{0:T(128)}, s32[1]{0:T(128)}, u32[]{:S(2)}, u32[]{:S(2)}) collective-permute-start(s32[1]{0:T(128)} %param.23), channel_id=1, source_target_pairs={{0,8},{1,9},{2,10},{3,11},{4,12},{5,13},{6,14},{7,15},{8,0},{9,1},... | collective-permute-start | bytes 20 | tf_op jit(solution)/shard_map/ppermute | solution.py:62
  7.4 25.0 %collective-permute-start.8 = (s32[1]{0:T(128)}, s32[1]{0:T(128)}, u32[]{:S(2)}, u32[]{:S(2)}) collective-permute-start(s32[1]{0:T(128)} %param.23), channel_id=1, source_target_pairs={{0,16},{1,17},{2,18},{3,19},{4,20},{5,21},{6,22},{7,23},{8,24},{9,... | collective-permute-start | bytes 20 | tf_op jit(solution)/shard_map/ppermute | solution.py:62
  10.0 35.2 %collective-permute-start.1 = (f32[1,6,1536]{2,0,1:T(1,128)}, f32[1,6,1536]{2,0,1:T(1,128)}, u32[]{:S(2)}, u32[]{:S(2)}) collective-permute-start(f32[1,6,1536]{2,0,1:T(1,128)} %param.25), channel_id=1, source_target_pairs={{0,0},{1,1},{2,16},{3,17},{4,8},{5,9},{6,24},{7,25},{8,2},{9,3},{1... | collective-permute-start | bytes 110600 | tf_op jit(solution)/shard_map/ppermute | solution.py:62
  15.4 29.9 %collective-permute-start = (bf16[192,1536]{1,0:T(8,128)(2,1)}, bf16[192,1536]{1,0:T(8,128)(2,1)S(1)}, u32[]{:S(2)}, u32[]{:S(2)}) collective-permute-start(bf16[192,1536]{1,0:T(8,128)(2,1)} %pad_maximum_fusion.7), channel_id=1, source_target_pairs={{0,0},{1,1},{2,16},{3,17},{4,8},{5,9},{6,24},{7,25},{8,2},{9,3},{1... | collective-permute-start | bytes 1769480 | tf_op jit(solution)/shard_map/ppermute | solution.py:62
  19.4 25.8 %collective-permute-start.6 = (s32[386]{0:T(512)S(1)}, s32[386]{0:T(512)S(1)}, u32[]{:S(2)}, u32[]{:S(2)}) collective-permute-start(s32[386]{0:T(512)S(1)} %pad_add_fusion.3), channel_id=1, source_target_pairs={{0,0},{1,1},{2,16},{3,17},{4,8},{5,9},{6,24},{7,25},{8,2},{9,3},{1... | collective-permute-start | bytes 4640 | tf_op jit(solution)/shard_map/ppermute | solution.py:62
  45.3 123.9 %all-gather.10.cloned.1.call-start = ((), (), s32[]{:S(2)}) async-start(), calls=%async_computation.1 | async-start | bytes 2211840 | tf_op jit(solution)/shard_map/all_gather | solution.py:128
  106.8 200.0 %all-gather.12.cloned.1.call-start = ((), (), s32[]{:S(2)}) async-start(), calls=%async_computation.2 | async-start | bytes 11943936 | tf_op jit(solution)/shard_map/all_gather | solution.py:128
  107.5 227.5 %all-gather.14.cloned.1.call-start = ((), (), s32[]{:S(2)}) async-start(), calls=%async_computation.3 | async-start | bytes 9289728 | tf_op jit(solution)/shard_map/all_gather | solution.py:128
  117.0 30.6 %collective-permute-start.18 = (s32[3,128]{1,0:T(4,128)S(1)}, s32[3,128]{1,0:T(4,128)S(1)}, u32[]{:S(2)}, u32[]{:S(2)}) collective-permute-start(s32[3,128]{1,0:T(4,128)S(1)} %get-tuple-element.752), channel_id=1, source_target_pairs={{0,17},{1,16},{2,19},{3,18},{4,21},{5,20},{6,23},{7,22},{8,25},{9,... | collective-permute-start | bytes 4616 | tf_op jit(solution)/shard_map/ppermute | solution.py:62
  139.3 80.4 %collective-permute-start.97 = (bf16[128,1536]{1,0:T(8,128)(2,1)}, bf16[128,1536]{1,0:T(8,128)(2,1)}, u32[]{:S(2)}, u32[]{:S(2)}) collective-permute-start(bf16[128,1536]{1,0:T(8,128)(2,1)} %param.20), channel_id=1, source_target_pairs={{0,0},{1,1},{2,16},{3,17},{4,8},{5,9},{6,24},{7,25},{8,2},{9,3},{1... | collective-permute-start | bytes 1179656 | tf_op jit(solution)/shard_map/ppermute | solution.py:62
  240.1 171.6 %all-gather.16.cloned.1.call-start = ((), (), s32[]{:S(2)}) async-start(), calls=%async_computation.4 | async-start | bytes 8626176 | tf_op jit(solution)/shard_map/all_gather | solution.py:128
  240.7 289.0 %all-gather.18.cloned.1.call-start = ((), (), s32[]{:S(2)}) async-start(), calls=%async_computation.5 | async-start | bytes 11943936 | tf_op jit(solution)/shard_map/all_gather | solution.py:128
  245.2 28.4 %collective-permute-start.76 = (bf16[192,3456]{1,0:T(8,128)(2,1)}, bf16[192,3456]{1,0:T(8,128)(2,1)S(1)}, u32[]{:S(2)}, u32[]{:S(2)}) collective-permute-start(bf16[192,3456]{1,0:T(8,128)(2,1)} %get-tuple-element.264), channel_id=1, source_target_pairs={{0,1},{2,3},{4,5},{6,7},{9,8},{11,10},{13,12},{15,14},{16,17},{18,... | collective-permute-start | bytes 3981320 | tf_op jit(solution)/shard_map/ppermute | solution.py:62
  246.5 26.3 %collective-permute-start.27 = (bf16[128,1536]{1,0:T(8,128)(2,1)}, bf16[128,1536]{1,0:T(8,128)(2,1)S(1)}, u32[]{:S(2)}, u32[]{:S(2)}) collective-permute-start(bf16[128,1536]{1,0:T(8,128)(2,1)} %get-tuple-element.220.refs_0_.refs_8_), channel_id=1, source_target_pairs={{0,1},{1,0},{2,3},{3,2},{4,5},{5,4},{6,7},{7,6},{8,9},{9,8},{10,11... | collective-permute-start | bytes 1179656 | tf_op jit(solution)/shard_map/ppermute | solution.py:62
  279.6 331.6 %all-gather.20.cloned.1.call-start = ((), (), s32[]{:S(2)}) async-start(), calls=%async_computation.6 | async-start | bytes 8626176 | tf_op jit(solution)/shard_map/all_gather | solution.py:128
  356.7 59.8 %collective-permute-start.55 = (bf16[3,192,896]{2,1,0:T(8,128)(2,1)S(1)}, bf16[3,192,896]{2,1,0:T(8,128)(2,1)}, u32[]{:S(2)}, u32[]{:S(2)}) collective-permute-start(bf16[3,192,896]{2,1,0:T(8,128)(2,1)S(1)} %get-tuple-element.442), channel_id=1, source_target_pairs={{0,8},{1,9},{2,10},{3,11},{4,12},{5,13},{6,14},{7,15},{8,0},{9,1},... | collective-permute-start | bytes 3096584 | tf_op jit(solution)/shard_map/ppermute | solution.py:62
  376.1 37.7 %collective-permute-start.47 = (bf16[128,1536]{1,0:T(8,128)(2,1)}, bf16[128,1536]{1,0:T(8,128)(2,1)S(1)}, u32[]{:S(2)}, u32[]{:S(2)}) collective-permute-start(bf16[128,1536]{1,0:T(8,128)(2,1)} %get-tuple-element.237.refs_0_.refs_5_), channel_id=1, source_target_pairs={{0,1},{1,0},{2,3},{3,2},{4,5},{5,4},{6,7},{7,6},{8,9},{9,8},{10,11... | collective-permute-start | bytes 1179656 | tf_op jit(solution)/shard_map/ppermute | solution.py:62
  377.6 37.6 %collective-permute-start.48 = (bf16[128,1536]{1,0:T(8,128)(2,1)}, bf16[128,1536]{1,0:T(8,128)(2,1)S(1)}, u32[]{:S(2)}, u32[]{:S(2)}) collective-permute-start(bf16[128,1536]{1,0:T(8,128)(2,1)} %get-tuple-element.237.refs_0_.refs_5_), channel_id=1, source_target_pairs={{0,16},{1,17},{2,18},{3,19},{4,20},{5,21},{6,22},{7,23},{8,24},{9,... | collective-permute-start | bytes 1179656 | tf_op jit(solution)/shard_map/ppermute | solution.py:62
  547.7 24.0 %collective-permute-start.83 = (bf16[256,768]{1,0:T(8,128)(2,1)}, bf16[256,768]{1,0:T(8,128)(2,1)S(1)}, u32[]{:S(2)}, u32[]{:S(2)}) collective-permute-start(bf16[256,768]{1,0:T(8,128)(2,1)} %get-tuple-element.272.refs_2_.refs_7_), channel_id=1, source_target_pairs={{0,8},{1,9},{2,10},{3,11},{4,12},{5,13},{6,14},{7,15},{8,0},{9,1},... | collective-permute-start | bytes 1179656 | tf_op jit(solution)/shard_map/ppermute | solution.py:62
  599.8 35.1 %collective-permute-start.100 = (bf16[128,768]{1,0:T(8,128)(2,1)S(1)}, bf16[128,768]{1,0:T(8,128)(2,1)S(1)}, u32[]{:S(2)}, u32[]{:S(2)}) collective-permute-start(bf16[128,768]{1,0:T(8,128)(2,1)S(1)} %slice.1857), channel_id=1, source_target_pairs={{0,16},{1,17},{2,18},{3,19},{4,20},{5,21},{6,22},{7,23},{8,24},{9,... | collective-permute-start | bytes 589832 | tf_op jit(solution)/shard_map/ppermute | solution.py:62
  601.8 33.1 %collective-permute-start.101 = (bf16[128,768]{1,0:T(8,128)(2,1)S(1)}, bf16[128,768]{1,0:T(8,128)(2,1)S(1)}, u32[]{:S(2)}, u32[]{:S(2)}) collective-permute-start(bf16[128,768]{1,0:T(8,128)(2,1)S(1)} %slice.1858), channel_id=1, source_target_pairs={{0,1},{1,0},{2,3},{3,2},{4,5},{5,4},{6,7},{7,6},{8,9},{9,8},{10,11... | collective-permute-start | bytes 589832 | tf_op jit(solution)/shard_map/ppermute | solution.py:62
  767.8 22.9 %collective-permute-start.121 = (bf16[512,768]{1,0:T(8,128)(2,1)S(1)}, bf16[512,768]{1,0:T(8,128)(2,1)S(1)}, u32[]{:S(2)}, u32[]{:S(2)}) collective-permute-start(bf16[512,768]{1,0:T(8,128)(2,1)S(1)} %convert_element_type.610), channel_id=1, source_target_pairs={{0,8},{1,9},{2,10},{3,11},{4,12},{5,13},{6,14},{7,15},{8,0},{9,1},... | collective-permute-start | bytes 2359304 | tf_op jit(solution)/shard_map/ppermute | solution.py:62
  800.1 35.4 %collective-permute-start.161 = (bf16[256,768]{1,0:T(8,128)(2,1)S(1)}, bf16[256,768]{1,0:T(8,128)(2,1)S(1)}, u32[]{:S(2)}, u32[]{:S(2)}) collective-permute-start(bf16[256,768]{1,0:T(8,128)(2,1)S(1)} %convert_element_type.638), channel_id=1, source_target_pairs={{0,8},{1,9},{2,10},{3,11},{4,12},{5,13},{6,14},{7,15},{8,0},{9,1},... | collective-permute-start | bytes 1179656 | tf_op jit(solution)/shard_map/ppermute | solution.py:62
  811.4 28.8 %collective-permute-start.125 = (bf16[256,768]{1,0:T(8,128)(2,1)}, bf16[256,768]{1,0:T(8,128)(2,1)S(1)}, u32[]{:S(2)}, u32[]{:S(2)}) collective-permute-start(bf16[256,768]{1,0:T(8,128)(2,1)} %get-tuple-element.319), channel_id=1, source_target_pairs={{0,1},{1,0},{2,3},{3,2},{4,5},{5,4},{6,7},{7,6},{8,9},{9,8},{10,11... | collective-permute-start | bytes 1179656 | tf_op jit(solution)/shard_map/ppermute | solution.py:62
  813.0 28.2 %collective-permute-start.127 = (bf16[256,768]{1,0:T(8,128)(2,1)}, bf16[256,768]{1,0:T(8,128)(2,1)S(1)}, u32[]{:S(2)}, u32[]{:S(2)}) collective-permute-start(bf16[256,768]{1,0:T(8,128)(2,1)} %get-tuple-element.321), channel_id=1, source_target_pairs={{0,16},{1,17},{2,18},{3,19},{4,20},{5,21},{6,22},{7,23},{8,24},{9,... | collective-permute-start | bytes 1179656 | tf_op jit(solution)/shard_map/ppermute | solution.py:62
  922.7 26.6 %collective-permute-start.192 = (bf16[560,256]{0,1:T(8,128)(2,1)S(1)}, bf16[560,256]{0,1:T(8,128)(2,1)S(1)}, u32[]{:S(2)}, u32[]{:S(2)}) collective-permute-start(bf16[560,256]{0,1:T(8,128)(2,1)S(1)} %pad_maximum_fusion.11), channel_id=1, source_target_pairs={{0,16},{1,17},{2,18},{3,19},{4,20},{5,21},{6,22},{7,23},{8,24},{9,... | collective-permute-start | bytes 860168 | tf_op jit(solution)/shard_map/ppermute | solution.py:62
  1009.2 27.0 %collective-permute-start.173 = (bf16[64,1536]{1,0:T(8,128)(2,1)S(1)}, bf16[64,1536]{1,0:T(8,128)(2,1)S(1)}, u32[]{:S(2)}, u32[]{:S(2)}) collective-permute-start(bf16[64,1536]{1,0:T(8,128)(2,1)S(1)} %pad_maximum_fusion.13), channel_id=1, source_target_pairs={{0,0},{1,1},{2,8},{3,9},{4,16},{5,17},{6,24},{7,25},{8,4},{9,5},{1... | collective-permute-start | bytes 589832 | tf_op jit(solution)/shard_map/ppermute | solution.py:62
  1058.3 28.4 %collective-permute-start.156 = (bf16[256,768]{1,0:T(8,128)(2,1)}, bf16[256,768]{1,0:T(8,128)(2,1)}, u32[]{:S(2)}, u32[]{:S(2)}) collective-permute-start(bf16[256,768]{1,0:T(8,128)(2,1)} %get-tuple-element.358), channel_id=1, source_target_pairs={{0,1},{1,0},{2,3},{3,2},{4,5},{5,4},{6,7},{7,6},{8,9},{9,8},{10,11... | collective-permute-start | bytes 1179656 | tf_op jit(solution)/shard_map/ppermute | solution.py:62
  1059.4 30.2 %collective-permute-start.158 = (bf16[256,768]{1,0:T(8,128)(2,1)}, bf16[256,768]{1,0:T(8,128)(2,1)}, u32[]{:S(2)}, u32[]{:S(2)}) collective-permute-start(bf16[256,768]{1,0:T(8,128)(2,1)} %get-tuple-element.360), channel_id=1, source_target_pairs={{0,16},{1,17},{2,18},{3,19},{4,20},{5,21},{6,22},{7,23},{8,24},{9,... | collective-permute-start | bytes 1179656 | tf_op jit(solution)/shard_map/ppermute | solution.py:62
  1088.4 30.3 %collective-permute-start.157 = (bf16[128,768]{1,0:T(8,128)(2,1)}, bf16[128,768]{1,0:T(8,128)(2,1)S(1)}, u32[]{:S(2)}, u32[]{:S(2)}) collective-permute-start(bf16[128,768]{1,0:T(8,128)(2,1)} %add_convert_fusion.8), channel_id=1, source_target_pairs={{0,16},{1,17},{2,18},{3,19},{4,20},{5,21},{6,22},{7,23},{8,24},{9,... | collective-permute-start | bytes 589832 | tf_op jit(solution)/shard_map/ppermute | solution.py:62
  1091.2 27.5 %collective-permute-start.159 = (bf16[128,768]{1,0:T(8,128)(2,1)}, bf16[128,768]{1,0:T(8,128)(2,1)S(1)}, u32[]{:S(2)}, u32[]{:S(2)}) collective-permute-start(bf16[128,768]{1,0:T(8,128)(2,1)} %add_convert_fusion.7), channel_id=1, source_target_pairs={{0,1},{1,0},{2,3},{3,2},{4,5},{5,4},{6,7},{7,6},{8,9},{9,8},{10,11... | collective-permute-start | bytes 589832 | tf_op jit(solution)/shard_map/ppermute | solution.py:62
  (430 other events, 3145.5 us)
Sparse Core Ops, SparseCore 0:
  45.4 64.7 all-gather.7
  111.9 26.6 all-gather.9
  140.8 109.0 all-gather.11
  251.9 82.8 all-gather.13
  336.9 74.7 all-gather.15
  413.8 99.0 all-gather.17
  514.5 74.4 all-gather.19
